TPU v7x, 32 devices: a whole 2x2x4 slice. The times are simulated.
32 devices in a mesh: lat: 4 (over y, core), lev: 8 (over z, x).
Axes of the slice: x: 2, y: 2, z: 4, core: 2. Of those that a mesh axis runs over, the one named last changes fastest.
Arguments:
- species_fractions: float32 [32, 32, 16, 128], P(None, 'lev', 'lat'), may hold values from 0.1 to 2
- cell_flow_ratios: float32 [2, 32, 16, 128], P(None, 'lev', 'lat'), may hold values from -0.9 to 0.9
- layer_pressure_depth: float32 [32, 16, 128], P(None, 'lat', 'lev'), may hold values from 0.5 to 2
- layer_thickness_fraction: float32 [32], replicated, may hold values from 0.5 to 2
- cell_kelvin_field: float32 [32, 16, 128], P(None, 'lat', 'lev'), may hold values from 200 to 300
- daytime_indicator: int32 [4, 16, 128], P(None, 'lat', 'lev'), may hold values from 0 to 1, as said below
- kinetic_factor_times_step: float32 [256], replicated, may hold values from 0.001 to 0.01
- arrhenius_barrier: float32 [256], replicated, may hold values from 0 to 3
- species_yield_matrix: int32 [256, 32], replicated, may hold values from -2 to 2
- reagent_pairs: int32 [2, 256], replicated, may hold values from 0 to 31
Outputs:
- tracers: float32 [32, 32, 16, 128], P(None, 'lev', 'lat')
Inputs may be any that keep to these rules, and one draw needn't show every extreme that they name: `daytime_indicator`: A run of 64 longitudes in a row, cyclic and starting at a drawn longitude (daylight), is active in each substep with probability 7/8 independently; outside it only substep 0 can be active, with probability 1/2.
All inputs are finite; a program needn't handle non-finite values.
Results may differ from a plain program's by a relative error of at most 0.0003.
Values sent between devices are 32-bit elements; how exact they have to be, the bound alone decides.
No kernel may reach another device: no remote copies, remote signals or barrier semaphores. Data moves between devices by JAX's collectives and lax.ppermute only.
A program may use at most 64 MiB of HBM per device.

v0:
```python
import jax
import jax.numpy as jnp
from jax import lax
from jax.sharding import PartitionSpec as P


def padded_2(value, sides, width):
    for axis, dim in sides:
        size, length = (lax.axis_size(axis), value.shape[dim])
        up = [(i, (i + 1) % size) for i in range(size - 1)]
        down = [(j, i) for i, j in up]
        last = lax.slice_in_dim(value, length - width, length, axis=dim)
        first = lax.slice_in_dim(value, 0, width, axis=dim)
        before = lax.ppermute(last, axis, up)
        after = lax.ppermute(first, axis, down)
        value = jnp.concatenate([before, value, after], axis=dim)
    return value


def swapped(block, axis, apart):
    count = lax.axis_size(axis)
    route = []
    for low in range(count):
        high = low | 1 << apart
        if high != low and high < count:
            route += [(low, high), (high, low)]
    return lax.ppermute(block, axis, route)


def minmod(left, right):
    return 0.5 * (jnp.sign(left) + jnp.sign(right)) * jnp.minimum(jnp.abs(left), jnp.abs(right))


def face_flux(courant, before, before_slope, after_cell, after_slope):
    forward = courant * (before + 0.5 * (1.0 - courant) * before_slope)
    backward = courant * (after_cell - 0.5 * (1.0 + courant) * after_slope)
    return jnp.where(courant > 0.0, forward, backward)


def lon_update(tracer, zonal_wind):
    before = jnp.roll(tracer, 1, axis=-1)
    behind = jnp.roll(tracer, -1, axis=-1)
    slopes = minmod(tracer - before, behind - tracer)
    courant = 0.5 * (jnp.roll(zonal_wind, 1, axis=-1) + zonal_wind)
    fluxes = face_flux(courant, before, jnp.roll(slopes, 1, axis=-1), tracer, slopes)
    return tracer - (jnp.roll(fluxes, -1, axis=-1) - fluxes)


def lat_update(padded, merid_wind, face_ok):
    row_count = padded.shape[-2]
    slopes = minmod(
        padded[..., 1:-1, :] - padded[..., :-2, :], padded[..., 2:, :] - padded[..., 1:-1, :]
    )
    courant = (
        0.5
        * (merid_wind[..., 1 : row_count - 2, :] + merid_wind[..., 2 : row_count - 1, :])
        * face_ok[2 : row_count - 1][:, None]
    )
    fluxes = face_flux(
        courant,
        padded[..., 1 : row_count - 2, :],
        slopes[..., 0 : row_count - 3, :],
        padded[..., 2 : row_count - 1, :],
        slopes[..., 1 : row_count - 2, :],
    )
    return padded[..., 2 : row_count - 2, :] - (fluxes[..., 1:, :] - fluxes[..., :-1, :])


def remap(vertical_profiles, layer_pressure_depth, layer_thickness_fraction):
    upper_edge = jnp.cumsum(layer_pressure_depth, axis=0)
    lower_edge = jnp.concatenate([jnp.zeros_like(upper_edge[:1]), upper_edge[:-1]], axis=0)
    column_total = upper_edge[-1]
    expand = (slice(None),) + (None,) * column_total.ndim
    share_sum = jnp.sum(layer_thickness_fraction)
    fraction_top = jnp.cumsum(layer_thickness_fraction) / share_sum
    fraction_bottom = jnp.concatenate([jnp.zeros((1,), fraction_top.dtype), fraction_top[:-1]])
    target_top = fraction_top[expand] * column_total[None]
    target_bottom = fraction_bottom[expand] * column_total[None]
    intersection = jnp.maximum(
        0.0,
        jnp.minimum(upper_edge[None], target_top[:, None])
        - jnp.maximum(lower_edge[None], target_bottom[:, None]),
    )
    target_thick = (layer_thickness_fraction / share_sum)[expand] * column_total[None]
    carried = jnp.einsum(
        "ts...,ns...->nt...", intersection, vertical_profiles, precision=lax.Precision.HIGHEST
    )
    return carried / target_thick[None]


def react_block(
    vertical_profiles,
    cell_kelvin_field,
    daytime_indicator,
    kinetic_factor_times_step,
    arrhenius_barrier,
    yield_matrix_floating,
    first_axis_position,
    final_axis_position,
):
    species = vertical_profiles.shape[0]
    flattened = vertical_profiles.reshape(species, -1)
    reciprocal_specific_warmth = (300.0 / cell_kelvin_field).reshape(1, -1) - 1.0
    constants = kinetic_factor_times_step[:, None] * jnp.exp(
        -arrhenius_barrier[:, None] * reciprocal_specific_warmth
    )
    for kinetics_minor_step in range(daytime_indicator.shape[0]):
        switched_on = (
            jnp.broadcast_to(
                daytime_indicator[kinetics_minor_step][None], cell_kelvin_field.shape
            ).reshape(1, -1)
            > 0.5
        )

        def advance(current):
            rates = (
                constants
                * jnp.take(current, first_axis_position, axis=0)
                * jnp.take(current, final_axis_position, axis=0)
            )
            change = jnp.dot(yield_matrix_floating.T, rates, precision=lax.Precision.HIGHEST)
            return jnp.where(switched_on, current + change, current)

        flattened = lax.cond(jnp.any(switched_on), advance, lambda current: current, flattened)
    return flattened.reshape(vertical_profiles.shape)


def back_to_levels(vertical_profiles):
    return lax.all_to_all(vertical_profiles, "lev", split_axis=1, concat_axis=3, tiled=True)


def body(
    species_fractions,
    cell_flow_ratios,
    layer_pressure_depth,
    layer_thickness_fraction,
    cell_kelvin_field,
    daytime_indicator,
    kinetic_factor_times_step,
    arrhenius_barrier,
    species_yield_matrix,
    reagent_pairs,
):
    band_rows = species_fractions.shape[2]
    lat_start = lax.axis_index("lat") * band_rows
    lat_total = band_rows * lax.axis_size("lat")
    tracer = species_fractions
    merid_wind = padded_2(cell_flow_ratios[1], (("lat", 1),), 1)
    merid_wind = jnp.pad(merid_wind, ((0, 0), (1, 1), (0, 0)))
    global_row = lat_start + jnp.arange(band_rows + 4, dtype=jnp.int32) - 2
    rim_mask = ((global_row >= 1) & (global_row <= lat_total - 1)).astype(jnp.float32)
    for sweep_index in range(2):
        tracer = lon_update(tracer, cell_flow_ratios[0])
        padded = padded_2(tracer, (("lat", 2),), 2)
        tracer = lat_update(padded, merid_wind, rim_mask)
    vertical_profiles = lax.all_to_all(tracer, "lev", split_axis=3, concat_axis=1, tiled=True)
    vertical_profiles = remap(vertical_profiles, layer_pressure_depth, layer_thickness_fraction)
    yield_matrix_floating = species_yield_matrix.astype(jnp.float32)
    first_axis_position = reagent_pairs[0]
    final_axis_position = reagent_pairs[1]
    mask_float = daytime_indicator.astype(jnp.float32)
    ghost_border_cells = vertical_profiles.shape[3] // 2
    kept_block = react_block(
        vertical_profiles[..., :ghost_border_cells],
        cell_kelvin_field[..., :ghost_border_cells],
        mask_float[..., :ghost_border_cells],
        kinetic_factor_times_step,
        arrhenius_barrier,
        yield_matrix_floating,
        first_axis_position,
        final_axis_position,
    )
    species = vertical_profiles.shape[0]
    level_list = vertical_profiles.shape[1]
    stacked_rows = species * level_list
    outgoing = jnp.concatenate(
        [
            vertical_profiles[..., ghost_border_cells:].reshape(stacked_rows, band_rows, -1),
            cell_kelvin_field[..., ghost_border_cells:],
            mask_float[..., ghost_border_cells:],
        ],
        axis=0,
    )
    partner_bit = lax.axis_size("lev").bit_length() - 2
    incoming = swapped(outgoing, "lev", partner_bit)
    guest_block = react_block(
        incoming[:stacked_rows].reshape(species, level_list, band_rows, -1),
        incoming[stacked_rows : stacked_rows + level_list],
        incoming[stacked_rows + level_list :],
        kinetic_factor_times_step,
        arrhenius_barrier,
        yield_matrix_floating,
        first_axis_position,
        final_axis_position,
    )
    returned = swapped(guest_block, "lev", partner_bit)
    vertical_profiles = jnp.concatenate([kept_block, returned], axis=3)
    return back_to_levels(vertical_profiles)


def solution(mesh):
    placed = (
        P(None, "lev", "lat", None),
        P(None, "lev", "lat", None),
        P(None, "lat", "lev"),
        P(),
        P(None, "lat", "lev"),
        P(None, "lat", "lev"),
        P(),
        P(),
        P(),
        P(),
    )
    return jax.shard_map(
        body, mesh=mesh, in_specs=placed, out_specs=P(None, "lev", "lat", None), check_vma=False
    )
```

profile of v0, /device:TPU:0, one launch (start us, length us, event | category | flops | bytes accessed | tf_op | source)
XLA Modules:
  0.0 134.8 jit_solution(13841183734667816932)
XLA Ops:
  0.0 1.3 fusion.106
  1.3 1.2 fusion.107
  4.3 1.3 collective-permute-start.3
  5.6 3.0 %collective-permute-start.2 = (f32[32,4,2,128]{3,0,2,1:T(8,128)S(1)}, f32[32,4,2,128]{3,0,2,1:T(8,128)S(1)}, u32[]{:S(2)}, u32[]{:S(2)}) collective-permute-start(f32[32,4,2,128]{3,0,2,1:T(8,128)S(1)} %get-tuple-element.296), channel_id=1, source_target_pairs={{0,8},{8,16},{16,24},{1,9},{9,17},{17,25},{2,10},{10,18},{18,26},{... | collective-permute-start | bytes 393224 | tf_op jit(solution)/shard_map/ppermute | solution.py:14
  8.7 4.5 %collective-permute-start = (f32[4,1,128]{2,1,0:T(1,128)S(1)}, f32[4,1,128]{2,1,0:T(1,128)S(1)}, u32[]{:S(2)}, u32[]{:S(2)}) collective-permute-start(f32[4,1,128]{2,1,0:T(1,128)S(1)} %get-tuple-element.308), channel_id=1, source_target_pairs={{0,8},{8,16},{16,24},{1,9},{9,17},{17,25},{2,10},{10,18},{18,26},{... | collective-permute-start | bytes 6152 | tf_op jit(solution)/shard_map/ppermute | solution.py:14
  13.2 1.3 collective-permute-start.1
  14.8 0.6 reduce_sum.9
  15.6 0.7 fusion.99
  18.3 1.3 collective-permute-start.5
  19.6 4.6 %collective-permute-start.4 = (f32[32,4,2,128]{3,0,2,1:T(8,128)S(1)}, f32[32,4,2,128]{3,0,2,1:T(8,128)S(1)}, u32[]{:S(2)}, u32[]{:S(2)}) collective-permute-start(f32[32,4,2,128]{3,0,2,1:T(8,128)S(1)} %get-tuple-element.290), channel_id=1, source_target_pairs={{0,8},{8,16},{16,24},{1,9},{9,17},{17,25},{2,10},{10,18},{18,26},{... | collective-permute-start | bytes 393224 | tf_op jit(solution)/shard_map/ppermute | solution.py:14
  24.4 0.8 collective-permute-done.4
  25.6 0.6 copy.291
  26.2 1.4 %reshape.417 = f32[8,1,8192]{2,1,0:T(1,128)} reshape(f32[128,4,4,32]{3,2,1,0:T(4,128)S(1)} %bitcast.108) | data formatting | bytes 524288
  27.6 5.8 %all-to-all-start = ((f32[8,1,8192]{2,1,0:T(1,128)}), f32[8,1,8192]{2,1,0:T(1,128)S(1)}, u32[]{:S(2)}, u32[]{:S(2)}) async-start(f32[8,1,8192]{2,1,0:T(1,128)} %reshape.417), calls=%async_computation | async-start | bytes 524288 | tf_op jit(solution)/shard_map/all_to_all | solution.py:156
  33.4 0.7 pad_maximum_fusion.11
  34.4 7.4 %all-to-all-done = f32[8,1,8192]{2,1,0:T(1,128)S(1)} async-done(((f32[8,1,8192]{2,1,0:T(1,128)}), f32[8,1,8192]{2,1,0:T(1,128)S(1)}, u32[]{:S(2)}, u32[]{:S(2)}) %all-to-all-start) | async-done | bytes 262176 | tf_op jit(solution)/shard_map/all_to_all | solution.py:156
  41.8 0.5 broadcast.361
  42.3 1.2 reduce.32
  43.5 0.5 reshape.418
  44.5 2.8 %fusion.48 = f32[32,32,4,16]{1,0,3,2:T(8,128)S(1)} fusion(f32[32,32,4,16]{0,3,2,1:T(8,128)S(1)} %bitcast.119, f32[32,4,16]{0,2,1:T(8,128)S(1)} %get-tuple-element.320, f32[32,4,16]{0,2,1:T(8,128)S(1)} %get-tuple-element.319, f32[32,4,16]{0,2,1:T(8,128)S(1)} %concatenate.101.clone, f32[32,4,16]{0,2,1:T(8,128)S(1)} %get-tuple-element.318, ...), kind=kOutput, calls=%fused_computation.139 | convolution fusion | flops 25493504 | bytes 565248 | tf_op jit(solution)/shard_map/ts...,ns...->nt.../dot_general | solution.py:85
  47.3 0.9 fusion.101
  48.6 2.2 %collective-permute-start.6 = (f32[1060,4,8]{0,2,1:T(8,128)S(1)}, f32[1060,4,8]{0,2,1:T(8,128)S(1)}, u32[]{:S(2)}, u32[]{:S(2)}) collective-permute-start(f32[1060,4,8]{0,2,1:T(8,128)S(1)} %concatenate.103), channel_id=1, source_target_pairs={{0,4},{4,0},{1,5},{5,1},{2,6},{6,2},{3,7},{7,3},{8,12},{12,8},{9,1... | collective-permute-start | bytes 407048 | tf_op jit(solution)/shard_map/ppermute | solution.py:27
  51.5 0.8 broadcast_reduce_fusion.7
  52.3 6.9 %collective-permute-done.6 = f32[1060,4,8]{0,2,1:T(8,128)S(1)} collective-permute-done((f32[1060,4,8]{0,2,1:T(8,128)S(1)}, f32[1060,4,8]{0,2,1:T(8,128)S(1)}, u32[]{:S(2)}, u32[]{:S(2)}) %collective-permute-start.6) | collective-permute-done | bytes 135712 | tf_op jit(solution)/shard_map/ppermute | solution.py:27
  59.3 0.7 broadcast_reduce_fusion.3
  61.1 0.7 broadcast_reduce_fusion.2
  62.4 0.7 broadcast_reduce_fusion.1
  63.8 0.7 broadcast_reduce_fusion
  65.2 0.8 copy.305
  66.0 2.5 %reshape_reshape.6 = f32[32,1024]{1,0:T(8,128)S(1)} reshape(f32[1024,4,8]{2,1,0:T(4,128)S(1)} %copy.305) | data formatting | bytes 262144 | tf_op jit(solution)/shard_map/reshape;reshape | solution.py:102
  68.8 0.4 exponential_multiply_fusion.1
  69.2 5.5 %conditional.12 = (f32[32,1024]{1,0:T(8,128)S(1)}) conditional(s32[]{:T(128)} %convert_element_type.42, f32[32,1024]{1,0:T(8,128)S(1)} %reshape_reshape.6, (pred[4,8]{1,0:T(4,128)(4,1)S(1)}, f32[32,1024]{1,0:T(8,128)S(1)}, s32[256]{0:T(256)S(1)}, f32[256,1024]{1,0:T(8,128)S(1)}, s32[256]{0:T(256)S(1)}, /*index=5*/f32[256,32]{1,0:T(8,128)S(1)}) %tuple.149), branch_computations={%region_19.21_spmd, %region_20.22_spmd} | conditional | flops 101784064 | bytes 7658536 | solution.py:124
  69.3 1.1 gather_fusion.9
  70.3 2.0 %gather_fusion.8 = f32[256,1024]{1,0:T(8,128)} fusion(f32[32,1024]{1,0:T(8,128)S(1)} %get-tuple-element.176, s32[1024]{0:T(1024)S(1)} %pad_clamp_fusion.7), kind=kCustom, calls=%fused_computation.8.clone | custom fusion | bytes 2098176 | tf_op jit(solution)/shard_map/cond/branch_1_fun/jit(_take)/gather | solution.py:118
  72.5 2.2 %fusion.19 = f32[32,1024]{1,0:T(8,128)S(1)} fusion(f32[32,1024]{1,0:T(8,128)S(1)} %get-tuple-element.176, f32[256,32]{1,0:T(8,128)S(1)} %get-tuple-element.180, f32[256,1024]{1,0:T(8,128)S(1)} %gather_fusion.9, f32[256,1024]{1,0:T(8,128)S(1)} %get-tuple-element.177, f32[256,1024]{1,0:T(8,128)} %gather_fusion.8, pred[256]{0:T(512)(128)(4,1)S(1)} %get-tuple-element.270, ...), kind=kOutput, calls=%fused_computation.63 | convolution fusion | flops 101777408 | bytes 3442176 | tf_op jit(solution)/shard_map/cond/branch_1_fun/dot_general | solution.py:121
  74.7 5.7 %conditional.13 = (f32[32,1024]{1,0:T(8,128)S(1)}) conditional(s32[]{:T(128)} %convert_element_type.41, f32[32,1024]{1,0:T(8,128)S(1)} %get-tuple-element.330, (pred[4,8]{1,0:T(4,128)(4,1)S(1)}, f32[32,1024]{1,0:T(8,128)S(1)}, s32[256]{0:T(256)S(1)}, f32[256,1024]{1,0:T(8,128)S(1)}, s32[256]{0:T(256)S(1)}, ...), branch_computations={%region_21.23_spmd, %region_22.24_spmd} | conditional | flops 101784064 | bytes 7658536 | solution.py:124
  75.0 1.1 gather_fusion.11
  76.1 2.0 %gather_fusion.10 = f32[256,1024]{1,0:T(8,128)} fusion(f32[32,1024]{1,0:T(8,128)S(1)} %get-tuple-element.182, s32[1024]{0:T(1024)S(1)} %pad_clamp_fusion.9), kind=kCustom, calls=%fused_computation.10.clone | custom fusion | bytes 2098176 | tf_op jit(solution)/shard_map/cond/branch_1_fun/jit(_take)/gather | solution.py:118
  78.2 2.2 %fusion.25 = f32[32,1024]{1,0:T(8,128)S(1)} fusion(f32[32,1024]{1,0:T(8,128)S(1)} %get-tuple-element.182, f32[256,32]{1,0:T(8,128)S(1)} %get-tuple-element.186, f32[256,1024]{1,0:T(8,128)S(1)} %gather_fusion.11, f32[256,1024]{1,0:T(8,128)S(1)} %get-tuple-element.183, f32[256,1024]{1,0:T(8,128)} %gather_fusion.10, pred[256]{0:T(512)(128)(4,1)S(1)} %get-tuple-element.274, ...), kind=kOutput, calls=%fused_computation.78 | convolution fusion | flops 101777408 | bytes 3442176 | tf_op jit(solution)/shard_map/cond/branch_1_fun/dot_general | solution.py:121
  80.5 5.5 %conditional.14 = (f32[32,1024]{1,0:T(8,128)S(1)}) conditional(s32[]{:T(128)} %convert_element_type.40, f32[32,1024]{1,0:T(8,128)S(1)} %get-tuple-element.331, (pred[4,8]{1,0:T(4,128)(4,1)S(1)}, f32[32,1024]{1,0:T(8,128)S(1)}, s32[256]{0:T(256)S(1)}, f32[256,1024]{1,0:T(8,128)S(1)}, s32[256]{0:T(256)S(1)}, ...), branch_computations={%region_23.25_spmd, %region_24.26_spmd} | conditional | flops 101784064 | bytes 7658536 | solution.py:124
  80.5 1.1 gather_fusion.13
  81.6 2.0 %gather_fusion.12 = f32[256,1024]{1,0:T(8,128)} fusion(f32[32,1024]{1,0:T(8,128)S(1)} %get-tuple-element.188, s32[1024]{0:T(1024)S(1)} %pad_clamp_fusion.11), kind=kCustom, calls=%fused_computation.12.clone | custom fusion | bytes 2098176 | tf_op jit(solution)/shard_map/cond/branch_1_fun/jit(_take)/gather | solution.py:118
  83.8 2.2 %fusion.31 = f32[32,1024]{1,0:T(8,128)S(1)} fusion(f32[32,1024]{1,0:T(8,128)S(1)} %get-tuple-element.188, f32[256,32]{1,0:T(8,128)S(1)} %get-tuple-element.192, f32[256,1024]{1,0:T(8,128)S(1)} %gather_fusion.13, f32[256,1024]{1,0:T(8,128)S(1)} %get-tuple-element.189, f32[256,1024]{1,0:T(8,128)} %gather_fusion.12, pred[256]{0:T(512)(128)(4,1)S(1)} %get-tuple-element.278, ...), kind=kOutput, calls=%fused_computation.93 | convolution fusion | flops 101777408 | bytes 3442176 | tf_op jit(solution)/shard_map/cond/branch_1_fun/dot_general | solution.py:121
  86.0 5.6 %conditional.15 = (f32[32,1024]{1,0:T(8,128)S(1)}) conditional(s32[]{:T(128)} %convert_element_type.39, f32[32,1024]{1,0:T(8,128)S(1)} %get-tuple-element.332, (f32[4,8]{1,0:T(4,128)S(1)}, f32[1,1024]{1,0:T(1,128)S(1)}, f32[32,1024]{1,0:T(8,128)S(1)}, s32[256]{0:T(256)S(1)}, f32[256,1024]{1,0:T(8,128)S(1)}, /*index=5*/s32[256]{0:T(256)S(1)}, ...), branch_computations={%region_25.27_spmd, %region_26.28_spmd} | conditional | flops 101785088 | bytes 7677064 | solution.py:124
  86.1 1.1 gather_fusion.15
  87.2 2.0 %gather_fusion.14 = f32[256,1024]{1,0:T(8,128)} fusion(f32[32,1024]{1,0:T(8,128)S(1)} %get-tuple-element.195, s32[1024]{0:T(1024)S(1)} %pad_clamp_fusion.15), kind=kCustom, calls=%fused_computation.14.clone | custom fusion | bytes 2098176 | tf_op jit(solution)/shard_map/cond/branch_1_fun/jit(_take)/gather | solution.py:118
  89.4 2.2 %fusion.43 = f32[32,1024]{1,0:T(8,128)S(1)} fusion(f32[32,1024]{1,0:T(8,128)S(1)} %get-tuple-element.195, f32[256,32]{1,0:T(8,128)S(1)} %get-tuple-element.199, f32[256,1024]{1,0:T(8,128)S(1)} %gather_fusion.15, f32[256,1024]{1,0:T(8,128)S(1)} %get-tuple-element.196, f32[256,1024]{1,0:T(8,128)} %gather_fusion.14, ...), kind=kOutput, calls=%fused_computation.124 | convolution fusion | flops 101777408 | bytes 3442176 | tf_op jit(solution)/shard_map/cond/branch_1_fun/dot_general | solution.py:121
  91.6 1.0 copy.307
  92.6 0.7 broadcast_reduce_fusion.6
  94.7 0.8 broadcast_reduce_fusion.4
  96.8 1.5 %copy.299 = f32[32,32,4,8]{0,3,2,1:T(8,128)S(1)} copy(f32[32,32,4,8]{1,0,3,2:T(8,128)} %get-tuple-element.288) | data formatting | bytes 262144 | tf_op jit(solution)/shard_map/slice | solution.py:164
  98.3 5.3 %conditional.8 = (f32[32,1024]{1,0:T(8,128)S(1)}) conditional(s32[]{:T(128)} %convert_element_type.37, (f32[32,1024]{0,1:T(8,128)S(1)}) %tuple.139, (pred[4,8]{1,0:T(4,128)(4,1)S(1)}, f32[32,1024]{0,1:T(8,128)S(1)}, s32[256]{0:T(256)S(1)}, f32[256,1024]{1,0:T(8,128)S(1)}, s32[256]{0:T(256)S(1)}, /*index=5*/f32[256,32]{1,0:T(8,128)S(1)}) %tuple.153), branch_computations={%region_7.8_spmd, %region_8.10_spmd} | conditional | flops 101784064 | bytes 7920992 | solution.py:124
  98.5 1.1 gather_fusion.1
  99.6 1.1 gather_fusion
  100.7 0.5 compare_and_fusion
  101.3 0.7 broadcast_in_dim.127
  102.0 1.7 %fusion.1 = f32[32,1024]{1,0:T(8,128)S(1)} fusion(f32[32,1024]{1,0:T(8,128)S(1)} %copy.303, f32[256,32]{1,0:T(8,128)S(1)} %get-tuple-element.155, f32[256,1024]{1,0:T(8,128)S(1)} %gather_fusion.1, f32[256,1024]{1,0:T(8,128)S(1)} %get-tuple-element.152, f32[256,1024]{1,0:T(8,128)S(1)} %gather_fusion, pred[256]{0:T(512)(128)(4,1)} %get-tuple-element.258, ...), kind=kOutput, calls=%fused_computation.18 | convolution fusion | flops 101777408 | bytes 3442176 | tf_op jit(solution)/shard_map/cond/branch_1_fun/dot_general | solution.py:121
  103.7 0.6 copy-done.14
  104.5 13.4 %collective-permute-done.7 = f32[32,32,4,8]{0,3,2,1:T(8,128)} collective-permute-done((f32[32,32,4,8]{0,3,2,1:T(8,128)}, f32[32,32,4,8]{0,3,2,1:T(8,128)}, u32[]{:S(2)}, u32[]{:S(2)}) %collective-permute-start.7) | collective-permute-done | bytes 131104 | tf_op jit(solution)/shard_map/ppermute | solution.py:27
  117.9 1.3 fusion.112
  119.2 0.5 reshape.419
  119.7 12.4 %all_to_all.36 = f32[8,1,8192]{2,1,0:T(1,128)S(1)} all-to-all(f32[8,1,8192]{2,1,0:T(1,128)S(1)} %reshape.419), channel_id=1, replica_groups=mesh['lat'=4,'lev'=8] {'lev'}, dimensions={0} | all-to-all | bytes 524288 | tf_op jit(solution)/shard_map/all_to_all | solution.py:129
  132.1 1.2 reduce.33
  133.7 1.0 copy.309
  (149 shorter events, 8.7 us)
Async XLA Ops:
  0.0 3.0 %copy-start = (f32[32,4,4,128]{3,2,1,0:T(4,128)S(1)}, f32[32,4,4,128]{3,2,1,0:T(4,128)}, u32[]{:S(2)}) copy-start(f32[32,4,4,128]{3,2,1,0:T(4,128)} %param.28) | copy-start | bytes 786436
  0.0 2.5 %copy-start.4 = (f32[2,4,4,128]{3,2,1,0:T(4,128)S(1)}, f32[2,4,4,128]{3,2,1,0:T(4,128)}, u32[]{:S(2)}) copy-start(f32[2,4,4,128]{3,2,1,0:T(4,128)} %param.29) | copy-start | bytes 49156
  3.7 10.9 %copy-start.5 = (f32[32,4,16]{0,2,1:T(8,128)S(1)}, f32[32,4,16]{0,2,1:T(8,128)}, u32[]{:S(2)}) copy-start(f32[32,4,16]{0,2,1:T(8,128)} %param.30) | copy-start | bytes 24580
  3.7 11.0 %copy-start.16 = (f32[32]{0:T(128)S(1)}, f32[32]{0:T(128)}, u32[]{:S(2)}) copy-start(f32[32]{0:T(128)} %param.31) | copy-start | bytes 388
  3.7 11.8 %copy-start.8 = (s32[4,4,16]{2,1,0:T(4,128)S(1)}, s32[4,4,16]{2,1,0:T(4,128)}, u32[]{:S(2)}) copy-start(s32[4,4,16]{2,1,0:T(4,128)} %param.33) | copy-start | bytes 3076
  3.7 11.9 %copy-start.15 = (s32[2,256]{1,0:T(2,128)S(1)}, s32[2,256]{1,0:T(2,128)}, u32[]{:S(2)}) copy-start(s32[2,256]{1,0:T(2,128)} %param.37) | copy-start | bytes 6148
  4.3 12.4 %collective-permute-start.3 = (f32[32,4,2,128]{3,0,2,1:T(8,128)S(1)}, f32[32,4,2,128]{3,0,2,1:T(8,128)S(1)}, u32[]{:S(2)}, u32[]{:S(2)}) collective-permute-start(f32[32,4,2,128]{3,0,2,1:T(8,128)S(1)} %get-tuple-element.297), channel_id=1, source_target_pairs={{8,0},{16,8},{24,16},{9,1},{17,9},{25,17},{10,2},{18,10},{26,18},{... | collective-permute-start | bytes 393224 | tf_op jit(solution)/shard_map/ppermute | solution.py:15
  5.6 11.1 %collective-permute-start.2 = (f32[32,4,2,128]{3,0,2,1:T(8,128)S(1)}, f32[32,4,2,128]{3,0,2,1:T(8,128)S(1)}, u32[]{:S(2)}, u32[]{:S(2)}) collective-permute-start(f32[32,4,2,128]{3,0,2,1:T(8,128)S(1)} %get-tuple-element.296), channel_id=1, source_target_pairs={{0,8},{8,16},{16,24},{1,9},{9,17},{17,25},{2,10},{10,18},{18,26},{... | collective-permute-start | bytes 393224 | tf_op jit(solution)/shard_map/ppermute | solution.py:14
  8.7 7.8 %collective-permute-start = (f32[4,1,128]{2,1,0:T(1,128)S(1)}, f32[4,1,128]{2,1,0:T(1,128)S(1)}, u32[]{:S(2)}, u32[]{:S(2)}) collective-permute-start(f32[4,1,128]{2,1,0:T(1,128)S(1)} %get-tuple-element.308), channel_id=1, source_target_pairs={{0,8},{8,16},{16,24},{1,9},{9,17},{17,25},{2,10},{10,18},{18,26},{... | collective-permute-start | bytes 6152 | tf_op jit(solution)/shard_map/ppermute | solution.py:14
  13.2 3.4 %collective-permute-start.1 = (f32[4,1,128]{2,1,0:T(1,128)S(1)}, f32[4,1,128]{2,1,0:T(1,128)S(1)}, u32[]{:S(2)}, u32[]{:S(2)}) collective-permute-start(f32[4,1,128]{2,1,0:T(1,128)S(1)} %get-tuple-element.309), channel_id=1, source_target_pairs={{8,0},{16,8},{24,16},{9,1},{17,9},{25,17},{10,2},{18,10},{26,18},{... | collective-permute-start | bytes 6152 | tf_op jit(solution)/shard_map/ppermute | solution.py:15
  15.6 18.6 %copy-start.2 = (f32[4,4,16]{0,2,1:T(8,128)}, f32[4,4,16]{0,2,1:T(8,128)S(1)}, u32[]{:S(2)}) copy-start(f32[4,4,16]{0,2,1:T(8,128)S(1)} %convert_element_type.33) | copy-start | bytes 3076
  18.3 6.0 %collective-permute-start.5 = (f32[32,4,2,128]{3,0,2,1:T(8,128)S(1)}, f32[32,4,2,128]{3,0,2,1:T(8,128)S(1)}, u32[]{:S(2)}, u32[]{:S(2)}) collective-permute-start(f32[32,4,2,128]{3,0,2,1:T(8,128)S(1)} %get-tuple-element.291), channel_id=1, source_target_pairs={{8,0},{16,8},{24,16},{9,1},{17,9},{25,17},{10,2},{18,10},{26,18},{... | collective-permute-start | bytes 393224 | tf_op jit(solution)/shard_map/ppermute | solution.py:15
  19.6 5.6 %collective-permute-start.4 = (f32[32,4,2,128]{3,0,2,1:T(8,128)S(1)}, f32[32,4,2,128]{3,0,2,1:T(8,128)S(1)}, u32[]{:S(2)}, u32[]{:S(2)}) collective-permute-start(f32[32,4,2,128]{3,0,2,1:T(8,128)S(1)} %get-tuple-element.290), channel_id=1, source_target_pairs={{0,8},{8,16},{16,24},{1,9},{9,17},{17,25},{2,10},{10,18},{18,26},{... | collective-permute-start | bytes 393224 | tf_op jit(solution)/shard_map/ppermute | solution.py:14
  25.5 8.8 %copy-start.7 = (f32[32,4,16]{0,2,1:T(8,128)S(1)}, f32[32,4,16]{0,2,1:T(8,128)}, u32[]{:S(2)}) copy-start(f32[32,4,16]{0,2,1:T(8,128)} %param.32) | copy-start | bytes 24580
  27.6 14.3 %all-to-all-start = ((f32[8,1,8192]{2,1,0:T(1,128)}), f32[8,1,8192]{2,1,0:T(1,128)S(1)}, u32[]{:S(2)}, u32[]{:S(2)}) async-start(f32[8,1,8192]{2,1,0:T(1,128)} %reshape.417), calls=%async_computation | async-start | bytes 524288 | tf_op jit(solution)/shard_map/all_to_all | solution.py:156
  47.3 1.2 slice-start
  47.3 3.5 %copy-start.3 = (f32[4,4,16]{0,2,1:T(8,128)S(1)}, f32[4,4,16]{0,2,1:T(8,128)}, u32[]{:S(2)}) copy-start(f32[4,4,16]{0,2,1:T(8,128)} %copy-done.2) | copy-start | bytes 3076
  47.3 4.0 %copy-start.18 = (f32[256]{0:T(256)S(1)}, f32[256]{0:T(256)}, u32[]{:S(2)}) copy-start(f32[256]{0:T(256)} %param.35) | copy-start | bytes 3076
  47.3 4.0 %copy-start.6 = (s32[256,32]{0,1:T(8,128)S(1)}, s32[256,32]{0,1:T(8,128)}, u32[]{:S(2)}) copy-start(s32[256,32]{0,1:T(8,128)} %param.36) | copy-start | bytes 98308
  48.6 10.6 %collective-permute-start.6 = (f32[1060,4,8]{0,2,1:T(8,128)S(1)}, f32[1060,4,8]{0,2,1:T(8,128)S(1)}, u32[]{:S(2)}, u32[]{:S(2)}) collective-permute-start(f32[1060,4,8]{0,2,1:T(8,128)S(1)} %concatenate.103), channel_id=1, source_target_pairs={{0,4},{4,0},{1,5},{5,1},{2,6},{6,2},{3,7},{7,3},{8,12},{12,8},{9,1... | collective-permute-start | bytes 407048 | tf_op jit(solution)/shard_map/ppermute | solution.py:27
  51.1 41.5 %copy-start.13 = (pred[4,8]{1,0:T(4,128)(4,1)}, pred[4,8]{1,0:T(4,128)(4,1)S(1)}, u32[]{:S(2)}) copy-start(pred[4,8]{1,0:T(4,128)(4,1)S(1)} %get-tuple-element.251) | copy-start | bytes 100
  51.1 43.5 %copy-start.9 = (pred[4,8]{1,0:T(4,128)(4,1)}, pred[4,8]{1,0:T(4,128)(4,1)S(1)}, u32[]{:S(2)}) copy-start(pred[4,8]{1,0:T(4,128)(4,1)S(1)} %get-tuple-element.250) | copy-start | bytes 100
  65.2 3.6 %copy-start.17 = (f32[256]{0:T(256)S(1)}, f32[256]{0:T(256)}, u32[]{:S(2)}) copy-start(f32[256]{0:T(256)} %param.34) | copy-start | bytes 3076
  92.6 25.3 %collective-permute-start.7 = (f32[32,32,4,8]{0,3,2,1:T(8,128)}, f32[32,32,4,8]{0,3,2,1:T(8,128)}, u32[]{:S(2)}, u32[]{:S(2)}) collective-permute-start(f32[32,32,4,8]{0,3,2,1:T(8,128)} %bitcast.26), channel_id=1, source_target_pairs={{0,4},{4,0},{1,5},{5,1},{2,6},{6,2},{3,7},{7,3},{8,12},{12,8},{9,1... | collective-permute-start | bytes 393224 | tf_op jit(solution)/shard_map/ppermute | solution.py:27
  98.3 1.3 copy-start.11
  99.6 1.6 %copy-start.12 = (pred[4,8]{1,0:T(4,128)(4,1)S(1)}, pred[4,8]{1,0:T(4,128)(4,1)}, u32[]{:S(2)}) copy-start(pred[4,8]{1,0:T(4,128)(4,1)} %copy-done.11) | copy-start | bytes 100 | tf_op jit(solution)/shard_map/cond
  103.6 0.6 copy-start.14
  104.5 13.4 %copy-start.1 = (f32[32,32,4,8]{0,3,2,1:T(8,128)}, f32[32,32,4,8]{0,3,2,1:T(8,128)S(1)}, u32[]{:S(2)}) copy-start(f32[32,32,4,8]{0,3,2,1:T(8,128)S(1)} %get-tuple-element.206) | copy-start | bytes 393220
where the time goes:
time: 135 us
  local copies, waits for them, and re-layouts  34.4 us (25%)
  waiting for transfers between devices  28.6 us (21%)
  starting transfers between devices  24 us (18%)
  other arithmetic  15.4 us (11%)
  matrix products  13.4 us (10%)
  blocking collectives  12.4 us (9%)
  between operations  6 us (4%)
    ppermute x2, waiting for transfers between devices, swapped(): return lax.ppermute(block, axis, route)  20.3 us
    all_to_all x1, blocking collectives, back_to_levels(): lax.all_to_all(vertical_profiles, 'lev', split_axis=1, concat_axis=3, til...  12.4 us
    ppermute x3, starting transfers between devices, padded_2(): before = lax.ppermute(last, axis, up)  12.1 us
    dot_general x5, matrix products, advance(): jnp.dot(yield_matrix_floating.T, rates, precision=lax.Precision.HIGHEST)  10.6 us
    gather x5, local copies, waits for them, and re-layouts, advance(): jnp.take(current, first_axis_position, axis=0)  9.16 us
    all_to_all x1, waiting for transfers between devices, body(): lax.all_to_all(tracer, 'lev', split_axis=3, concat_axis=1, tiled=True)  7.4 us
    all_to_all x1, starting transfers between devices, body(): lax.all_to_all(tracer, 'lev', split_axis=3, concat_axis=1, tiled=True)  5.81 us
    gather x5, local copies, waits for them, and re-layouts, advance(): jnp.take(current, final_axis_position, axis=0)  5.36 us
  transfers between devices with their start and end apart: 9, of which 4 were waited for; matrix products, arithmetic and copies ran while one was open for 10% of the time, Pallas kernels for 0%

commit v1 on v0

--- a/solution.py
+++ b/solution.py
@@ -15,16 +15,6 @@
         after = lax.ppermute(first, axis, down)
         value = jnp.concatenate([before, value, after], axis=dim)
     return value
-
-
-def swapped(block, axis, apart):
-    count = lax.axis_size(axis)
-    route = []
-    for low in range(count):
-        high = low | 1 << apart
-        if high != low and high < count:
-            route += [(low, high), (high, low)]
-    return lax.ppermute(block, axis, route)
 
 
 def minmod(left, right):
@@ -66,13 +56,20 @@
     return padded[..., 2 : row_count - 2, :] - (fluxes[..., 1:, :] - fluxes[..., :-1, :])
 
 
+def running_sum(value):
+    rows = [value[0]]
+    for item in range(1, value.shape[0]):
+        rows.append(rows[-1] + value[item])
+    return jnp.stack(rows)
+
+
 def remap(vertical_profiles, layer_pressure_depth, layer_thickness_fraction):
-    upper_edge = jnp.cumsum(layer_pressure_depth, axis=0)
+    upper_edge = running_sum(layer_pressure_depth)
     lower_edge = jnp.concatenate([jnp.zeros_like(upper_edge[:1]), upper_edge[:-1]], axis=0)
     column_total = upper_edge[-1]
     expand = (slice(None),) + (None,) * column_total.ndim
     share_sum = jnp.sum(layer_thickness_fraction)
-    fraction_top = jnp.cumsum(layer_thickness_fraction) / share_sum
+    fraction_top = running_sum(layer_thickness_fraction) / share_sum
     fraction_bottom = jnp.concatenate([jnp.zeros((1,), fraction_top.dtype), fraction_top[:-1]])
     target_top = fraction_top[expand] * column_total[None]
     target_bottom = fraction_bottom[expand] * column_total[None]
@@ -112,16 +109,13 @@
             > 0.5
         )
 
-        def advance(current):
-            rates = (
-                constants
-                * jnp.take(current, first_axis_position, axis=0)
-                * jnp.take(current, final_axis_position, axis=0)
-            )
-            change = jnp.dot(yield_matrix_floating.T, rates, precision=lax.Precision.HIGHEST)
-            return jnp.where(switched_on, current + change, current)
-
-        flattened = lax.cond(jnp.any(switched_on), advance, lambda current: current, flattened)
+        rates = (
+            constants
+            * jnp.take(flattened, first_axis_position, axis=0)
+            * jnp.take(flattened, final_axis_position, axis=0)
+        )
+        change = jnp.dot(yield_matrix_floating.T, rates, precision=lax.Precision.HIGHEST)
+        flattened = jnp.where(switched_on, flattened + change, flattened)
     return flattened.reshape(vertical_profiles.shape)
 
 
@@ -159,42 +153,16 @@
     first_axis_position = reagent_pairs[0]
     final_axis_position = reagent_pairs[1]
     mask_float = daytime_indicator.astype(jnp.float32)
-    ghost_border_cells = vertical_profiles.shape[3] // 2
-    kept_block = react_block(
-        vertical_profiles[..., :ghost_border_cells],
-        cell_kelvin_field[..., :ghost_border_cells],
-        mask_float[..., :ghost_border_cells],
+    vertical_profiles = react_block(
+        vertical_profiles,
+        cell_kelvin_field,
+        mask_float,
         kinetic_factor_times_step,
         arrhenius_barrier,
         yield_matrix_floating,
         first_axis_position,
         final_axis_position,
     )
-    species = vertical_profiles.shape[0]
-    level_list = vertical_profiles.shape[1]
-    stacked_rows = species * level_list
-    outgoing = jnp.concatenate(
-        [
-            vertical_profiles[..., ghost_border_cells:].reshape(stacked_rows, band_rows, -1),
-            cell_kelvin_field[..., ghost_border_cells:],
-            mask_float[..., ghost_border_cells:],
-        ],
-        axis=0,
-    )
-    partner_bit = lax.axis_size("lev").bit_length() - 2
-    incoming = swapped(outgoing, "lev", partner_bit)
-    guest_block = react_block(
-        incoming[:stacked_rows].reshape(species, level_list, band_rows, -1),
-        incoming[stacked_rows : stacked_rows + level_list],
-        incoming[stacked_rows + level_list :],
-        kinetic_factor_times_step,
-        arrhenius_barrier,
-        yield_matrix_floating,
-        first_axis_position,
-        final_axis_position,
-    )
-    returned = swapped(guest_block, "lev", partner_bit)
-    vertical_profiles = jnp.concatenate([kept_block, returned], axis=3)
     return back_to_levels(vertical_profiles)
 
 

time: 135 us -> 126 us (0.933)
  waiting for transfers between devices: 28.6 us -> 9.85 us
  between operations: 6 us -> 20.6 us
  other arithmetic: 15.4 us -> 7.94 us
  matrix products: 13.4 us -> 18 us
  starting transfers between devices: 24 us -> 21.6 us
  blocking collectives: 12.4 us -> 14.4 us
  local copies, waits for them, and re-layouts: 34.4 us -> 32.7 us
    ppermute x2 -> x0, waiting for transfers between devices: 20.3 us -> none  [swapped(): return lax.ppermute(block, axis, route)]
    reduce_or x7 -> x0, other arithmetic: 5.12 us -> none  [react_block(): jnp.any(switched_on)]
    dot_general x5 -> x4, matrix products: 10.6 us -> 15.2 us  [react_block(): jnp.dot(yield_matrix_floating.T, rates, precision=lax.Precision.HIGHEST)]
    gather x10 -> x8, local copies, waits for them, and re-layouts: 14.5 us -> 17.8 us  [the longest x4 10.7 us: react_block(): jnp.take(flattened, first_axis_position, axis=0)]
    ppermute x3, waiting for transfers between devices: 0.01 us -> 3.14 us  [padded_2(): after = lax.ppermute(first, axis, down)]
    slice x11 -> x3, local copies, waits for them, and re-layouts: 3.73 us -> 1.43 us  [the longest x2 1.42 us: running_sum(): rows.append(rows[-1] + value[item])]
    ppermute x2 -> x0, starting transfers between devices: 2.2 us -> none  [swapped(): return lax.ppermute(block, axis, route)]
    all_to_all x1, blocking collectives: 12.4 us -> 14.4 us  [back_to_levels(): lax.all_to_all(vertical_profiles, 'lev', split_axis=1, concat_axis=3, til...]
  transfers between devices with their start and end apart: 9 -> 7, of which waited for: 4 -> 2; matrix products, arithmetic and copies ran while one was open for 10% -> 8% of each run, Pallas kernels for 0% -> 0%
where the time goes in v1:
time: 126 us; the launch traced here: 125 us
  local copies, waits for them, and re-layouts  32.7 us (26%)
  starting transfers between devices  21.6 us (17%)
  between operations  20.6 us (16%)
  matrix products  18 us (14%)
  blocking collectives  14.4 us (11%)
  waiting for transfers between devices  9.85 us (8%)
  other arithmetic  7.94 us (6%)
    dot_general x4, matrix products, react_block(): jnp.dot(yield_matrix_floating.T, rates, precision=lax.Precision.HIGHEST)  15.2 us
    all_to_all x1, blocking collectives, back_to_levels(): lax.all_to_all(vertical_profiles, 'lev', split_axis=1, concat_axis=3, til...  14.4 us
    ppermute x3, starting transfers between devices, padded_2(): before = lax.ppermute(last, axis, up)  11.8 us
    gather x4, local copies, waits for them, and re-layouts, react_block(): jnp.take(flattened, first_axis_position, axis=0)  10.7 us
    gather x4, local copies, waits for them, and re-layouts, react_block(): jnp.take(flattened, final_axis_position, axis=0)  7.06 us
    all_to_all x1, waiting for transfers between devices, body(): lax.all_to_all(tracer, 'lev', split_axis=3, concat_axis=1, tiled=True)  6.7 us
    all_to_all x1, starting transfers between devices, body(): lax.all_to_all(tracer, 'lev', split_axis=3, concat_axis=1, tiled=True)  5.81 us
    ppermute x3, starting transfers between devices, padded_2(): after = lax.ppermute(first, axis, down)  4.01 us
  transfers between devices with their start and end apart: 7, of which 2 were waited for; matrix products, arithmetic and copies ran while one was open for 8% of the time, Pallas kernels for 0%

profile of v1, /device:TPU:0, one launch (start us, length us, event | category | flops | bytes accessed | tf_op | source)
XLA Modules:
  0.0 125.1 jit_solution(11511658015366495742)
XLA Ops:
  0.0 0.7 slice_bitcast_fusion.1
  0.8 0.8 multiply_bitcast_fusion.1
  1.6 2.4 %collective-permute-start = (f32[4,1,128]{2,1,0:T(1,128)S(1)}, f32[4,1,128]{2,1,0:T(1,128)S(1)}, u32[]{:S(2)}, u32[]{:S(2)}) collective-permute-start(f32[4,1,128]{2,1,0:T(1,128)S(1)} %get-tuple-element.63), channel_id=1, source_target_pairs={{0,8},{8,16},{16,24},{1,9},{9,17},{17,25},{2,10},{10,18},{18,26},{... | collective-permute-start | bytes 6152 | tf_op jit(solution)/shard_map/ppermute | solution.py:14
  4.0 1.4 %collective-permute-start.1 = (f32[4,1,128]{2,1,0:T(1,128)S(1)}, f32[4,1,128]{2,1,0:T(1,128)S(1)}, u32[]{:S(2)}, u32[]{:S(2)}) collective-permute-start(f32[4,1,128]{2,1,0:T(1,128)S(1)} %get-tuple-element.64), channel_id=1, source_target_pairs={{8,0},{16,8},{24,16},{9,1},{17,9},{25,17},{10,2},{18,10},{26,18},{... | collective-permute-start | bytes 6152 | tf_op jit(solution)/shard_map/ppermute | solution.py:15
  5.4 1.2 fusion.95
  6.6 1.2 fusion.94
  8.3 0.3 minimum_multiply_fusion.3
  8.6 0.1 slice.509
  8.9 0.3 fusion.65
  9.3 0.2 fusion.66
  9.5 5.2 %collective-permute-start.2 = (f32[32,4,2,128]{3,0,2,1:T(8,128)S(1)}, f32[32,4,2,128]{3,0,2,1:T(8,128)S(1)}, u32[]{:S(2)}, u32[]{:S(2)}) collective-permute-start(f32[32,4,2,128]{3,0,2,1:T(8,128)S(1)} %get-tuple-element.32), channel_id=1, source_target_pairs={{0,8},{8,16},{16,24},{1,9},{9,17},{17,25},{2,10},{10,18},{18,26},{... | collective-permute-start | bytes 393224 | tf_op jit(solution)/shard_map/ppermute | solution.py:14
  14.7 1.3 %collective-permute-start.3 = (f32[32,4,2,128]{3,0,2,1:T(8,128)S(1)}, f32[32,4,2,128]{3,0,2,1:T(8,128)S(1)}, u32[]{:S(2)}, u32[]{:S(2)}) collective-permute-start(f32[32,4,2,128]{3,0,2,1:T(8,128)S(1)} %get-tuple-element.33), channel_id=1, source_target_pairs={{8,0},{16,8},{24,16},{9,1},{17,9},{25,17},{10,2},{18,10},{26,18},{... | collective-permute-start | bytes 393224 | tf_op jit(solution)/shard_map/ppermute | solution.py:15
  16.0 0.7 fusion.101
  16.7 0.7 fusion.100
  17.4 0.6 reduce_sum.9
  18.1 0.3 slice_add_fusion.1
  38.4 0.8 stack.152
  39.2 0.7 broadcast_divide_fusion
  39.9 0.2 slice_add_fusion.5
  40.0 0.1 slice_add_fusion.3
  40.4 0.2 minimum_multiply_fusion.1
  40.6 0.1 fusion.57
  40.8 0.1 fusion.92
  41.0 0.1 fusion.91
  41.1 0.3 minimum_multiply_fusion.2
  41.5 0.2 fusion.69
  41.8 0.1 slice.531
  41.9 0.1 fusion.70
  42.1 4.3 %collective-permute-start.4 = (f32[32,4,2,128]{3,0,2,1:T(8,128)S(1)}, f32[32,4,2,128]{3,0,2,1:T(8,128)S(1)}, u32[]{:S(2)}, u32[]{:S(2)}) collective-permute-start(f32[32,4,2,128]{3,0,2,1:T(8,128)S(1)} %get-tuple-element.26), channel_id=1, source_target_pairs={{0,8},{8,16},{16,24},{1,9},{9,17},{17,25},{2,10},{10,18},{18,26},{... | collective-permute-start | bytes 393224 | tf_op jit(solution)/shard_map/ppermute | solution.py:14
  46.4 1.3 %collective-permute-start.5 = (f32[32,4,2,128]{3,0,2,1:T(8,128)S(1)}, f32[32,4,2,128]{3,0,2,1:T(8,128)S(1)}, u32[]{:S(2)}, u32[]{:S(2)}) collective-permute-start(f32[32,4,2,128]{3,0,2,1:T(8,128)S(1)} %get-tuple-element.27), channel_id=1, source_target_pairs={{8,0},{16,8},{24,16},{9,1},{17,9},{25,17},{10,2},{18,10},{26,18},{... | collective-permute-start | bytes 393224 | tf_op jit(solution)/shard_map/ppermute | solution.py:15
  47.7 3.1 %collective-permute-done.5 = f32[32,4,2,128]{3,0,2,1:T(8,128)S(1)} collective-permute-done((f32[32,4,2,128]{3,0,2,1:T(8,128)S(1)}, f32[32,4,2,128]{3,0,2,1:T(8,128)S(1)}, u32[]{:S(2)}, u32[]{:S(2)}) %collective-permute-start.5) | collective-permute-done | bytes 131104 | tf_op jit(solution)/shard_map/ppermute | solution.py:15
  50.9 0.2 minimum_multiply_fusion
  51.1 0.1 fusion.50
  51.2 0.6 copy.173
  51.9 1.4 %reshape.468 = f32[8,1,8192]{2,1,0:T(1,128)} reshape(f32[128,4,4,32]{3,2,1,0:T(4,128)S(1)} %bitcast.103) | data formatting | bytes 524288
  53.2 5.8 %all-to-all-start = ((f32[8,1,8192]{2,1,0:T(1,128)}), f32[8,1,8192]{2,1,0:T(1,128)S(1)}, u32[]{:S(2)}, u32[]{:S(2)}) async-start(f32[8,1,8192]{2,1,0:T(1,128)} %reshape.468), calls=%async_computation | async-start | bytes 524288 | tf_op jit(solution)/shard_map/all_to_all | solution.py:150
  59.8 0.3 stack.153
  60.1 0.3 stack.60
  60.6 6.7 %all-to-all-done = f32[8,1,8192]{2,1,0:T(1,128)S(1)} async-done(((f32[8,1,8192]{2,1,0:T(1,128)}), f32[8,1,8192]{2,1,0:T(1,128)S(1)}, u32[]{:S(2)}, u32[]{:S(2)}) %all-to-all-start) | async-done | bytes 262176 | tf_op jit(solution)/shard_map/all_to_all | solution.py:150
  67.3 0.5 broadcast.206
  67.8 1.3 %reduce.2 = f32[8,8192]{1,0:T(8,128)S(1)} reduce(f32[8,1,8192]{2,1,0:T(1,128)S(1)} %all-to-all-done, f32[]{:T(128)} %broadcast.206), dimensions={1}, to_apply=%all_to_all.26.reduce_sub_computation | reduce | bytes 524292 | tf_op jit(solution)/shard_map/all_to_all | solution.py:150
  69.1 0.5 reshape.469
  69.6 0.3 copy.174
  70.1 2.8 %fusion.8 = f32[32,32,4,16]{1,0,3,2:T(8,128)S(1)} fusion(f32[32,32,4,16]{0,3,2,1:T(8,128)S(1)} %bitcast.114, f32[32,4,16]{0,2,1:T(8,128)S(1)} %get-tuple-element.73, f32[32,4,16]{0,2,1:T(8,128)S(1)} %get-tuple-element.72, f32[32,4,16]{0,2,1:T(8,128)S(1)} %concatenate.100, f32[32,4,16]{0,2,1:T(8,128)S(1)} %get-tuple-element.71, f32[32,4,16]{0,2,1:T(8,128)S(1)} %stack.60), kind=kOutput, calls=%fused_computation.30 | convolution fusion | flops 25493504 | bytes 565248 | tf_op jit(solution)/shard_map/ts...,ns...->nt.../dot_general | solution.py:82
  72.9 0.9 copy.177
  73.8 0.3 copy.181
  74.1 1.5 %gather_fusion.1 = f32[256,2048]{1,0:T(8,128)S(1)} fusion(f32[32,2048]{1,0:T(8,128)S(1)} %copy.181, s32[1024]{0:T(1024)S(1)} %pad_clamp_fusion), kind=kCustom, calls=%fused_computation.1.clone | custom fusion | bytes 4195328 | tf_op jit(solution)/shard_map/jit(_take)/gather | solution.py:115
  75.6 2.7 %gather_fusion = f32[256,2048]{1,0:T(8,128)} fusion(f32[32,2048]{1,0:T(8,128)S(1)} %copy.181, s32[1024]{0:T(1024)S(1)} %pad_clamp_fusion.1), kind=kCustom, calls=%fused_computation.clone | custom fusion | bytes 4195328 | tf_op jit(solution)/shard_map/jit(_take)/gather | solution.py:114
  78.3 3.6 %fusion.1 = f32[32,2048]{1,0:T(8,128)S(1)} fusion(f32[32,2048]{1,0:T(8,128)S(1)} %copy.181, f32[256,2048]{1,0:T(8,128)S(1)} %gather_fusion.1, f32[256,2048]{1,0:T(8,128)} %gather_fusion, f32[2048]{0:T(1024)S(1)} %sub.106, f32[256]{0:T(256)S(1)} %neg.4, f32[256]{0:T(256)S(1)} %copy-done.9, pred[256]{0:T(512)(128)(4,1)S(1)} %get-tuple-element.108, ...), kind=kOutput, calls=%fused_computation.13 | convolution fusion | flops 204611584 | bytes 4764160 | tf_op jit(solution)/shard_map/dot_general | solution.py:117
  81.9 2.7 %gather_fusion.3 = f32[256,2048]{1,0:T(8,128)} fusion(f32[32,2048]{1,0:T(8,128)S(1)} %fusion.1, s32[1024]{0:T(1024)S(1)} %pad_clamp_fusion), kind=kCustom, calls=%fused_computation.3.clone | custom fusion | bytes 4195328 | tf_op jit(solution)/shard_map/jit(_take)/gather | solution.py:115
  84.6 2.7 %gather_fusion.2 = f32[256,2048]{1,0:T(8,128)} fusion(f32[32,2048]{1,0:T(8,128)S(1)} %fusion.1, s32[1024]{0:T(1024)S(1)} %pad_clamp_fusion.1), kind=kCustom, calls=%fused_computation.2.clone | custom fusion | bytes 4195328 | tf_op jit(solution)/shard_map/jit(_take)/gather | solution.py:114
  87.2 4.4 %fusion.3 = f32[32,2048]{1,0:T(8,128)S(1)} fusion(f32[32,2048]{1,0:T(8,128)S(1)} %fusion.1, f32[256,2048]{1,0:T(8,128)} %gather_fusion.3, f32[256,2048]{1,0:T(8,128)} %gather_fusion.2, f32[2048]{0:T(1024)S(1)} %sub.106, f32[256]{0:T(256)S(1)} %neg.4, f32[256]{0:T(256)S(1)} %copy-done.9, pred[256]{0:T(512)(128)(4,1)S(1)} %get-tuple-element.108, ...), kind=kOutput, calls=%fused_computation.15 | convolution fusion | flops 204611584 | bytes 4764160 | tf_op jit(solution)/shard_map/dot_general | solution.py:117
  91.6 1.5 %gather_fusion.5 = f32[256,2048]{1,0:T(8,128)S(1)} fusion(f32[32,2048]{1,0:T(8,128)S(1)} %fusion.3, s32[1024]{0:T(1024)S(1)} %pad_clamp_fusion), kind=kCustom, calls=%fused_computation.5.clone | custom fusion | bytes 4195328 | tf_op jit(solution)/shard_map/jit(_take)/gather | solution.py:115
  93.1 2.7 %gather_fusion.4 = f32[256,2048]{1,0:T(8,128)} fusion(f32[32,2048]{1,0:T(8,128)S(1)} %fusion.3, s32[1024]{0:T(1024)S(1)} %pad_clamp_fusion.1), kind=kCustom, calls=%fused_computation.4.clone | custom fusion | bytes 4195328 | tf_op jit(solution)/shard_map/jit(_take)/gather | solution.py:114
  95.8 3.6 %fusion.5 = f32[32,2048]{1,0:T(8,128)S(1)} fusion(f32[32,2048]{1,0:T(8,128)S(1)} %fusion.3, f32[256,2048]{1,0:T(8,128)S(1)} %gather_fusion.5, f32[256,2048]{1,0:T(8,128)} %gather_fusion.4, f32[2048]{0:T(1024)S(1)} %sub.106, f32[256]{0:T(256)S(1)} %neg.4, f32[256]{0:T(256)S(1)} %copy-done.9, pred[256]{0:T(512)(128)(4,1)S(1)} %get-tuple-element.108, ...), kind=kOutput, calls=%fused_computation.17 | convolution fusion | flops 204611584 | bytes 4764160 | tf_op jit(solution)/shard_map/dot_general | solution.py:117
  99.4 1.5 %gather_fusion.7 = f32[256,2048]{1,0:T(8,128)S(1)} fusion(f32[32,2048]{1,0:T(8,128)S(1)} %fusion.5, s32[1024]{0:T(1024)S(1)} %pad_clamp_fusion), kind=kCustom, calls=%fused_computation.7.clone | custom fusion | bytes 4195328 | tf_op jit(solution)/shard_map/jit(_take)/gather | solution.py:115
  100.9 2.7 %gather_fusion.6 = f32[256,2048]{1,0:T(8,128)} fusion(f32[32,2048]{1,0:T(8,128)S(1)} %fusion.5, s32[1024]{0:T(1024)S(1)} %pad_clamp_fusion.1), kind=kCustom, calls=%fused_computation.6.clone | custom fusion | bytes 4195328 | tf_op jit(solution)/shard_map/jit(_take)/gather | solution.py:114
  103.6 3.6 %fusion.7 = f32[32,2048]{1,0:T(8,128)S(1)} fusion(f32[32,2048]{1,0:T(8,128)S(1)} %fusion.5, f32[256,2048]{1,0:T(8,128)S(1)} %gather_fusion.7, f32[256,2048]{1,0:T(8,128)} %gather_fusion.6, f32[2048]{0:T(1024)S(1)} %sub.106, f32[256]{0:T(256)S(1)} %neg.4, f32[256]{0:T(256)S(1)} %copy-done.9, pred[256]{0:T(512)(128)(4,1)S(1)} %get-tuple-element.108, ...), kind=kOutput, calls=%fused_computation.19 | convolution fusion | flops 204611584 | bytes 4764160 | tf_op jit(solution)/shard_map/dot_general | solution.py:117
  107.2 0.3 copy.183
  107.5 0.5 reshape.470
  108.0 14.4 %all_to_all.36 = f32[8,1,8192]{2,1,0:T(1,128)S(1)} all-to-all(f32[8,1,8192]{2,1,0:T(1,128)S(1)} %reshape.470), channel_id=1, replica_groups=mesh['lat'=4,'lev'=8] {'lev'}, dimensions={0} | all-to-all | bytes 524288 | tf_op jit(solution)/shard_map/all_to_all | solution.py:123
  122.3 1.3 %reduce.3 = f32[8,8192]{1,0:T(8,128)S(1)} reduce(f32[8,1,8192]{2,1,0:T(1,128)S(1)} %all_to_all.36, f32[]{:T(128)} %broadcast.206), dimensions={1}, to_apply=%all_to_all.30.reduce_sub_computation | reduce | bytes 524292 | tf_op jit(solution)/shard_map/all_to_all | solution.py:123
  123.6 0.3 reshape.471
  124.1 1.0 copy.185
  (69 shorter events, 2.3 us)
Async XLA Ops:
  1.6 38.7 %collective-permute-start = (f32[4,1,128]{2,1,0:T(1,128)S(1)}, f32[4,1,128]{2,1,0:T(1,128)S(1)}, u32[]{:S(2)}, u32[]{:S(2)}) collective-permute-start(f32[4,1,128]{2,1,0:T(1,128)S(1)} %get-tuple-element.63), channel_id=1, source_target_pairs={{0,8},{8,16},{16,24},{1,9},{9,17},{17,25},{2,10},{10,18},{18,26},{... | collective-permute-start | bytes 6152 | tf_op jit(solution)/shard_map/ppermute | solution.py:14
  3.9 4.3 %copy-start.1 = (f32[32,4,4,128]{3,2,1,0:T(4,128)S(1)}, f32[32,4,4,128]{3,2,1,0:T(4,128)}, u32[]{:S(2)}) copy-start(f32[32,4,4,128]{3,2,1,0:T(4,128)} %param.12) | copy-start | bytes 786436
  4.0 36.3 %collective-permute-start.1 = (f32[4,1,128]{2,1,0:T(1,128)S(1)}, f32[4,1,128]{2,1,0:T(1,128)S(1)}, u32[]{:S(2)}, u32[]{:S(2)}) collective-permute-start(f32[4,1,128]{2,1,0:T(1,128)S(1)} %get-tuple-element.64), channel_id=1, source_target_pairs={{8,0},{16,8},{24,16},{9,1},{17,9},{25,17},{10,2},{18,10},{26,18},{... | collective-permute-start | bytes 6152 | tf_op jit(solution)/shard_map/ppermute | solution.py:15
  7.9 0.9 copy-start.3
  8.8 7.1 %copy-start.2 = (f32[32]{0:T(128)S(1)}, f32[32]{0:T(128)}, u32[]{:S(2)}) copy-start(f32[32]{0:T(128)} %param.15) | copy-start | bytes 388
  8.8 9.2 %copy-start.6 = (s32[2,256]{1,0:T(2,128)S(1)}, s32[2,256]{1,0:T(2,128)}, u32[]{:S(2)}) copy-start(s32[2,256]{1,0:T(2,128)} %param.21) | copy-start | bytes 6148
  8.8 9.2 %copy-start.5 = (s32[4,4,16]{2,1,0:T(4,128)S(1)}, s32[4,4,16]{2,1,0:T(4,128)}, u32[]{:S(2)}) copy-start(s32[4,4,16]{2,1,0:T(4,128)} %param.17) | copy-start | bytes 3076
  8.9 9.2 %copy-start.4 = (f32[32,4,16]{0,2,1:T(8,128)S(1)}, f32[32,4,16]{0,2,1:T(8,128)}, u32[]{:S(2)}) copy-start(f32[32,4,16]{0,2,1:T(8,128)} %param.16) | copy-start | bytes 24580
  8.9 9.3 %copy-start = (f32[32,4,16]{0,2,1:T(8,128)S(1)}, f32[32,4,16]{0,2,1:T(8,128)}, u32[]{:S(2)}) copy-start(f32[32,4,16]{0,2,1:T(8,128)} %param.14) | copy-start | bytes 24580
  9.5 30.9 %collective-permute-start.2 = (f32[32,4,2,128]{3,0,2,1:T(8,128)S(1)}, f32[32,4,2,128]{3,0,2,1:T(8,128)S(1)}, u32[]{:S(2)}, u32[]{:S(2)}) collective-permute-start(f32[32,4,2,128]{3,0,2,1:T(8,128)S(1)} %get-tuple-element.32), channel_id=1, source_target_pairs={{0,8},{8,16},{16,24},{1,9},{9,17},{17,25},{2,10},{10,18},{18,26},{... | collective-permute-start | bytes 393224 | tf_op jit(solution)/shard_map/ppermute | solution.py:14
  14.7 25.8 %collective-permute-start.3 = (f32[32,4,2,128]{3,0,2,1:T(8,128)S(1)}, f32[32,4,2,128]{3,0,2,1:T(8,128)S(1)}, u32[]{:S(2)}, u32[]{:S(2)}) collective-permute-start(f32[32,4,2,128]{3,0,2,1:T(8,128)S(1)} %get-tuple-element.33), channel_id=1, source_target_pairs={{8,0},{16,8},{24,16},{9,1},{17,9},{25,17},{10,2},{18,10},{26,18},{... | collective-permute-start | bytes 393224 | tf_op jit(solution)/shard_map/ppermute | solution.py:15
  42.1 5.6 %collective-permute-start.4 = (f32[32,4,2,128]{3,0,2,1:T(8,128)S(1)}, f32[32,4,2,128]{3,0,2,1:T(8,128)S(1)}, u32[]{:S(2)}, u32[]{:S(2)}) collective-permute-start(f32[32,4,2,128]{3,0,2,1:T(8,128)S(1)} %get-tuple-element.26), channel_id=1, source_target_pairs={{0,8},{8,16},{16,24},{1,9},{9,17},{17,25},{2,10},{10,18},{18,26},{... | collective-permute-start | bytes 393224 | tf_op jit(solution)/shard_map/ppermute | solution.py:14
  46.4 4.5 %collective-permute-start.5 = (f32[32,4,2,128]{3,0,2,1:T(8,128)S(1)}, f32[32,4,2,128]{3,0,2,1:T(8,128)S(1)}, u32[]{:S(2)}, u32[]{:S(2)}) collective-permute-start(f32[32,4,2,128]{3,0,2,1:T(8,128)S(1)} %get-tuple-element.27), channel_id=1, source_target_pairs={{8,0},{16,8},{24,16},{9,1},{17,9},{25,17},{10,2},{18,10},{26,18},{... | collective-permute-start | bytes 393224 | tf_op jit(solution)/shard_map/ppermute | solution.py:15
  51.2 7.9 %copy-start.7 = (f32[256]{0:T(256)S(1)}, f32[256]{0:T(256)}, u32[]{:S(2)}) copy-start(f32[256]{0:T(256)} %param.19) | copy-start | bytes 3076
  53.2 14.1 %all-to-all-start = ((f32[8,1,8192]{2,1,0:T(1,128)}), f32[8,1,8192]{2,1,0:T(1,128)S(1)}, u32[]{:S(2)}, u32[]{:S(2)}) async-start(f32[8,1,8192]{2,1,0:T(1,128)} %reshape.468), calls=%async_computation | async-start | bytes 524288 | tf_op jit(solution)/shard_map/all_to_all | solution.py:150
  75.5 2.7 %copy-start.8 = (s32[256,32]{0,1:T(8,128)S(1)}, s32[256,32]{0,1:T(8,128)}, u32[]{:S(2)}) copy-start(s32[256,32]{0,1:T(8,128)} %param.20) | copy-start | bytes 98308
  75.6 2.7 %copy-start.9 = (f32[256]{0:T(256)S(1)}, f32[256]{0:T(256)}, u32[]{:S(2)}) copy-start(f32[256]{0:T(256)} %param.18) | copy-start | bytes 3076

commit v2 on v1

v2 whole, which is shorter than its diff:
```python
import functools

import jax
import jax.numpy as jnp
from jax import lax
from jax.experimental import pallas as pl
from jax.experimental.pallas import tpu as pltpu
from jax.sharding import PartitionSpec as P

LANES = 128
OCTET = 8
SWEEPS = 2
VMEM = pl.BlockSpec(memory_space=pltpu.VMEM)


def limited_slope(left, right):
    return jnp.maximum(jnp.minimum(left, right), 0.0) + jnp.minimum(jnp.maximum(left, right), 0.0)


def upwind_weights(courant):
    ahead = jnp.maximum(courant, 0.0)
    behind = jnp.minimum(courant, 0.0)
    return ahead, 0.5 * ahead * (1.0 - courant), behind, -0.5 * behind * (1.0 + courant)


def block_transpose(tiles, width):
    tiles = list(tiles)
    lane_block = lax.broadcasted_iota(jnp.int32, tiles[0].shape, 1) // width
    step = 1
    while step < len(tiles):
        upper = (lane_block // step) % 2 == 1
        for low in range(len(tiles)):
            if low & step:
                continue
            first, second = tiles[low], tiles[low + step]
            tiles[low] = jnp.where(upper, pltpu.roll(second, step * width, 1), first)
            tiles[low + step] = jnp.where(
                upper, second, pltpu.roll(first, LANES - step * width, 1)
            )
        step *= 2
    return tiles


def lon_step(f, weights):
    ahead, ahead_slope, behind, behind_slope = weights
    size = f.shape[1]
    left = f - pltpu.roll(f, 1, 1)
    slope = limited_slope(left, pltpu.roll(left, size - 1, 1))
    east = ahead * f + ahead_slope * slope
    west = behind * f + behind_slope * slope
    return f - ((east - pltpu.roll(east, 1, 1)) + (pltpu.roll(west, size - 1, 1) - west))


def lat_step(f, first_row, weights_at):
    jumps = [f[i + 1] - f[i] for i in range(len(f) - 1)]
    slopes = [None] + [limited_slope(jumps[i - 1], jumps[i]) for i in range(1, len(f) - 1)]
    fluxes = []
    for i in range(2, len(f) - 1):
        ahead, ahead_slope, behind, behind_slope = weights_at(first_row + i)
        fluxes.append(
            (ahead * f[i - 1] + ahead_slope * slopes[i - 1])
            + (behind * f[i] + behind_slope * slopes[i])
        )
    return [f[i] - (fluxes[i - 1] - fluxes[i - 2]) for i in range(2, len(f) - 2)]


def advect_kernel(
    sizes, own_ref, core_ref, chip_ref, own_wind, core_wind, chip_wind, out_ref, wind, zonal, merid
):
    species, levels, rows, parts, width = sizes
    halo = 2 * SWEEPS
    band = lax.axis_index("lat")
    even = band % 2 == 0
    plane = levels * rows

    per_band = 2 * plane * parts
    wind[0:per_band] = jnp.where(even, chip_wind[...], core_wind[...])
    wind[per_band : 2 * per_band] = own_wind[...]
    wind[2 * per_band : 3 * per_band] = jnp.where(even, core_wind[...], chip_wind[...])

    for source in range(3):
        flow = jnp.concatenate(
            [wind[pl.ds(source * per_band + k, plane, parts), :] for k in range(parts)], axis=1
        )
        size = flow.shape[1]
        west_face = 0.5 * (pltpu.roll(flow, 1, 1) + flow)
        east_face = pltpu.roll(west_face, size - 1, 1)
        there = slice(source * plane, (source + 1) * plane)
        zonal[0, there], zonal[1, there] = upwind_weights(east_face)[:2]
        zonal[2, there], zonal[3, there] = upwind_weights(west_face)[2:]

    def flow_row(row):
        source, inside = divmod(row + rows, rows)
        start = source * per_band + (plane + inside) * parts
        return jnp.concatenate(
            [wind[pl.ds(start + k, levels, rows * parts), :] for k in range(parts)], axis=1
        )

    total = rows * lax.axis_size("lat")
    low_face = 2 - halo
    for face in range(low_face, rows + halo - 1):
        place = band * rows + face
        open_face = jnp.logical_and(place >= 1, place <= total - 1).astype(jnp.float32)
        courant = 0.5 * (flow_row(face - 1) + flow_row(face)) * open_face
        for which, weight in enumerate(upwind_weights(courant)):
            merid[which, face - low_face] = weight

    def octet_rows(ref, octet, level, row):
        start = (octet * OCTET * plane + level * rows + row) * parts
        return jnp.concatenate(
            [ref[pl.ds(start + k, OCTET, plane * parts), :] for k in range(parts)], axis=1
        )

    def step(index, carry):
        pair, octet = index // (species // OCTET), index % (species // OCTET)
        done = []
        for parity in range(2):
            level = pair * 2 + parity

            def zonal_at(row):
                source, inside = divmod(row + rows, rows)
                at = source * plane + level * rows + inside
                return [zonal[which, pl.ds(at, 1), :] for which in range(4)]

            def merid_at(face):
                return [merid[which, face - low_face, pl.ds(level, 1), :] for which in range(4)]

            before, after = [], []
            for row in range(rows):
                by_core = octet_rows(core_ref, octet, level, row)
                by_chip = octet_rows(chip_ref, octet, level, row)
                before.append(jnp.where(even, by_chip, by_core))
                after.append(jnp.where(even, by_core, by_chip))
            here = [octet_rows(own_ref, octet, level, row) for row in range(rows)]
            f = before[rows - halo :] + here + after[:halo]
            first_row = -halo
            for sweep in range(SWEEPS):
                f = [lon_step(item, zonal_at(first_row + i)) for i, item in enumerate(f)]
                f = lat_step(f, first_row, merid_at)
                first_row += 2
            done += f
        start = pl.multiple_of(pair * species + octet * OCTET, OCTET)
        per_part = LANES // width
        for k in range(parts):
            cut = [item[:, k * LANES : (k + 1) * LANES] for item in done]
            for j, tile in enumerate(block_transpose(cut, width)):
                out_ref[k * per_part + j, pl.ds(start, OCTET), :] = tile
        return carry

    lax.fori_loop(0, (levels // 2) * (species // OCTET), step, 0)


def spread_kernel(sizes, in_ref, out_ref):
    species, levels, rows, parts, width = sizes
    plane = levels * rows
    per_part = LANES // width
    for pair in range(levels // 2):
        for octet in range(species // OCTET):
            for k in range(parts):
                start = pair * species + octet * OCTET
                cut = [in_ref[k * per_part + j, start : start + OCTET, :] for j in range(per_part)]
                for g, tile in enumerate(block_transpose(cut, width)):
                    at = (octet * OCTET * plane + pair * 2 * rows + g) * parts + k
                    out_ref[pl.ds(at, OCTET, plane * parts), :] = tile


def column_kernel(
    sizes,
    moved_ref,
    depth_ref,
    share_ref,
    kelvin_ref,
    active_ref,
    factor_ref,
    barrier_ref,
    pick_ref,
    yield_ref,
    out_ref,
    lower_ref,
    overlap_ref,
    rate_ref,
):
    pairs, species, tile_pairs = sizes
    half = LANES // 2
    levels = 2 * pairs
    reactions = factor_ref.shape[0]
    odd = lax.broadcasted_iota(jnp.int32, (1, LANES), 1) >= half

    depth = depth_ref[...]
    other = pltpu.roll(depth, half, 1)
    both = depth + other
    edge = jnp.zeros((1, LANES), jnp.float32)
    for s in range(pairs):
        lower_ref[s : s + 1] = edge
        edge = edge + both[s : s + 1]
    total = edge
    lower = lower_ref[...] + jnp.where(odd, other, 0.0)
    upper = lower + depth

    share_sum = share_ref[0:1]
    for t in range(1, levels):
        share_sum = share_sum + share_ref[t : t + 1]
    below = jnp.zeros((1, LANES), jnp.float32)
    target_low = below
    for t in range(levels):
        share = share_ref[t : t + 1]
        below = below + share
        target_top = below / share_sum * total
        shared = jnp.maximum(
            jnp.minimum(upper, target_top) - jnp.maximum(lower, target_low), 0.0
        )
        overlap_ref[t] = shared / (share / share_sum * total)
        target_low = target_top

    def tile_step(tile, carry):
        held = []
        for inside in range(tile_pairs):
            t = tile * tile_pairs + inside
            sums = []
            for parity in range(2):
                acc = None
                for s in range(pairs):
                    term = overlap_ref[2 * t + parity, s : s + 1, :] * moved_ref[s]
                    acc = term if acc is None else acc + term
                sums.append(acc)
            kept = jnp.where(odd, sums[1], sums[0])
            crossed = jnp.where(odd, sums[0], sums[1])
            held.append(kept + pltpu.roll(crossed, half, 1))

        for inside in range(tile_pairs):
            t = tile * tile_pairs + inside
            warmth = 300.0 / kelvin_ref[pl.ds(t, 1), :] - 1.0
            rate_ref[:, inside * LANES : (inside + 1) * LANES] = factor_ref[...] * jnp.exp(
                -barrier_ref[...] * warmth
            )
        q = jnp.concatenate(held, axis=1)
        for substep in range(active_ref.shape[0]):
            on = jnp.concatenate([active_ref[substep : substep + 1, :]] * tile_pairs, axis=1)
            high = q.astype(jnp.bfloat16)
            low = (q - high.astype(jnp.float32)).astype(jnp.bfloat16)
            picked = jnp.dot(
                pick_ref[...],
                jnp.concatenate([high, low], axis=0),
                preferred_element_type=jnp.float32,
            )
            rates = rate_ref[...] * picked[:reactions] * picked[reactions:]
            high = rates.astype(jnp.bfloat16)
            low = (rates - high.astype(jnp.float32)).astype(jnp.bfloat16)
            change = jnp.dot(
                yield_ref[...],
                jnp.concatenate([high, low], axis=0),
                preferred_element_type=jnp.float32,
            )
            q = jnp.where(on > 0, q + change, q)
        for inside in range(tile_pairs):
            out_ref[tile * tile_pairs + inside] = q[:, inside * LANES : (inside + 1) * LANES]
        return carry

    lax.fori_loop(0, pairs // tile_pairs, tile_step, 0)


def swap_pairs(count, first):
    route = []
    for low in range(first, count - 1, 2):
        route += [(low, low + 1), (low + 1, low)]
    return route


def body(
    species_fractions,
    cell_flow_ratios,
    layer_pressure_depth,
    layer_thickness_fraction,
    cell_kelvin_field,
    daytime_indicator,
    kinetic_factor_times_step,
    arrhenius_barrier,
    species_yield_matrix,
    reagent_pairs,
):
    species, levels, rows, lons = species_fractions.shape
    all_levels = layer_pressure_depth.shape[0]
    width = layer_pressure_depth.shape[2]
    blocks = lax.axis_size("lev")
    bands = lax.axis_size("lat")
    parts = lons // LANES
    substeps = daytime_indicator.shape[0]
    reactions = kinetic_factor_times_step.shape[0]
    assert 2 * rows * width == LANES and levels % 2 == 0 and rows == 2 * SWEEPS
    sizes = (species, levels, rows, parts, width)

    by_core, by_chip = swap_pairs(bands, 0), swap_pairs(bands, 1)
    core_wind = lax.ppermute(cell_flow_ratios, "lat", by_core)
    chip_wind = lax.ppermute(cell_flow_ratios, "lat", by_chip)
    core_band = lax.ppermute(species_fractions, "lat", by_core)
    chip_band = lax.ppermute(species_fractions, "lat", by_chip)

    def flat(value):
        return value.reshape(-1, LANES)

    packed = pl.pallas_call(
        functools.partial(advect_kernel, sizes),
        out_shape=jax.ShapeDtypeStruct((blocks, levels // 2 * species, LANES), jnp.float32),
        in_specs=[VMEM] * 6,
        out_specs=VMEM,
        scratch_shapes=[
            pltpu.VMEM((3 * 2 * levels * rows * parts, LANES), jnp.float32),
            pltpu.VMEM((4, 3 * levels * rows, lons), jnp.float32),
            pltpu.VMEM((4, 3 * rows - 3, levels, lons), jnp.float32),
        ],
        name="advect",
    )(
        flat(species_fractions),
        flat(core_band),
        flat(chip_band),
        flat(cell_flow_ratios),
        flat(core_wind),
        flat(chip_wind),
    )
    moved = lax.all_to_all(packed, "lev", split_axis=0, concat_axis=0, tiled=True)

    pairs = all_levels // 2
    first_pick = reagent_pairs.reshape(-1)[:, None] == (
        lax.broadcasted_iota(jnp.int32, (2 * reactions, 2 * species), 1) % species
    )
    yields = species_yield_matrix.T.astype(jnp.bfloat16)
    active = daytime_indicator.reshape(substeps, -1)
    tile_pairs = 4
    reacted = pl.pallas_call(
        functools.partial(column_kernel, (pairs, species, tile_pairs)),
        out_shape=jax.ShapeDtypeStruct((pairs, species, LANES), jnp.float32),
        in_specs=[VMEM] * 9,
        out_specs=VMEM,
        scratch_shapes=[
            pltpu.VMEM((pairs, LANES), jnp.float32),
            pltpu.VMEM((all_levels, pairs, LANES), jnp.float32),
            pltpu.VMEM((reactions, tile_pairs * LANES), jnp.float32),
        ],
        compiler_params=pltpu.CompilerParams(vmem_limit_bytes=32 * 2**20),
        name="columns",
    )(
        moved.reshape(pairs, species, LANES),
        layer_pressure_depth.reshape(pairs, LANES),
        jnp.broadcast_to(layer_thickness_fraction[:, None], (all_levels, LANES)),
        cell_kelvin_field.reshape(pairs, LANES),
        jnp.concatenate([active, active], axis=1),
        jnp.broadcast_to(kinetic_factor_times_step[:, None], (reactions, LANES)),
        jnp.broadcast_to(arrhenius_barrier[:, None], (reactions, LANES)),
        first_pick.astype(jnp.bfloat16),
        jnp.concatenate([yields, yields], axis=1),
    )
    returned = lax.all_to_all(
        reacted.reshape(packed.shape), "lev", split_axis=0, concat_axis=0, tiled=True
    )
    out = pl.pallas_call(
        functools.partial(spread_kernel, sizes),
        out_shape=jax.ShapeDtypeStruct((species * levels * rows * parts, LANES), jnp.float32),
        in_specs=[VMEM],
        out_specs=VMEM,
        name="spread",
    )(returned)
    return out.reshape(species_fractions.shape)


def solution(mesh):
    placed = (
        P(None, "lev", "lat", None),
        P(None, "lev", "lat", None),
        P(None, "lat", "lev"),
        P(),
        P(None, "lat", "lev"),
        P(None, "lat", "lev"),
        P(),
        P(),
        P(),
        P(),
    )
    return jax.shard_map(
        body, mesh=mesh, in_specs=placed, out_specs=P(None, "lev", "lat", None), check_vma=False
    )
```

time: 126 us -> 55.3 us (0.44)
  local copies, waits for them, and re-layouts: 32.7 us -> 4.52 us
  between operations: 20.6 us -> 0.16 us
  matrix products: 18 us -> 0 us
  Pallas kernels: 0 us -> 17.9 us
  starting transfers between devices: 21.6 us -> 11.6 us
  other arithmetic: 7.94 us -> 0.98 us
  waiting for transfers between devices: 9.85 us -> 5.63 us
    dot_general x5 -> x0, matrix products: 18 us -> none  [the longest x4 15.2 us: react_block(): jnp.dot(yield_matrix_floating.T, rates, precision=lax.Precision.HIGHEST)]
    pallas_call x0 -> x3, Pallas kernels: none -> 17.9 us  [the longest x1 8 us: body(): pl.pallas_call(functools.partial(column_kernel, (pairs, species, tile_pai...]
    gather x8 -> x0, local copies, waits for them, and re-layouts: 17.8 us -> none  [the longest x4 10.7 us: react_block(): jnp.take(flattened, first_axis_position, axis=0)]
    ppermute x6 -> x4, starting transfers between devices: 15.8 us -> 5.7 us  [the longest x1 3.93 us: body(): core_wind = lax.ppermute(cell_flow_ratios, 'lat', by_core)]
    slice x16 -> x0, local copies, waits for them, and re-layouts: 4.78 us -> none  [the longest x4 2.73 us: lon_update(): before = jnp.roll(tracer, 1, axis=-1)]
    ppermute x6 -> x4, waiting for transfers between devices: 3.15 us -> 0.01 us  [the longest x1 0.01 us: body(): chip_wind = lax.ppermute(cell_flow_ratios, 'lat', by_chip)]
    all_to_all x2 -> x0, other arithmetic: 2.52 us -> none  [the longest x1 1.26 us: back_to_levels(): lax.all_to_all(vertical_profiles, 'lev', split_axis=1, concat_axis=3, til...]
    all_to_all x5 -> x0, local copies, waits for them, and re-layouts: 2.11 us -> none  [the longest x2 1.15 us: back_to_levels(): lax.all_to_all(vertical_profiles, 'lev', split_axis=1, concat_axis=3, til...]
  transfers between devices with their start and end apart: 7 -> 5, of which waited for: 2 -> 1; matrix products, arithmetic and copies ran while one was open for 8% -> 3% of each run, Pallas kernels for 0% -> 0%
where the time goes in v2:
time: 55.3 us; the launch traced here: 54.7 us
  Pallas kernels  17.9 us (32%)
  blocking collectives  13.9 us (25%)
  starting transfers between devices  11.6 us (21%)
  waiting for transfers between devices  5.63 us (10%)
  local copies, waits for them, and re-layouts  4.52 us (8%)
  other arithmetic  0.98 us (2%)
    all_to_all x1, blocking collectives, body(): lax.all_to_all(reacted.reshape(packed.shape), 'lev', split_axis=0, concat...  13.9 us
    pallas_call x1, Pallas kernels, body(): pl.pallas_call(functools.partial(column_kernel, (pairs, species, tile_pai...  8 us
    pallas_call x1, Pallas kernels, body(): pl.pallas_call(functools.partial(advect_kernel, sizes), out_shape=jax.Sha...  7.85 us
    all_to_all x1, starting transfers between devices, body(): lax.all_to_all(packed, 'lev', split_axis=0, concat_axis=0, tiled=True)  5.94 us
    all_to_all x1, waiting for transfers between devices, body(): lax.all_to_all(packed, 'lev', split_axis=0, concat_axis=0, tiled=True)  5.62 us
    unnamed x25, local copies, waits for them, and re-layouts  3.99 us
    ppermute x1, starting transfers between devices, body(): core_wind = lax.ppermute(cell_flow_ratios, 'lat', by_core)  3.93 us
    pallas_call x1, Pallas kernels, body(): pl.pallas_call(functools.partial(spread_kernel, sizes), out_shape=jax.Sha...  2.02 us
  transfers between devices with their start and end apart: 5, of which 1 were waited for; matrix products, arithmetic and copies ran while one was open for 3% of the time, Pallas kernels for 0%

profile of v2, /device:TPU:0, one launch (start us, length us, event | category | flops | bytes accessed | tf_op | source)
XLA Modules:
  0.0 54.7 jit_solution(4349039590639911872)
XLA Ops:
  0.0 0.5 collective-permute-start
  0.5 0.7 %collective-permute-start.1 = (f32[32,4,4,128]{3,2,1,0:T(4,128)}, f32[32,4,4,128]{3,2,1,0:T(4,128)S(1)}, u32[]{:S(2)}, u32[]{:S(2)}) collective-permute-start(f32[32,4,4,128]{3,2,1,0:T(4,128)} %param.10), channel_id=1, source_target_pairs={{8,16},{16,8},{9,17},{17,9},{10,18},{18,10},{11,19},{19,11},{12,20... | collective-permute-start | bytes 786440 | tf_op jit(solution)/shard_map/ppermute | solution.py:296
  1.1 3.9 %collective-permute-start.2 = (f32[2,4,4,128]{3,2,1,0:T(4,128)}, f32[2,4,4,128]{3,2,1,0:T(4,128)S(1)}, u32[]{:S(2)}, u32[]{:S(2)}) collective-permute-start(f32[2,4,4,128]{3,2,1,0:T(4,128)} %param.11), channel_id=1, source_target_pairs={{0,8},{8,0},{16,24},{24,16},{1,9},{9,1},{17,25},{25,17},{2,10},{10... | collective-permute-start | bytes 49160 | tf_op jit(solution)/shard_map/ppermute | solution.py:293
  5.1 0.7 %collective-permute-start.3 = (f32[2,4,4,128]{3,2,1,0:T(4,128)}, f32[2,4,4,128]{3,2,1,0:T(4,128)S(1)}, u32[]{:S(2)}, u32[]{:S(2)}) collective-permute-start(f32[2,4,4,128]{3,2,1,0:T(4,128)} %param.11), channel_id=1, source_target_pairs={{8,16},{16,8},{9,17},{17,9},{10,18},{18,10},{11,19},{19,11},{12,20... | collective-permute-start | bytes 49160 | tf_op jit(solution)/shard_map/ppermute | solution.py:294
  5.7 0.8 %convert_bitcast_fusion = bf16[32,256]{1,0:T(8,128)(2,1)S(1)} fusion(s32[256,32]{0,1:T(8,128)} %param.18), kind=kLoop, calls=%fused_computation.3 | loop fusion | flops 8192 | bytes 49152 | tf_op jit(solution)/shard_map/convert_element_type | solution.py:326
  6.5 0.0 collective-permute-done.2
  6.5 0.0 copy-start.4
  6.5 0.0 collective-permute-done.3
  6.5 0.0 copy-start.5
  6.5 0.0 collective-permute-done
  6.5 0.0 copy-start
  6.5 0.0 collective-permute-done.1
  6.6 0.0 copy-start.1
  6.6 0.5 copy-done.4
  7.1 0.0 copy-done.5
  7.1 0.1 copy-done
  7.2 0.1 copy-done.1
  7.3 7.9 %advect.1 = f32[8,64,128]{2,1,0:T(8,128)} custom-call(f32[512,128]{1,0:T(8,128)} %bitcast.15, f32[512,128]{1,0:T(8,128)} %bitcast.16, f32[512,128]{1,0:T(8,128)} %bitcast.17, f32[32,128]{1,0:T(8,128)} %bitcast.18, f32[32,128]{1,0:T(8,128)} %bitcast.19, f32[32,128]{1,0:T(8,128)} %bitcast.20), custom_call_target="tpu_custom_call" | custom-call | tf_op jit(solution)/shard_map/advect/pallas_call | solution.py:301
  15.2 0.0 copy-start.2
  15.2 5.9 %all-to-all-start = ((f32[8,64,128]{2,1,0:T(8,128)}), f32[8,64,128]{2,1,0:T(8,128)S(1)}, u32[]{:S(2)}, u32[]{:S(2)}) async-start(f32[8,64,128]{2,1,0:T(8,128)} %advect.1), calls=%async_computation | async-start | bytes 524288 | tf_op jit(solution)/shard_map/all_to_all | solution.py:320
  21.1 0.0 copy-start.7
  21.1 0.7 %copy-done.7 = s32[2,256]{1,0:T(2,128)S(1)} copy-done((s32[2,256]{1,0:T(2,128)S(1)}, s32[2,256]{1,0:T(2,128)}, u32[]{:S(2)}) %copy-start.7) | copy-done | bytes 2072
  21.8 0.0 copy-done.2
  21.8 0.1 copy.13
  21.9 0.0 copy-start.3
  21.9 0.1 reshape.47.depth_ref
  22.0 0.7 %copy-done.3 = f32[32,4,16]{0,2,1:T(8,128)S(1)} copy-done((f32[32,4,16]{0,2,1:T(8,128)S(1)}, f32[32,4,16]{0,2,1:T(8,128)}, u32[]{:S(2)}) %copy-start.3) | copy-done | bytes 8216
  22.6 0.1 copy.14
  22.7 0.0 copy-start.6
  22.7 0.1 reshape.48.kelvin_ref
  22.8 0.6 %copy-done.6 = s32[4,4,16]{2,1,0:T(4,128)S(1)} copy-done((s32[4,4,16]{2,1,0:T(4,128)S(1)}, s32[4,4,16]{2,1,0:T(4,128)}, u32[]{:S(2)}) %copy-start.6) | copy-done | bytes 1048
  23.4 0.1 reshape.49
  23.5 0.1 pad_add_fusion.active_ref
  23.6 0.1 fusion.pick_ref
  23.7 0.0 copy-start.8
  23.7 5.6 %all-to-all-done = f32[8,64,128]{2,1,0:T(8,128)S(1)} async-done(((f32[8,64,128]{2,1,0:T(8,128)}), f32[8,64,128]{2,1,0:T(8,128)S(1)}, u32[]{:S(2)}, u32[]{:S(2)}) %all-to-all-start) | async-done | bytes 262176 | tf_op jit(solution)/shard_map/all_to_all | solution.py:320
  29.4 0.0 copy-done.8
  29.4 0.0 copy-start.9
  29.4 0.1 broadcast_in_dim.7.factor_ref
  29.5 0.6 %copy-done.9 = f32[256]{0:T(256)S(1)} copy-done((f32[256]{0:T(256)S(1)}, f32[256]{0:T(256)}, u32[]{:S(2)}) %copy-start.9) | copy-done | bytes 1048
  30.1 0.0 copy-start.10
  30.1 0.1 broadcast_in_dim.8.barrier_ref
  30.1 0.6 %copy-done.10 = f32[32]{0:T(128)S(1)} copy-done((f32[32]{0:T(128)S(1)}, f32[32]{0:T(128)}, u32[]{:S(2)}) %copy-start.10) | copy-done | bytes 152
  30.7 0.1 broadcast_in_dim.6.share_ref
  30.8 8.0 %columns.1 = f32[16,32,128]{2,1,0:T(8,128)S(1)} custom-call(f32[16,32,128]{2,1,0:T(8,128)S(1)} %bitcast.13, f32[16,128]{1,0:T(8,128)S(1)} %reshape.47.depth_ref, f32[32,128]{1,0:T(8,128)S(1)} %broadcast_in_dim.6.share_ref, f32[16,128]{1,0:T(8,128)S(1)} %reshape.48.kelvin_ref, s32[4,128]{1,0:T(4,128)S(1)} %pad_add_fusion.active_ref, ...), custom_call_target="tpu_custom_call" | custom-call | tf_op jit(solution)/shard_map/columns/pallas_call | solution.py:329
  38.8 13.9 %all_to_all.10.in_ref = f32[8,64,128]{2,1,0:T(8,128)} all-to-all(f32[8,64,128]{2,1,0:T(8,128)S(1)} %bitcast.14), channel_id=1, replica_groups=mesh['lat'=4,'lev'=8] {'lev'}, dimensions={0} | all-to-all | bytes 524288 | tf_op jit(solution)/shard_map/all_to_all | solution.py:352
  52.6 2.0 %spread.1 = f32[512,128]{1,0:T(8,128)} custom-call(f32[8,64,128]{2,1,0:T(8,128)} %all_to_all.10.in_ref), custom_call_target="tpu_custom_call" | custom-call | tf_op jit(solution)/shard_map/spread/pallas_call | solution.py:355
  (4 shorter events, 0.0 us)
Async XLA Ops:
  0.0 6.5 %collective-permute-start = (f32[32,4,4,128]{3,2,1,0:T(4,128)}, f32[32,4,4,128]{3,2,1,0:T(4,128)S(1)}, u32[]{:S(2)}, u32[]{:S(2)}) collective-permute-start(f32[32,4,4,128]{3,2,1,0:T(4,128)} %param.10), channel_id=1, source_target_pairs={{0,8},{8,0},{16,24},{24,16},{1,9},{9,1},{17,25},{25,17},{2,10},{10... | collective-permute-start | bytes 786440 | tf_op jit(solution)/shard_map/ppermute | solution.py:295
  0.5 6.1 %collective-permute-start.1 = (f32[32,4,4,128]{3,2,1,0:T(4,128)}, f32[32,4,4,128]{3,2,1,0:T(4,128)S(1)}, u32[]{:S(2)}, u32[]{:S(2)}) collective-permute-start(f32[32,4,4,128]{3,2,1,0:T(4,128)} %param.10), channel_id=1, source_target_pairs={{8,16},{16,8},{9,17},{17,9},{10,18},{18,10},{11,19},{19,11},{12,20... | collective-permute-start | bytes 786440 | tf_op jit(solution)/shard_map/ppermute | solution.py:296
  1.1 5.4 %collective-permute-start.2 = (f32[2,4,4,128]{3,2,1,0:T(4,128)}, f32[2,4,4,128]{3,2,1,0:T(4,128)S(1)}, u32[]{:S(2)}, u32[]{:S(2)}) collective-permute-start(f32[2,4,4,128]{3,2,1,0:T(4,128)} %param.11), channel_id=1, source_target_pairs={{0,8},{8,0},{16,24},{24,16},{1,9},{9,1},{17,25},{25,17},{2,10},{10... | collective-permute-start | bytes 49160 | tf_op jit(solution)/shard_map/ppermute | solution.py:293
  5.1 1.4 %collective-permute-start.3 = (f32[2,4,4,128]{3,2,1,0:T(4,128)}, f32[2,4,4,128]{3,2,1,0:T(4,128)S(1)}, u32[]{:S(2)}, u32[]{:S(2)}) collective-permute-start(f32[2,4,4,128]{3,2,1,0:T(4,128)} %param.11), channel_id=1, source_target_pairs={{8,16},{16,8},{9,17},{17,9},{10,18},{18,10},{11,19},{19,11},{12,20... | collective-permute-start | bytes 49160 | tf_op jit(solution)/shard_map/ppermute | solution.py:294
  6.5 0.6 %copy-start.4 = (f32[2,4,4,128]{3,2,1,0:T(4,128)}, f32[2,4,4,128]{3,2,1,0:T(4,128)S(1)}, u32[]{:S(2)}) copy-start(f32[2,4,4,128]{3,2,1,0:T(4,128)S(1)} %collective-permute-done.2) | copy-start | bytes 49156
  6.5 0.6 %copy-start.5 = (f32[2,4,4,128]{3,2,1,0:T(4,128)}, f32[2,4,4,128]{3,2,1,0:T(4,128)S(1)}, u32[]{:S(2)}) copy-start(f32[2,4,4,128]{3,2,1,0:T(4,128)S(1)} %collective-permute-done.3) | copy-start | bytes 49156
  6.5 0.7 %copy-start = (f32[32,4,4,128]{3,2,1,0:T(4,128)}, f32[32,4,4,128]{3,2,1,0:T(4,128)S(1)}, u32[]{:S(2)}) copy-start(f32[32,4,4,128]{3,2,1,0:T(4,128)S(1)} %collective-permute-done) | copy-start | bytes 786436
  6.6 0.8 %copy-start.1 = (f32[32,4,4,128]{3,2,1,0:T(4,128)}, f32[32,4,4,128]{3,2,1,0:T(4,128)S(1)}, u32[]{:S(2)}) copy-start(f32[32,4,4,128]{3,2,1,0:T(4,128)S(1)} %collective-permute-done.1) | copy-start | bytes 786436
  15.2 6.6 %copy-start.2 = (f32[32,4,16]{0,2,1:T(8,128)S(1)}, f32[32,4,16]{0,2,1:T(8,128)}, u32[]{:S(2)}) copy-start(f32[32,4,16]{0,2,1:T(8,128)} %param.12) | copy-start | bytes 24580
  15.2 14.2 %all-to-all-start = ((f32[8,64,128]{2,1,0:T(8,128)}), f32[8,64,128]{2,1,0:T(8,128)S(1)}, u32[]{:S(2)}, u32[]{:S(2)}) async-start(f32[8,64,128]{2,1,0:T(8,128)} %advect.1), calls=%async_computation | async-start | bytes 524288 | tf_op jit(solution)/shard_map/all_to_all | solution.py:320
  21.1 0.7 %copy-start.7 = (s32[2,256]{1,0:T(2,128)S(1)}, s32[2,256]{1,0:T(2,128)}, u32[]{:S(2)}) copy-start(s32[2,256]{1,0:T(2,128)} %param.19) | copy-start | bytes 6148
  21.9 0.8 %copy-start.3 = (f32[32,4,16]{0,2,1:T(8,128)S(1)}, f32[32,4,16]{0,2,1:T(8,128)}, u32[]{:S(2)}) copy-start(f32[32,4,16]{0,2,1:T(8,128)} %param.14) | copy-start | bytes 24580
  22.7 0.7 %copy-start.6 = (s32[4,4,16]{2,1,0:T(4,128)S(1)}, s32[4,4,16]{2,1,0:T(4,128)}, u32[]{:S(2)}) copy-start(s32[4,4,16]{2,1,0:T(4,128)} %param.15) | copy-start | bytes 3076
  23.7 5.6 %copy-start.8 = (f32[256]{0:T(256)S(1)}, f32[256]{0:T(256)}, u32[]{:S(2)}) copy-start(f32[256]{0:T(256)} %param.16) | copy-start | bytes 3076
  29.4 0.7 %copy-start.9 = (f32[256]{0:T(256)S(1)}, f32[256]{0:T(256)}, u32[]{:S(2)}) copy-start(f32[256]{0:T(256)} %param.17) | copy-start | bytes 3076
  30.1 0.7 %copy-start.10 = (f32[32]{0:T(128)S(1)}, f32[32]{0:T(128)}, u32[]{:S(2)}) copy-start(f32[32]{0:T(128)} %param.13) | copy-start | bytes 388

commit v3 on v2

--- a/solution.py
+++ b/solution.py
@@ -11,6 +11,7 @@
 OCTET = 8
 SWEEPS = 2
 VMEM = pl.BlockSpec(memory_space=pltpu.VMEM)
+PARAMS = pltpu.CompilerParams(vmem_limit_bytes=16 * 2**20)
 
 
 def limited_slope(left, right):
@@ -308,6 +309,7 @@
             pltpu.VMEM((4, 3 * levels * rows, lons), jnp.float32),
             pltpu.VMEM((4, 3 * rows - 3, levels, lons), jnp.float32),
         ],
+        compiler_params=PARAMS,
         name="advect",
     )(
         flat(species_fractions),
@@ -325,7 +327,7 @@
     )
     yields = species_yield_matrix.T.astype(jnp.bfloat16)
     active = daytime_indicator.reshape(substeps, -1)
-    tile_pairs = 4
+    tile_pairs = pairs // 2
     reacted = pl.pallas_call(
         functools.partial(column_kernel, (pairs, species, tile_pairs)),
         out_shape=jax.ShapeDtypeStruct((pairs, species, LANES), jnp.float32),
@@ -336,7 +338,7 @@
             pltpu.VMEM((all_levels, pairs, LANES), jnp.float32),
             pltpu.VMEM((reactions, tile_pairs * LANES), jnp.float32),
         ],
-        compiler_params=pltpu.CompilerParams(vmem_limit_bytes=32 * 2**20),
+        compiler_params=PARAMS,
         name="columns",
     )(
         moved.reshape(pairs, species, LANES),
@@ -357,6 +359,7 @@
         out_shape=jax.ShapeDtypeStruct((species * levels * rows * parts, LANES), jnp.float32),
         in_specs=[VMEM],
         out_specs=VMEM,
+        compiler_params=PARAMS,
         name="spread",
     )(returned)
     return out.reshape(species_fractions.shape)

time: 55.3 us -> 50.4 us (0.911)
  Pallas kernels: 17.9 us -> 12.7 us
    pallas_call x1, Pallas kernels: 8 us -> 4.9 us  [body(): pl.pallas_call(functools.partial(column_kernel, (pairs, species, tile_pai...]
    pallas_call x1, Pallas kernels: 7.85 us -> 6.73 us  [body(): pl.pallas_call(functools.partial(advect_kernel, sizes), out_shape=jax.Sha...]
    pallas_call x1, Pallas kernels: 2.02 us -> 1.08 us  [body(): pl.pallas_call(functools.partial(spread_kernel, sizes), out_shape=jax.Sha...]
    unnamed x25 -> x21, local copies, waits for them, and re-layouts: 3.99 us -> 4.19 us
where the time goes in v3:
time: 50.4 us; the launch traced here: 49.9 us
  blocking collectives  14 us (28%)
  Pallas kernels  12.7 us (25%)
  starting transfers between devices  11.6 us (23%)
  waiting for transfers between devices  5.63 us (11%)
  local copies, waits for them, and re-layouts  4.72 us (9%)
  other arithmetic  0.99 us (2%)
    all_to_all x1, blocking collectives, body(): lax.all_to_all(reacted.reshape(packed.shape), 'lev', split_axis=0, concat...  14 us
    pallas_call x1, Pallas kernels, body(): pl.pallas_call(functools.partial(advect_kernel, sizes), out_shape=jax.Sha...  6.73 us
    all_to_all x1, starting transfers between devices, body(): lax.all_to_all(packed, 'lev', split_axis=0, concat_axis=0, tiled=True)  5.94 us
    all_to_all x1, waiting for transfers between devices, body(): lax.all_to_all(packed, 'lev', split_axis=0, concat_axis=0, tiled=True)  5.62 us
    pallas_call x1, Pallas kernels, body(): pl.pallas_call(functools.partial(column_kernel, (pairs, species, tile_pai...  4.9 us
    unnamed x21, local copies, waits for them, and re-layouts  4.19 us
    ppermute x1, starting transfers between devices, body(): core_wind = lax.ppermute(cell_flow_ratios, 'lat', by_core)  3.93 us
    pallas_call x1, Pallas kernels, body(): pl.pallas_call(functools.partial(spread_kernel, sizes), out_shape=jax.Sha...  1.08 us
  transfers between devices with their start and end apart: 5, of which 1 were waited for; matrix products, arithmetic and copies ran while one was open for 3% of the time, Pallas kernels for 0%

profile of v3, /device:TPU:0, one launch (start us, length us, event | category | flops | bytes accessed | tf_op | source)
XLA Modules:
  0.0 49.9 jit_solution(942300615394149110)
XLA Ops:
  0.0 0.5 collective-permute-start
  0.5 0.7 %collective-permute-start.1 = (f32[32,4,4,128]{3,2,1,0:T(4,128)}, f32[32,4,4,128]{3,2,1,0:T(4,128)S(1)}, u32[]{:S(2)}, u32[]{:S(2)}) collective-permute-start(f32[32,4,4,128]{3,2,1,0:T(4,128)} %param.10), channel_id=1, source_target_pairs={{8,16},{16,8},{9,17},{17,9},{10,18},{18,10},{11,19},{19,11},{12,20... | collective-permute-start | bytes 786440 | tf_op jit(solution)/shard_map/ppermute | solution.py:297
  1.1 3.9 %collective-permute-start.2 = (f32[2,4,4,128]{3,2,1,0:T(4,128)}, f32[2,4,4,128]{3,2,1,0:T(4,128)S(1)}, u32[]{:S(2)}, u32[]{:S(2)}) collective-permute-start(f32[2,4,4,128]{3,2,1,0:T(4,128)} %param.11), channel_id=1, source_target_pairs={{0,8},{8,0},{16,24},{24,16},{1,9},{9,1},{17,25},{25,17},{2,10},{10... | collective-permute-start | bytes 49160 | tf_op jit(solution)/shard_map/ppermute | solution.py:294
  5.1 0.7 %collective-permute-start.3 = (f32[2,4,4,128]{3,2,1,0:T(4,128)}, f32[2,4,4,128]{3,2,1,0:T(4,128)S(1)}, u32[]{:S(2)}, u32[]{:S(2)}) collective-permute-start(f32[2,4,4,128]{3,2,1,0:T(4,128)} %param.11), channel_id=1, source_target_pairs={{8,16},{16,8},{9,17},{17,9},{10,18},{18,10},{11,19},{19,11},{12,20... | collective-permute-start | bytes 49160 | tf_op jit(solution)/shard_map/ppermute | solution.py:295
  5.7 0.0 copy-start.1
  5.7 0.8 %convert_bitcast_fusion = bf16[32,256]{1,0:T(8,128)(2,1)S(1)} fusion(s32[256,32]{0,1:T(8,128)} %param.18), kind=kLoop, calls=%fused_computation.3 | loop fusion | flops 8192 | bytes 49152 | tf_op jit(solution)/shard_map/convert_element_type | solution.py:328
  6.5 0.0 collective-permute-done.2
  6.5 0.0 collective-permute-done.3
  6.5 0.0 collective-permute-done
  6.5 0.0 collective-permute-done.1
  6.5 0.0 copy-done.1
  6.5 0.0 copy-start
  6.6 0.9 %copy-done = f32[32,4,4,128]{3,2,1,0:T(4,128)S(1)} copy-done((f32[32,4,4,128]{3,2,1,0:T(4,128)S(1)}, f32[32,4,4,128]{3,2,1,0:T(4,128)}, u32[]{:S(2)}) %copy-start) | copy-done | bytes 262168
  7.5 6.7 %advect.1 = f32[8,64,128]{2,1,0:T(8,128)} custom-call(f32[512,128]{1,0:T(8,128)S(1)} %bitcast.15, f32[512,128]{1,0:T(8,128)S(1)} %bitcast.16, f32[512,128]{1,0:T(8,128)S(1)} %bitcast.17, f32[32,128]{1,0:T(8,128)S(1)} %bitcast.18, f32[32,128]{1,0:T(8,128)S(1)} %bitcast.19, f32[32,128]{1,0:T(8,128)S(1)} %bitcast.20), custom_call_target="tpu_custom_call" | custom-call | tf_op jit(solution)/shard_map/advect/pallas_call | solution.py:302
  14.2 0.0 copy-start.2
  14.2 5.9 %all-to-all-start = ((f32[8,64,128]{2,1,0:T(8,128)}), f32[8,64,128]{2,1,0:T(8,128)S(1)}, u32[]{:S(2)}, u32[]{:S(2)}) async-start(f32[8,64,128]{2,1,0:T(8,128)} %advect.1), calls=%async_computation | async-start | bytes 524288 | tf_op jit(solution)/shard_map/all_to_all | solution.py:322
  20.2 0.0 copy-start.5
  20.2 0.7 %copy-done.5 = s32[2,256]{1,0:T(2,128)S(1)} copy-done((s32[2,256]{1,0:T(2,128)S(1)}, s32[2,256]{1,0:T(2,128)}, u32[]{:S(2)}) %copy-start.5) | copy-done | bytes 2072
  20.9 0.0 copy-done.2
  20.9 0.1 copy.13
  20.9 0.0 copy-start.3
  21.0 0.1 reshape.47.depth_ref
  21.1 0.7 %copy-done.3 = f32[32,4,16]{0,2,1:T(8,128)S(1)} copy-done((f32[32,4,16]{0,2,1:T(8,128)S(1)}, f32[32,4,16]{0,2,1:T(8,128)}, u32[]{:S(2)}) %copy-start.3) | copy-done | bytes 8216
  21.7 0.1 copy.14
  21.8 0.0 copy-start.4
  21.8 0.1 reshape.48.kelvin_ref
  21.9 0.6 %copy-done.4 = s32[4,4,16]{2,1,0:T(4,128)S(1)} copy-done((s32[4,4,16]{2,1,0:T(4,128)S(1)}, s32[4,4,16]{2,1,0:T(4,128)}, u32[]{:S(2)}) %copy-start.4) | copy-done | bytes 1048
  22.5 0.1 reshape.49
  22.6 0.1 pad_add_fusion.active_ref
  22.7 0.1 fusion.pick_ref
  22.8 0.0 copy-start.6
  22.8 5.6 %all-to-all-done = f32[8,64,128]{2,1,0:T(8,128)S(1)} async-done(((f32[8,64,128]{2,1,0:T(8,128)}), f32[8,64,128]{2,1,0:T(8,128)S(1)}, u32[]{:S(2)}, u32[]{:S(2)}) %all-to-all-start) | async-done | bytes 262176 | tf_op jit(solution)/shard_map/all_to_all | solution.py:322
  28.4 0.0 copy-done.6
  28.4 0.0 copy-start.7
  28.4 0.1 broadcast_in_dim.7.factor_ref
  28.5 0.6 %copy-done.7 = f32[256]{0:T(256)S(1)} copy-done((f32[256]{0:T(256)S(1)}, f32[256]{0:T(256)}, u32[]{:S(2)}) %copy-start.7) | copy-done | bytes 1048
  29.1 0.0 copy-start.8
  29.1 0.1 broadcast_in_dim.8.barrier_ref
  29.2 0.6 %copy-done.8 = f32[32]{0:T(128)S(1)} copy-done((f32[32]{0:T(128)S(1)}, f32[32]{0:T(128)}, u32[]{:S(2)}) %copy-start.8) | copy-done | bytes 152
  29.8 0.1 broadcast_in_dim.6.share_ref
  29.8 4.9 %columns.1 = f32[16,32,128]{2,1,0:T(8,128)S(1)} custom-call(f32[16,32,128]{2,1,0:T(8,128)S(1)} %bitcast.13, f32[16,128]{1,0:T(8,128)S(1)} %reshape.47.depth_ref, f32[32,128]{1,0:T(8,128)S(1)} %broadcast_in_dim.6.share_ref, f32[16,128]{1,0:T(8,128)S(1)} %reshape.48.kelvin_ref, s32[4,128]{1,0:T(4,128)S(1)} %pad_add_fusion.active_ref, ...), custom_call_target="tpu_custom_call" | custom-call | tf_op jit(solution)/shard_map/columns/pallas_call | solution.py:331
  34.8 14.0 %all_to_all.10.in_ref = f32[8,64,128]{2,1,0:T(8,128)S(1)} all-to-all(f32[8,64,128]{2,1,0:T(8,128)S(1)} %bitcast.14), channel_id=1, replica_groups=mesh['lat'=4,'lev'=8] {'lev'}, dimensions={0} | all-to-all | bytes 524288 | tf_op jit(solution)/shard_map/all_to_all | solution.py:354
  48.8 1.1 %spread.1 = f32[512,128]{1,0:T(8,128)} custom-call(f32[8,64,128]{2,1,0:T(8,128)S(1)} %all_to_all.10.in_ref), custom_call_target="tpu_custom_call" | custom-call | tf_op jit(solution)/shard_map/spread/pallas_call | solution.py:357
  (4 shorter events, 0.0 us)
Async XLA Ops:
  0.0 6.5 %collective-permute-start = (f32[32,4,4,128]{3,2,1,0:T(4,128)}, f32[32,4,4,128]{3,2,1,0:T(4,128)S(1)}, u32[]{:S(2)}, u32[]{:S(2)}) collective-permute-start(f32[32,4,4,128]{3,2,1,0:T(4,128)} %param.10), channel_id=1, source_target_pairs={{0,8},{8,0},{16,24},{24,16},{1,9},{9,1},{17,25},{25,17},{2,10},{10... | collective-permute-start | bytes 786440 | tf_op jit(solution)/shard_map/ppermute | solution.py:296
  0.5 6.1 %collective-permute-start.1 = (f32[32,4,4,128]{3,2,1,0:T(4,128)}, f32[32,4,4,128]{3,2,1,0:T(4,128)S(1)}, u32[]{:S(2)}, u32[]{:S(2)}) collective-permute-start(f32[32,4,4,128]{3,2,1,0:T(4,128)} %param.10), channel_id=1, source_target_pairs={{8,16},{16,8},{9,17},{17,9},{10,18},{18,10},{11,19},{19,11},{12,20... | collective-permute-start | bytes 786440 | tf_op jit(solution)/shard_map/ppermute | solution.py:297
  1.1 5.4 %collective-permute-start.2 = (f32[2,4,4,128]{3,2,1,0:T(4,128)}, f32[2,4,4,128]{3,2,1,0:T(4,128)S(1)}, u32[]{:S(2)}, u32[]{:S(2)}) collective-permute-start(f32[2,4,4,128]{3,2,1,0:T(4,128)} %param.11), channel_id=1, source_target_pairs={{0,8},{8,0},{16,24},{24,16},{1,9},{9,1},{17,25},{25,17},{2,10},{10... | collective-permute-start | bytes 49160 | tf_op jit(solution)/shard_map/ppermute | solution.py:294
  5.1 1.4 %collective-permute-start.3 = (f32[2,4,4,128]{3,2,1,0:T(4,128)}, f32[2,4,4,128]{3,2,1,0:T(4,128)S(1)}, u32[]{:S(2)}, u32[]{:S(2)}) collective-permute-start(f32[2,4,4,128]{3,2,1,0:T(4,128)} %param.11), channel_id=1, source_target_pairs={{8,16},{16,8},{9,17},{17,9},{10,18},{18,10},{11,19},{19,11},{12,20... | collective-permute-start | bytes 49160 | tf_op jit(solution)/shard_map/ppermute | solution.py:295
  5.7 0.8 %copy-start.1 = (f32[2,4,4,128]{3,2,1,0:T(4,128)S(1)}, f32[2,4,4,128]{3,2,1,0:T(4,128)}, u32[]{:S(2)}) copy-start(f32[2,4,4,128]{3,2,1,0:T(4,128)} %param.11) | copy-start | bytes 49156
  6.5 1.0 %copy-start = (f32[32,4,4,128]{3,2,1,0:T(4,128)S(1)}, f32[32,4,4,128]{3,2,1,0:T(4,128)}, u32[]{:S(2)}) copy-start(f32[32,4,4,128]{3,2,1,0:T(4,128)} %param.10) | copy-start | bytes 786436
  14.2 6.6 %copy-start.2 = (f32[32,4,16]{0,2,1:T(8,128)S(1)}, f32[32,4,16]{0,2,1:T(8,128)}, u32[]{:S(2)}) copy-start(f32[32,4,16]{0,2,1:T(8,128)} %param.12) | copy-start | bytes 24580
  14.2 14.2 %all-to-all-start = ((f32[8,64,128]{2,1,0:T(8,128)}), f32[8,64,128]{2,1,0:T(8,128)S(1)}, u32[]{:S(2)}, u32[]{:S(2)}) async-start(f32[8,64,128]{2,1,0:T(8,128)} %advect.1), calls=%async_computation | async-start | bytes 524288 | tf_op jit(solution)/shard_map/all_to_all | solution.py:322
  20.2 0.7 %copy-start.5 = (s32[2,256]{1,0:T(2,128)S(1)}, s32[2,256]{1,0:T(2,128)}, u32[]{:S(2)}) copy-start(s32[2,256]{1,0:T(2,128)} %param.19) | copy-start | bytes 6148
  20.9 0.8 %copy-start.3 = (f32[32,4,16]{0,2,1:T(8,128)S(1)}, f32[32,4,16]{0,2,1:T(8,128)}, u32[]{:S(2)}) copy-start(f32[32,4,16]{0,2,1:T(8,128)} %param.14) | copy-start | bytes 24580
  21.8 0.7 %copy-start.4 = (s32[4,4,16]{2,1,0:T(4,128)S(1)}, s32[4,4,16]{2,1,0:T(4,128)}, u32[]{:S(2)}) copy-start(s32[4,4,16]{2,1,0:T(4,128)} %param.15) | copy-start | bytes 3076
  22.8 5.6 %copy-start.6 = (f32[256]{0:T(256)S(1)}, f32[256]{0:T(256)}, u32[]{:S(2)}) copy-start(f32[256]{0:T(256)} %param.16) | copy-start | bytes 3076
  28.4 0.7 %copy-start.7 = (f32[256]{0:T(256)S(1)}, f32[256]{0:T(256)}, u32[]{:S(2)}) copy-start(f32[256]{0:T(256)} %param.17) | copy-start | bytes 3076
  29.1 0.7 %copy-start.8 = (f32[32]{0:T(128)S(1)}, f32[32]{0:T(128)}, u32[]{:S(2)}) copy-start(f32[32]{0:T(128)} %param.13) | copy-start | bytes 388

commit v4 on v1

v4 whole, which is shorter than its diff:
```python
import functools

import jax
import jax.numpy as jnp
from jax import lax
from jax.experimental import pallas as pl
from jax.experimental.pallas import tpu as pltpu
from jax.sharding import PartitionSpec as P

LANES = 128
PAD = 8
SWEEPS = 2
PARAMS = pltpu.CompilerParams(vmem_limit_bytes=16 * 2**20)
F32 = jnp.float32


def limited_slope(left, right):
    return jnp.maximum(jnp.minimum(left, right), 0.0) + jnp.minimum(jnp.maximum(left, right), 0.0)


def slope_weight(courant):
    return courant * (0.5 * (jnp.where(courant > 0.0, 1.0, -1.0) - courant))


def face_flux(courant, weight, before, after, before_slope, after_slope):
    ahead = courant > 0.0
    return courant * jnp.where(ahead, before, after) + weight * jnp.where(
        ahead, before_slope, after_slope
    )


def put_cyclic(ref, row, value):
    size = value.shape[0]
    ref[row, PAD : PAD + size] = value
    ref[row, PAD - 1 : PAD] = value[size - 1 :]
    ref[row, PAD + size : PAD + size + 1] = value[:1]


def shifted(ref, row, size, by):
    return ref[row, PAD + by : PAD + by + size]


def lon_step(f_ref, slope_ref, flux_ref, row, courant, weight):
    size = courant.shape[0]
    f, left, right = (shifted(f_ref, row, size, by) for by in (0, -1, 1))
    slope = limited_slope(f - left, right - f)
    put_cyclic(slope_ref, row, slope)
    flux = face_flux(courant, weight, left, f, shifted(slope_ref, row, size, -1), slope)
    put_cyclic(flux_ref, row, flux)
    return f - (shifted(flux_ref, row, size, 1) - flux)


def lat_step(f, weights):
    jumps = [f[i + 1] - f[i] for i in range(len(f) - 1)]
    slopes = [None] + [limited_slope(jumps[i - 1], jumps[i]) for i in range(1, len(f) - 1)]
    fluxes = [
        face_flux(*weights[i - 2], f[i - 1], f[i], slopes[i - 1], slopes[i])
        for i in range(2, len(f) - 1)
    ]
    return [f[i] - (fluxes[i - 1] - fluxes[i - 2]) for i in range(2, len(f) - 2)]


def tracer_rows(sizes, ref, row):
    species, levels, rows, parts, _ = sizes
    return [
        ref[pl.ds(row * parts + k, species * levels, rows * parts), :] for k in range(parts)
    ]


def flow_rows(sizes, ref, which, row):
    species, levels, rows, parts, _ = sizes
    found = []
    for k in range(parts):
        start = (which * levels * rows + row) * parts + k
        level_rows = ref[pl.ds(start, levels, rows * parts), :]
        tile = jnp.concatenate([level_rows] * (8 // levels), axis=0)
        found.append(jnp.concatenate([tile] * (species * levels // 8), axis=0))
    return found


def turned(tiles):
    return jnp.concatenate([tile.T for tile in tiles], axis=0)


def zonal_weights(flow_ref, row, flow):
    put_cyclic(flow_ref, row, flow)
    courant = 0.5 * (shifted(flow_ref, row, flow.shape[0], -1) + flow)
    return courant, slope_weight(courant)


def own_kernel(
    sizes, band_ref, wind_ref, f_out, zonal_out, merid_out, f_ref, slope_ref, flux_ref, flow_ref
):
    rows = sizes[2]
    for row in range(rows):
        courant, weight = zonal_weights(
            flow_ref, row, turned(flow_rows(sizes, wind_ref, 0, row))
        )
        zonal_out[row, 0], zonal_out[row, 1] = courant, weight
        merid_out[row] = turned(flow_rows(sizes, wind_ref, 1, row))
        put_cyclic(f_ref, row, turned(tracer_rows(sizes, band_ref, row)))
        f_out[row] = lon_step(f_ref, slope_ref, flux_ref, row, courant, weight)


def advect_kernel(
    sizes,
    own_ref,
    own_zonal,
    own_merid,
    core_ref,
    chip_ref,
    core_wind,
    chip_wind,
    out_ref,
    f_ref,
    slope_ref,
    flux_ref,
    flow_ref,
    halo_zonal,
    halo_merid,
    merid_ref,
    next_ref,
):
    species, levels, rows, parts, width = sizes
    band = lax.axis_index("lat")
    even = band % 2 == 0

    def both_sides(by_core, by_chip):
        pairs = list(zip(by_core, by_chip, strict=True))
        before = [jnp.where(even, chip, core) for core, chip in pairs]
        after = [jnp.where(even, core, chip) for core, chip in pairs]
        return before, after

    for row in range(rows):
        zonal = both_sides(
            flow_rows(sizes, core_wind, 0, row), flow_rows(sizes, chip_wind, 0, row)
        )
        merid = both_sides(
            flow_rows(sizes, core_wind, 1, row), flow_rows(sizes, chip_wind, 1, row)
        )
        tracer = both_sides(
            tracer_rows(sizes, core_ref, row), tracer_rows(sizes, chip_ref, row)
        )
        for side in range(2):
            at = side * rows + row
            courant, weight = zonal_weights(flow_ref, at, turned(zonal[side]))
            halo_zonal[at, 0], halo_zonal[at, 1] = courant, weight
            halo_merid[at] = turned(merid[side])
            put_cyclic(f_ref, at, turned(tracer[side]))
            f_ref[at, PAD : PAD + courant.shape[0]] = lon_step(
                f_ref, slope_ref, flux_ref, at, courant, weight
            )

    def row_of(halo, own, row):
        if 0 <= row < rows:
            return own, row
        return halo, (row + rows if row < 0 else row)

    total = rows * lax.axis_size("lat")
    size = own_ref.shape[1]
    first_face, last_face = 2 - 2 * SWEEPS, rows + 2 * SWEEPS - 2
    for chunk in range(size // width):
        there = slice(chunk * width, (chunk + 1) * width)
        inner = slice(PAD + chunk * width, PAD + (chunk + 1) * width)

        def merid_at(row):
            ref, at = row_of(halo_merid, own_merid, row)
            return ref[at, there]

        weights = []
        for face in range(first_face, last_face + 1):
            place = band * rows + face
            open_face = jnp.logical_and(place >= 1, place <= total - 1).astype(F32)
            courant = 0.5 * (merid_at(face - 1) + merid_at(face)) * open_face
            weights.append((courant, slope_weight(courant)))
            if 0 <= face <= rows:
                merid_ref[face, 0, there], merid_ref[face, 1, there] = weights[-1]
        f = []
        for row in range(-rows, 2 * rows):
            ref, at = row_of(f_ref, own_ref, row)
            f.append(ref[at, there if ref is own_ref else inner])
        for at, value in enumerate(lat_step(f, weights)):
            next_ref[at, inner] = value

    swept = rows + 2 * SWEEPS
    for at in range(swept):
        next_ref[at, PAD - 1 : PAD] = next_ref[at, PAD + size - 1 : PAD + size]
        next_ref[at, PAD + size : PAD + size + 1] = next_ref[at, PAD : PAD + 1]
        ref, there = row_of(halo_zonal, own_zonal, at - 2)
        f_ref[at, PAD : PAD + size] = lon_step(
            next_ref, slope_ref, flux_ref, at, ref[there, 0], ref[there, 1]
        )
    for chunk in range(size // width):
        there = slice(chunk * width, (chunk + 1) * width)
        inner = slice(PAD + chunk * width, PAD + (chunk + 1) * width)
        f = [f_ref[at, inner] for at in range(swept)]
        weights = [
            (merid_ref[face, 0, there], merid_ref[face, 1, there]) for face in range(rows + 1)
        ]
        for row, value in enumerate(lat_step(f, weights)):
            out_ref[chunk, row * width : (row + 1) * width] = value


def spread_kernel(sizes, in_ref, out_ref):
    species, levels, rows, parts, width = sizes
    per_part = LANES // width
    for row in range(rows):
        for k in range(parts):
            found = [
                in_ref[k * per_part + j, row * width : (row + 1) * width] for j in range(per_part)
            ]
            out_ref[pl.ds(row * parts + k, species * levels, rows * parts), :] = jnp.concatenate(
                found, axis=0
            ).T


def paired(groups, levels, ref, place):
    rows, width = ref.shape[1], ref.shape[2]
    for pair in range(groups // 2):
        for parity in range(2):
            start = (2 * pair + parity) * levels
            for row in range(rows):
                lane = (parity * rows + row) * width
                place[pair * levels : (pair + 1) * levels, lane : lane + width] = ref[
                    start : start + levels, row, :
                ]


def prepare_kernel(
    groups,
    depth_ref,
    share_ref,
    kelvin_ref,
    active_ref,
    factor_ref,
    barrier_ref,
    yield_ref,
    pair_ref,
    overlap_out,
    rate_out,
    active_out,
    pick_out,
    yield_out,
    depth_at,
    kelvin_at,
    lower_at,
):
    all_levels, rows, width = depth_ref.shape
    levels = all_levels // groups
    half = LANES // 2
    odd = lax.broadcasted_iota(jnp.int32, (1, LANES), 1) >= half
    reactions, species = yield_ref.shape

    paired(groups, levels, kelvin_ref, kelvin_at)
    paired(groups, levels, depth_ref, depth_at)
    for parity in range(2):
        for row in range(rows):
            lane = (parity * rows + row) * width
            active_out[:, lane : lane + width] = active_ref[:, row, :]

    def column(ref):
        return jnp.broadcast_to(ref[...], (LANES, ref.shape[1])).T

    base = jnp.zeros((1, LANES), F32)
    for pair in range(groups // 2):
        inside = jnp.zeros((1, LANES), F32)
        for level in range(levels):
            at = pair * levels + level
            lower_at[at : at + 1] = inside
            inside = inside + depth_at[at : at + 1]
        other = pltpu.roll(inside, half, 1)
        start = base + jnp.where(odd, other, 0.0)
        here = slice(pair * levels, (pair + 1) * levels)
        lower_at[here] = lower_at[here] + start
        base = base + (inside + other)
    total = base
    lower = lower_at[...]
    upper = lower + depth_at[...]

    share = column(share_ref)
    share_sum = share[0:1]
    for t in range(1, all_levels):
        share_sum = share_sum + share[t : t + 1]
    below = jnp.zeros((1, LANES), F32)
    target_low = below
    for t in range(all_levels):
        below = below + share[t : t + 1]
        target_top = below / share_sum * total
        shared = jnp.maximum(
            jnp.minimum(upper, target_top) - jnp.maximum(lower, target_low), 0.0
        )
        overlap_out[t] = shared / (share[t : t + 1] / share_sum * total)
        target_low = target_top

    factor, barrier = column(factor_ref), column(barrier_ref)
    for at in range(kelvin_at.shape[0]):
        warmth = 300.0 / kelvin_at[at : at + 1] - 1.0
        rate_out[:, at * LANES : (at + 1) * LANES] = factor * jnp.exp(-barrier * warmth)

    one_species = lax.broadcasted_iota(jnp.int32, (2 * species, reactions), 0) % species
    for which in range(2):
        hit = (one_species == pair_ref[which : which + 1, :]).astype(F32)
        pick_out[which * reactions : (which + 1) * reactions] = hit.T.astype(jnp.bfloat16)
    yields = yield_ref[...].astype(F32).T.astype(jnp.bfloat16)
    yield_out[:, :reactions] = yields
    yield_out[:, reactions:] = yields


def column_kernel(
    sizes,
    moved_ref,
    overlap_ref,
    rate_ref,
    active_ref,
    pick_ref,
    yield_ref,
    out_ref,
    source_ref,
    target_ref,
):
    groups, levels, species, tile_pairs = sizes
    half = LANES // 2
    pairs = groups // 2 * levels
    reactions = yield_ref.shape[1] // 2
    odd = lax.broadcasted_iota(jnp.int32, (1, LANES), 1) >= half

    for pair in range(groups // 2):
        both = jnp.concatenate([moved_ref[2 * pair], moved_ref[2 * pair + 1]], axis=0)
        source_ref[pair] = both.T

    def remapped(at):
        pair, level = divmod(at, levels)
        sums = []
        for parity in range(2):
            t = (2 * pair + parity) * levels + level
            acc = None
            for s in range(pairs):
                source = source_ref[s // levels, pl.ds(s % levels, species, levels), :]
                term = overlap_ref[t, s : s + 1, :] * source
                acc = term if acc is None else acc + term
            sums.append(acc)
        kept = jnp.where(odd, sums[1], sums[0])
        crossed = jnp.where(odd, sums[0], sums[1])
        return kept + pltpu.roll(crossed, half, 1)

    for first in range(0, pairs, tile_pairs):
        tile = range(first, first + tile_pairs)
        lanes = slice(first * LANES, (first + tile_pairs) * LANES)
        q = jnp.concatenate([remapped(at) for at in tile], axis=1)
        for substep in range(active_ref.shape[0]):
            on = jnp.concatenate([active_ref[substep : substep + 1, :]] * tile_pairs, axis=1)
            high = q.astype(jnp.bfloat16)
            low = (q - high.astype(F32)).astype(jnp.bfloat16)
            picked = jnp.dot(
                pick_ref[...], jnp.concatenate([high, low], axis=0), preferred_element_type=F32
            )
            rates = rate_ref[:, lanes] * picked[:reactions] * picked[reactions:]
            high = rates.astype(jnp.bfloat16)
            low = (rates - high.astype(F32)).astype(jnp.bfloat16)
            change = jnp.dot(
                yield_ref[...], jnp.concatenate([high, low], axis=0), preferred_element_type=F32
            )
            q = jnp.where(on > 0, q + change, q)
        for at in tile:
            pair, level = divmod(at, levels)
            lane = (at - first) * LANES
            target_ref[pair, pl.ds(level, species, levels), :] = q[:, lane : lane + LANES]

    for pair in range(groups // 2):
        both = target_ref[pair].T
        out_ref[2 * pair], out_ref[2 * pair + 1] = both[:half], both[half:]


def swap_pairs(count, first):
    route = []
    for low in range(first, count - 1, 2):
        route += [(low, low + 1), (low + 1, low)]
    return route


def kernel_call(kernel, name, outs, scratch, cost=None):
    return pl.pallas_call(
        kernel,
        out_shape=outs,
        scratch_shapes=[pltpu.VMEM(shape, F32) for shape in scratch],
        compiler_params=PARAMS,
        cost_estimate=cost,
        name=name,
    )


def body(
    species_fractions,
    cell_flow_ratios,
    layer_pressure_depth,
    layer_thickness_fraction,
    cell_kelvin_field,
    daytime_indicator,
    kinetic_factor_times_step,
    arrhenius_barrier,
    species_yield_matrix,
    reagent_pairs,
):
    species, levels, rows, lons = species_fractions.shape
    all_levels = layer_pressure_depth.shape[0]
    width = layer_pressure_depth.shape[2]
    blocks = lax.axis_size("lev")
    bands = lax.axis_size("lat")
    parts = lons // LANES
    substeps = daytime_indicator.shape[0]
    reactions = kinetic_factor_times_step.shape[0]
    assert 2 * rows * width == LANES and rows == 2 * SWEEPS and blocks % 2 == 0
    sizes = (species, levels, rows, parts, width)
    mixed = species * levels

    by_core, by_chip = swap_pairs(bands, 0), swap_pairs(bands, 1)
    core_band = lax.ppermute(species_fractions, "lat", by_core)
    chip_band = lax.ppermute(species_fractions, "lat", by_chip)
    core_wind = lax.ppermute(cell_flow_ratios, "lat", by_core)
    chip_wind = lax.ppermute(cell_flow_ratios, "lat", by_chip)

    def flat(value):
        return value.reshape(-1, LANES)

    def arrays(*shapes):
        return [jax.ShapeDtypeStruct(shape, F32) for shape in shapes]

    padded = lons + 2 * PAD
    own = kernel_call(
        functools.partial(own_kernel, sizes),
        "own_rows",
        arrays((rows, lons, mixed), (rows, 2, lons, mixed), (rows, lons, mixed)),
        [(rows, padded, mixed)] * 4,
        pl.CostEstimate(flops=10**7, bytes_accessed=2 * 10**6, transcendentals=0),
    )(flat(species_fractions), flat(cell_flow_ratios))

    packed = kernel_call(
        functools.partial(advect_kernel, sizes),
        "advect",
        arrays((blocks, rows * width, mixed))[0],
        [(2 * rows, padded, mixed)] * 4
        + [
            (2 * rows, 2, lons, mixed),
            (2 * rows, lons, mixed),
            (rows + 1, 2, lons, mixed),
            (2 * rows, padded, mixed),
        ],
    )(*own, flat(core_band), flat(chip_band), flat(core_wind), flat(chip_wind))
    moved = lax.all_to_all(packed, "lev", split_axis=0, concat_axis=0, tiled=True)

    pairs = all_levels // 2
    prepared = kernel_call(
        functools.partial(prepare_kernel, blocks),
        "prepare",
        [
            *arrays((all_levels, pairs, LANES), (reactions, pairs * LANES)),
            jax.ShapeDtypeStruct((substeps, LANES), jnp.int32),
            jax.ShapeDtypeStruct((2 * reactions, 2 * species), jnp.bfloat16),
            jax.ShapeDtypeStruct((species, 2 * reactions), jnp.bfloat16),
        ],
        [(pairs, LANES)] * 3,
        pl.CostEstimate(flops=10**7, bytes_accessed=5 * 10**6, transcendentals=10**6),
    )(
        layer_pressure_depth,
        layer_thickness_fraction[None],
        cell_kelvin_field,
        daytime_indicator,
        kinetic_factor_times_step[None],
        arrhenius_barrier[None],
        species_yield_matrix,
        reagent_pairs,
    )
    reacted = kernel_call(
        functools.partial(column_kernel, (blocks, levels, species, pairs // 2)),
        "columns",
        arrays(packed.shape)[0],
        [(blocks // 2, mixed, LANES)] * 2,
    )(moved, *prepared)
    returned = lax.all_to_all(reacted, "lev", split_axis=0, concat_axis=0, tiled=True)
    out = kernel_call(
        functools.partial(spread_kernel, sizes),
        "spread",
        arrays((mixed * rows * parts, LANES))[0],
        [],
    )(returned)
    return out.reshape(species_fractions.shape)


def solution(mesh):
    placed = (
        P(None, "lev", "lat", None),
        P(None, "lev", "lat", None),
        P(None, "lat", "lev"),
        P(),
        P(None, "lat", "lev"),
        P(None, "lat", "lev"),
        P(),
        P(),
        P(),
        P(),
    )
    return jax.shard_map(
        body, mesh=mesh, in_specs=placed, out_specs=P(None, "lev", "lat", None), check_vma=False
    )
```

time: 126 us -> 46.5 us (0.37)
  local copies, waits for them, and re-layouts: 32.7 us -> 1.96 us
  between operations: 20.6 us -> 0.15 us
  matrix products: 18 us -> 0 us
  Pallas kernels: 0 us -> 9.25 us
  starting transfers between devices: 21.6 us -> 13 us
  other arithmetic: 7.94 us -> 0 us
  blocking collectives: 14.4 us -> 12.6 us
    dot_general x5 -> x0, matrix products: 18 us -> none  [the longest x4 15.2 us: react_block(): jnp.dot(yield_matrix_floating.T, rates, precision=lax.Precision.HIGHEST)]
    gather x8 -> x0, local copies, waits for them, and re-layouts: 17.8 us -> none  [the longest x4 10.7 us: react_block(): jnp.take(flattened, first_axis_position, axis=0)]
    pallas_call x0 -> x5, Pallas kernels: none -> 9.25 us  [the longest x1 4.89 us: body(): kernel_call(functools.partial(column_kernel, (blocks, levels, species, pa...]
    ppermute x6 -> x4, starting transfers between devices: 15.8 us -> 7.19 us  [the longest x1 4.39 us: body(): core_band = lax.ppermute(species_fractions, 'lat', by_core)]
    slice x16 -> x0, local copies, waits for them, and re-layouts: 4.78 us -> none  [the longest x4 2.73 us: lon_update(): before = jnp.roll(tracer, 1, axis=-1)]
    ppermute x6 -> x4, waiting for transfers between devices: 3.15 us -> 0.01 us  [the longest x1 0.01 us: body(): chip_wind = lax.ppermute(cell_flow_ratios, 'lat', by_chip)]
    all_to_all x2 -> x0, other arithmetic: 2.52 us -> none  [the longest x1 1.26 us: back_to_levels(): lax.all_to_all(vertical_profiles, 'lev', split_axis=1, concat_axis=3, til...]
    all_to_all x1, waiting for transfers between devices: 6.7 us -> 9.18 us  [body(): lax.all_to_all(packed, 'lev', split_axis=0, concat_axis=0, tiled=True)]
  transfers between devices with their start and end apart: 7 -> 5, of which waited for: 2 -> 1; matrix products, arithmetic and copies ran while one was open for 8% -> 1% of each run, Pallas kernels for 0% -> 2%
where the time goes in v4:
time: 46.5 us; the launch traced here: 46.2 us
  starting transfers between devices  13 us (28%)
  blocking collectives  12.6 us (27%)
  Pallas kernels  9.25 us (20%)
  waiting for transfers between devices  9.19 us (20%)
  local copies, waits for them, and re-layouts  1.96 us (4%)
    all_to_all x1, blocking collectives, body(): lax.all_to_all(reacted, 'lev', split_axis=0, concat_axis=0, tiled=True)  12.6 us
    all_to_all x1, waiting for transfers between devices, body(): lax.all_to_all(packed, 'lev', split_axis=0, concat_axis=0, tiled=True)  9.18 us
    all_to_all x1, starting transfers between devices, body(): lax.all_to_all(packed, 'lev', split_axis=0, concat_axis=0, tiled=True)  5.81 us
    pallas_call x1, Pallas kernels, body(): kernel_call(functools.partial(column_kernel, (blocks, levels, species, pa...  4.89 us
    ppermute x1, starting transfers between devices, body(): core_band = lax.ppermute(species_fractions, 'lat', by_core)  4.39 us
    pallas_call x1, Pallas kernels, body(): kernel_call(functools.partial(advect_kernel, sizes), 'advect', arrays((bl...  2.48 us
    unnamed x23, local copies, waits for them, and re-layouts  1.96 us
    ppermute x1, starting transfers between devices, body(): core_wind = lax.ppermute(cell_flow_ratios, 'lat', by_core)  1.35 us
  transfers between devices with their start and end apart: 5, of which 1 were waited for; matrix products, arithmetic and copies ran while one was open for 1% of the time, Pallas kernels for 2%

profile of v4, /device:TPU:0, one launch (start us, length us, event | category | flops | bytes accessed | tf_op | source)
XLA Modules:
  0.0 46.2 jit_solution(9454057027167452160)
XLA Ops:
  0.0 0.0 copy-start.3
  0.0 0.0 copy-start.4
  0.0 0.0 copy-start.6
  0.0 0.8 %collective-permute-start.1 = (f32[32,4,4,128]{3,2,1,0:T(4,128)}, f32[32,4,4,128]{3,2,1,0:T(4,128)S(1)}, u32[]{:S(2)}, u32[]{:S(2)}) collective-permute-start(f32[32,4,4,128]{3,2,1,0:T(4,128)} %param.10), channel_id=1, source_target_pairs={{8,16},{16,8},{9,17},{17,9},{10,18},{18,10},{11,19},{19,11},{12,20... | collective-permute-start | bytes 786440 | tf_op jit(solution)/shard_map/ppermute | solution.py:418
  0.8 4.4 %collective-permute-start = (f32[32,4,4,128]{3,2,1,0:T(4,128)}, f32[32,4,4,128]{3,2,1,0:T(4,128)S(1)}, u32[]{:S(2)}, u32[]{:S(2)}) collective-permute-start(f32[32,4,4,128]{3,2,1,0:T(4,128)} %param.10), channel_id=1, source_target_pairs={{0,8},{8,0},{16,24},{24,16},{1,9},{9,1},{17,25},{25,17},{2,10},{10... | collective-permute-start | bytes 786440 | tf_op jit(solution)/shard_map/ppermute | solution.py:417
  5.2 0.7 %collective-permute-start.3 = (f32[2,4,4,128]{3,2,1,0:T(4,128)}, f32[2,4,4,128]{3,2,1,0:T(4,128)S(1)}, u32[]{:S(2)}, u32[]{:S(2)}) collective-permute-start(f32[2,4,4,128]{3,2,1,0:T(4,128)} %param.11), channel_id=1, source_target_pairs={{8,16},{16,8},{9,17},{17,9},{10,18},{18,10},{11,19},{19,11},{12,20... | collective-permute-start | bytes 49160 | tf_op jit(solution)/shard_map/ppermute | solution.py:420
  5.9 1.3 %collective-permute-start.2 = (f32[2,4,4,128]{3,2,1,0:T(4,128)}, f32[2,4,4,128]{3,2,1,0:T(4,128)S(1)}, u32[]{:S(2)}, u32[]{:S(2)}) collective-permute-start(f32[2,4,4,128]{3,2,1,0:T(4,128)} %param.11), channel_id=1, source_target_pairs={{0,8},{8,0},{16,24},{24,16},{1,9},{9,1},{17,25},{25,17},{2,10},{10... | collective-permute-start | bytes 49160 | tf_op jit(solution)/shard_map/ppermute | solution.py:419
  7.2 0.0 copy-start
  7.2 0.9 %copy-done = f32[32,4,4,128]{3,2,1,0:T(4,128)S(1)} copy-done((f32[32,4,4,128]{3,2,1,0:T(4,128)S(1)}, f32[32,4,4,128]{3,2,1,0:T(4,128)}, u32[]{:S(2)}) %copy-start) | copy-done | bytes 262168
  8.2 0.0 copy-start.1
  8.2 0.7 %copy-done.1 = f32[2,4,4,128]{3,2,1,0:T(4,128)S(1)} copy-done((f32[2,4,4,128]{3,2,1,0:T(4,128)S(1)}, f32[2,4,4,128]{3,2,1,0:T(4,128)}, u32[]{:S(2)}) %copy-start.1) | copy-done | bytes 16408
  8.9 0.0 copy-start.7
  8.9 0.0 copy-start.8
  8.9 0.0 copy-start.9
  8.9 0.0 copy-start.2
  8.9 0.0 copy-start.5
  8.9 0.4 own_rows.1
  9.3 0.0 collective-permute-done.3
  9.3 0.0 collective-permute-done.2
  9.3 0.0 collective-permute-done.1
  9.3 0.0 collective-permute-done
  9.4 2.5 %advect.1 = f32[8,64,128]{2,1,0:T(8,128)} custom-call(f32[4,128,128]{2,1,0:T(8,128)S(1)} %get-tuple-element.13.own_ref, f32[4,2,128,128]{3,2,1,0:T(8,128)S(1)} %get-tuple-element.14.own_zonal, f32[4,128,128]{2,1,0:T(8,128)S(1)} %get-tuple-element.15.own_merid, f32[512,128]{1,0:T(8,128)S(1)} %bitcast.11, f32[512,128]{1,0:T(8,128)S(1)} %bitcast.10, ...), custom_call_target="tpu_custom_call" | custom-call | tf_op jit(solution)/shard_map/advect/pallas_call | solution.py:437
  11.8 5.8 %all-to-all-start = ((f32[8,64,128]{2,1,0:T(8,128)}), f32[8,64,128]{2,1,0:T(8,128)S(1)}, u32[]{:S(2)}, u32[]{:S(2)}) async-start(f32[8,64,128]{2,1,0:T(8,128)} %advect.1), calls=%async_computation | async-start | bytes 524288 | tf_op jit(solution)/shard_map/all_to_all | solution.py:449
  17.6 0.0 copy-done.7
  17.6 0.1 copy.11.depth_ref
  17.7 0.0 copy-done.8
  17.7 0.1 copy.12.kelvin_ref
  17.8 0.0 copy-done.9
  17.8 0.1 copy.13.yield_ref
  17.9 0.0 copy-done.3
  17.9 0.0 copy-done.4
  18.0 0.0 copy-done.6
  18.0 0.0 copy-done.2
  18.0 0.0 copy-done.5
  18.0 0.6 %prepare.1 = (f32[32,16,128]{2,1,0:T(8,128)S(1)}, f32[256,2048]{1,0:T(8,128)S(1)}, s32[4,128]{1,0:T(4,128)S(1)}, bf16[512,64]{1,0:T(8,128)(2,1)S(1)}, bf16[32,512]{1,0:T(8,128)(2,1)S(1)}) custom-call(f32[32,4,16]{2,1,0:T(4,128)S(1)} %copy.11.depth_ref, f32[1,32]{1,0:T(1,128)S(1)} %bitcast.18, f32[32,4,16]{2,1,0:T(4,128)S(1)} %copy.12.kelvin_ref, ...), custom_call_target="tpu_custom_call" | custom-call | flops 10000000 | bytes 5000000 | tf_op jit(solution)/shard_map/prepare/pallas_call | solution.py:452
  18.6 9.2 %all-to-all-done.moved_ref = f32[8,64,128]{2,1,0:T(8,128)S(1)} async-done(((f32[8,64,128]{2,1,0:T(8,128)}), f32[8,64,128]{2,1,0:T(8,128)S(1)}, u32[]{:S(2)}, u32[]{:S(2)}) %all-to-all-start) | async-done | bytes 262176 | tf_op jit(solution)/shard_map/all_to_all | solution.py:449
  27.8 4.9 %columns.1 = f32[8,64,128]{2,1,0:T(8,128)S(1)} custom-call(f32[8,64,128]{2,1,0:T(8,128)S(1)} %all-to-all-done.moved_ref, f32[32,16,128]{2,1,0:T(8,128)S(1)} %get-tuple-element.16.overlap_ref, f32[256,2048]{1,0:T(8,128)S(1)} %get-tuple-element.17.rate_ref, s32[4,128]{1,0:T(4,128)S(1)} %get-tuple-element.18.active_ref, ...), custom_call_target="tpu_custom_call" | custom-call | tf_op jit(solution)/shard_map/columns/pallas_call | solution.py:473
  32.7 12.6 %all_to_all.10.in_ref = f32[8,64,128]{2,1,0:T(8,128)S(1)} all-to-all(f32[8,64,128]{2,1,0:T(8,128)S(1)} %columns.1), channel_id=1, replica_groups=mesh['lat'=4,'lev'=8] {'lev'}, dimensions={0} | all-to-all | bytes 524288 | tf_op jit(solution)/shard_map/all_to_all | solution.py:479
  45.3 0.8 %spread.1 = f32[512,128]{1,0:T(8,128)} custom-call(f32[8,64,128]{2,1,0:T(8,128)S(1)} %all_to_all.10.in_ref), custom_call_target="tpu_custom_call" | custom-call | tf_op jit(solution)/shard_map/spread/pallas_call | solution.py:480
Async XLA Ops:
  0.0 17.9 %copy-start.3 = (s32[2,256]{1,0:T(2,128)S(1)}, s32[2,256]{1,0:T(2,128)}, u32[]{:S(2)}) copy-start(s32[2,256]{1,0:T(2,128)} %pair_ref.1) | copy-start | bytes 6148
  0.0 17.9 %copy-start.4 = (f32[256]{0:T(256)S(1)}, f32[256]{0:T(256)}, u32[]{:S(2)}) copy-start(f32[256]{0:T(256)} %param.16) | copy-start | bytes 3076
  0.0 18.0 %copy-start.6 = (f32[32]{0:T(128)S(1)}, f32[32]{0:T(128)}, u32[]{:S(2)}) copy-start(f32[32]{0:T(128)} %param.13) | copy-start | bytes 388
  0.0 9.3 %collective-permute-start.1 = (f32[32,4,4,128]{3,2,1,0:T(4,128)}, f32[32,4,4,128]{3,2,1,0:T(4,128)S(1)}, u32[]{:S(2)}, u32[]{:S(2)}) collective-permute-start(f32[32,4,4,128]{3,2,1,0:T(4,128)} %param.10), channel_id=1, source_target_pairs={{8,16},{16,8},{9,17},{17,9},{10,18},{18,10},{11,19},{19,11},{12,20... | collective-permute-start | bytes 786440 | tf_op jit(solution)/shard_map/ppermute | solution.py:418
  0.8 8.5 %collective-permute-start = (f32[32,4,4,128]{3,2,1,0:T(4,128)}, f32[32,4,4,128]{3,2,1,0:T(4,128)S(1)}, u32[]{:S(2)}, u32[]{:S(2)}) collective-permute-start(f32[32,4,4,128]{3,2,1,0:T(4,128)} %param.10), channel_id=1, source_target_pairs={{0,8},{8,0},{16,24},{24,16},{1,9},{9,1},{17,25},{25,17},{2,10},{10... | collective-permute-start | bytes 786440 | tf_op jit(solution)/shard_map/ppermute | solution.py:417
  5.2 4.1 %collective-permute-start.3 = (f32[2,4,4,128]{3,2,1,0:T(4,128)}, f32[2,4,4,128]{3,2,1,0:T(4,128)S(1)}, u32[]{:S(2)}, u32[]{:S(2)}) collective-permute-start(f32[2,4,4,128]{3,2,1,0:T(4,128)} %param.11), channel_id=1, source_target_pairs={{8,16},{16,8},{9,17},{17,9},{10,18},{18,10},{11,19},{19,11},{12,20... | collective-permute-start | bytes 49160 | tf_op jit(solution)/shard_map/ppermute | solution.py:420
  5.9 3.5 %collective-permute-start.2 = (f32[2,4,4,128]{3,2,1,0:T(4,128)}, f32[2,4,4,128]{3,2,1,0:T(4,128)S(1)}, u32[]{:S(2)}, u32[]{:S(2)}) collective-permute-start(f32[2,4,4,128]{3,2,1,0:T(4,128)} %param.11), channel_id=1, source_target_pairs={{0,8},{8,0},{16,24},{24,16},{1,9},{9,1},{17,25},{25,17},{2,10},{10... | collective-permute-start | bytes 49160 | tf_op jit(solution)/shard_map/ppermute | solution.py:419
  7.2 0.9 %copy-start = (f32[32,4,4,128]{3,2,1,0:T(4,128)S(1)}, f32[32,4,4,128]{3,2,1,0:T(4,128)}, u32[]{:S(2)}) copy-start(f32[32,4,4,128]{3,2,1,0:T(4,128)} %param.10) | copy-start | bytes 786436
  8.2 0.7 %copy-start.1 = (f32[2,4,4,128]{3,2,1,0:T(4,128)S(1)}, f32[2,4,4,128]{3,2,1,0:T(4,128)}, u32[]{:S(2)}) copy-start(f32[2,4,4,128]{3,2,1,0:T(4,128)} %param.11) | copy-start | bytes 49156
  8.9 8.8 %copy-start.7 = (f32[32,4,16]{0,2,1:T(8,128)S(1)}, f32[32,4,16]{0,2,1:T(8,128)}, u32[]{:S(2)}) copy-start(f32[32,4,16]{0,2,1:T(8,128)} %param.12) | copy-start | bytes 24580
  8.9 8.9 %copy-start.8 = (f32[32,4,16]{0,2,1:T(8,128)S(1)}, f32[32,4,16]{0,2,1:T(8,128)}, u32[]{:S(2)}) copy-start(f32[32,4,16]{0,2,1:T(8,128)} %param.14) | copy-start | bytes 24580
  8.9 8.9 %copy-start.9 = (s32[256,32]{0,1:T(8,128)S(1)}, s32[256,32]{0,1:T(8,128)}, u32[]{:S(2)}) copy-start(s32[256,32]{0,1:T(8,128)} %param.18) | copy-start | bytes 98308
  8.9 9.1 %copy-start.2 = (s32[4,4,16]{2,1,0:T(4,128)S(1)}, s32[4,4,16]{2,1,0:T(4,128)}, u32[]{:S(2)}) copy-start(s32[4,4,16]{2,1,0:T(4,128)} %active_ref.1) | copy-start | bytes 3076
  8.9 9.1 %copy-start.5 = (f32[256]{0:T(256)S(1)}, f32[256]{0:T(256)}, u32[]{:S(2)}) copy-start(f32[256]{0:T(256)} %param.17) | copy-start | bytes 3076
  11.8 16.0 %all-to-all-start = ((f32[8,64,128]{2,1,0:T(8,128)}), f32[8,64,128]{2,1,0:T(8,128)S(1)}, u32[]{:S(2)}, u32[]{:S(2)}) async-start(f32[8,64,128]{2,1,0:T(8,128)} %advect.1), calls=%async_computation | async-start | bytes 524288 | tf_op jit(solution)/shard_map/all_to_all | solution.py:449

commit v5 on v4

--- a/solution.py
+++ b/solution.py
@@ -88,7 +88,7 @@
     return courant, slope_weight(courant)
 
 
-def own_kernel(
+def own_rows(
     sizes, band_ref, wind_ref, f_out, zonal_out, merid_out, f_ref, slope_ref, flux_ref, flow_ref
 ):
     rows = sizes[2]
@@ -214,19 +214,37 @@
             ).T
 
 
-def paired(groups, levels, ref, place):
-    rows, width = ref.shape[1], ref.shape[2]
+def paired(groups, ref, place):
+    rows, width, all_levels = ref.shape
+    by_level = ref[...].reshape(rows * width, all_levels).T
+    levels = all_levels // groups
     for pair in range(groups // 2):
         for parity in range(2):
             start = (2 * pair + parity) * levels
-            for row in range(rows):
-                lane = (parity * rows + row) * width
-                place[pair * levels : (pair + 1) * levels, lane : lane + width] = ref[
-                    start : start + levels, row, :
-                ]
-
-
-def prepare_kernel(
+            lane = parity * rows * width
+            place[pair * levels : (pair + 1) * levels, lane : lane + rows * width] = by_level[
+                start : start + levels
+            ]
+
+
+def early_kernel(sizes, groups, *refs):
+    inputs, refs = refs[:10], refs[10:]
+    outputs, refs = refs[:8], refs[8:]
+    places, sems = refs[:10], refs[10]
+    own_scratch, prepare_scratch = refs[11:15], refs[15:]
+    copies = [
+        pltpu.make_async_copy(source, place, sems.at[i])
+        for i, (source, place) in enumerate(zip(inputs, places, strict=True))
+    ]
+    for copy in copies:
+        copy.start()
+    for copy in copies:
+        copy.wait()
+    own_rows(sizes, *places[:2], *outputs[:3], *own_scratch)
+    prepare(groups, *places[2:], *outputs[3:], *prepare_scratch)
+
+
+def prepare(
     groups,
     depth_ref,
     share_ref,
@@ -245,14 +263,14 @@
     kelvin_at,
     lower_at,
 ):
-    all_levels, rows, width = depth_ref.shape
+    rows, width, all_levels = depth_ref.shape
     levels = all_levels // groups
     half = LANES // 2
     odd = lax.broadcasted_iota(jnp.int32, (1, LANES), 1) >= half
-    reactions, species = yield_ref.shape
-
-    paired(groups, levels, kelvin_ref, kelvin_at)
-    paired(groups, levels, depth_ref, depth_at)
+    species, reactions = yield_ref.shape
+
+    paired(groups, kelvin_ref, kelvin_at)
+    paired(groups, depth_ref, depth_at)
     for parity in range(2):
         for row in range(rows):
             lane = (parity * rows + row) * width
@@ -301,9 +319,15 @@
     for which in range(2):
         hit = (one_species == pair_ref[which : which + 1, :]).astype(F32)
         pick_out[which * reactions : (which + 1) * reactions] = hit.T.astype(jnp.bfloat16)
-    yields = yield_ref[...].astype(F32).T.astype(jnp.bfloat16)
+    yields = yield_ref[...].astype(F32).astype(jnp.bfloat16)
     yield_out[:, :reactions] = yields
     yield_out[:, reactions:] = yields
+
+
+def in_two_parts(value):
+    high = value.astype(jnp.bfloat16)
+    low = (value - high.astype(F32)).astype(jnp.bfloat16)
+    return jnp.concatenate([high, low], axis=0)
 
 
 def column_kernel(
@@ -343,28 +367,31 @@
         crossed = jnp.where(odd, sums[0], sums[1])
         return kept + pltpu.roll(crossed, half, 1)
 
-    for first in range(0, pairs, tile_pairs):
-        tile = range(first, first + tile_pairs)
-        lanes = slice(first * LANES, (first + tile_pairs) * LANES)
-        q = jnp.concatenate([remapped(at) for at in tile], axis=1)
-        for substep in range(active_ref.shape[0]):
-            on = jnp.concatenate([active_ref[substep : substep + 1, :]] * tile_pairs, axis=1)
-            high = q.astype(jnp.bfloat16)
-            low = (q - high.astype(F32)).astype(jnp.bfloat16)
-            picked = jnp.dot(
-                pick_ref[...], jnp.concatenate([high, low], axis=0), preferred_element_type=F32
-            )
-            rates = rate_ref[:, lanes] * picked[:reactions] * picked[reactions:]
-            high = rates.astype(jnp.bfloat16)
-            low = (rates - high.astype(F32)).astype(jnp.bfloat16)
-            change = jnp.dot(
-                yield_ref[...], jnp.concatenate([high, low], axis=0), preferred_element_type=F32
-            )
-            q = jnp.where(on > 0, q + change, q)
-        for at in tile:
+    tiles = [range(first, first + tile_pairs) for first in range(0, pairs, tile_pairs)]
+    q = [jnp.concatenate([remapped(at) for at in tile], axis=1) for tile in tiles]
+    for substep in range(active_ref.shape[0]):
+        on = jnp.concatenate([active_ref[substep : substep + 1, :]] * tile_pairs, axis=1) > 0
+        picked = [
+            jnp.dot(pick_ref[...], in_two_parts(value), preferred_element_type=F32) for value in q
+        ]
+        rates = [
+            rate_ref[:, tile[0] * LANES : (tile[-1] + 1) * LANES]
+            * found[:reactions]
+            * found[reactions:]
+            for tile, found in zip(tiles, picked, strict=True)
+        ]
+        rates = [in_two_parts(value) for value in rates]
+        changes = [
+            jnp.dot(yield_ref[...], value, preferred_element_type=F32) for value in rates
+        ]
+        q = [
+            jnp.where(on, value + change, value) for value, change in zip(q, changes, strict=True)
+        ]
+    for tile, value in zip(tiles, q, strict=True):
+        for inside, at in enumerate(tile):
             pair, level = divmod(at, levels)
-            lane = (at - first) * LANES
-            target_ref[pair, pl.ds(level, species, levels), :] = q[:, lane : lane + LANES]
+            lane = inside * LANES
+            target_ref[pair, pl.ds(level, species, levels), :] = value[:, lane : lane + LANES]
 
     for pair in range(groups // 2):
         both = target_ref[pair].T
@@ -426,13 +453,42 @@
         return [jax.ShapeDtypeStruct(shape, F32) for shape in shapes]
 
     padded = lons + 2 * PAD
-    own = kernel_call(
-        functools.partial(own_kernel, sizes),
-        "own_rows",
-        arrays((rows, lons, mixed), (rows, 2, lons, mixed), (rows, lons, mixed)),
-        [(rows, padded, mixed)] * 4,
-        pl.CostEstimate(flops=10**7, bytes_accessed=2 * 10**6, transcendentals=0),
-    )(flat(species_fractions), flat(cell_flow_ratios))
+    pairs = all_levels // 2
+    operands = (
+        flat(species_fractions),
+        flat(cell_flow_ratios),
+        layer_pressure_depth.transpose(1, 2, 0),
+        layer_thickness_fraction[None],
+        cell_kelvin_field.transpose(1, 2, 0),
+        daytime_indicator,
+        kinetic_factor_times_step[None],
+        arrhenius_barrier[None],
+        species_yield_matrix.T,
+        reagent_pairs,
+    )
+    early = pl.pallas_call(
+        functools.partial(early_kernel, sizes, blocks),
+        out_shape=[
+            *arrays((rows, lons, mixed), (rows, 2, lons, mixed), (rows, lons, mixed)),
+            *arrays((all_levels, pairs, LANES), (reactions, pairs * LANES)),
+            jax.ShapeDtypeStruct((substeps, LANES), jnp.int32),
+            jax.ShapeDtypeStruct((2 * reactions, 2 * species), jnp.bfloat16),
+            jax.ShapeDtypeStruct((species, 2 * reactions), jnp.bfloat16),
+        ],
+        in_specs=[pl.BlockSpec(memory_space=pltpu.HBM)] * len(operands),
+        scratch_shapes=[
+            *[pltpu.VMEM(item.shape, item.dtype) for item in operands],
+            pltpu.SemaphoreType.DMA((len(operands),)),
+            *[pltpu.VMEM((rows, padded, mixed), F32)] * 4,
+            *[pltpu.VMEM((pairs, LANES), F32)] * 3,
+        ],
+        compiler_params=PARAMS,
+        cost_estimate=pl.CostEstimate(
+            flops=10**7, bytes_accessed=7 * 10**6, transcendentals=10**6
+        ),
+        name="early",
+    )(*[pltpu.with_memory_space_constraint(item, pltpu.HBM) for item in operands])
+    own, prepared = early[:3], early[3:]
 
     packed = kernel_call(
         functools.partial(advect_kernel, sizes),
@@ -448,30 +504,8 @@
     )(*own, flat(core_band), flat(chip_band), flat(core_wind), flat(chip_wind))
     moved = lax.all_to_all(packed, "lev", split_axis=0, concat_axis=0, tiled=True)
 
-    pairs = all_levels // 2
-    prepared = kernel_call(
-        functools.partial(prepare_kernel, blocks),
-        "prepare",
-        [
-            *arrays((all_levels, pairs, LANES), (reactions, pairs * LANES)),
-            jax.ShapeDtypeStruct((substeps, LANES), jnp.int32),
-            jax.ShapeDtypeStruct((2 * reactions, 2 * species), jnp.bfloat16),
-            jax.ShapeDtypeStruct((species, 2 * reactions), jnp.bfloat16),
-        ],
-        [(pairs, LANES)] * 3,
-        pl.CostEstimate(flops=10**7, bytes_accessed=5 * 10**6, transcendentals=10**6),
-    )(
-        layer_pressure_depth,
-        layer_thickness_fraction[None],
-        cell_kelvin_field,
-        daytime_indicator,
-        kinetic_factor_times_step[None],
-        arrhenius_barrier[None],
-        species_yield_matrix,
-        reagent_pairs,
-    )
     reacted = kernel_call(
-        functools.partial(column_kernel, (blocks, levels, species, pairs // 2)),
+        functools.partial(column_kernel, (blocks, levels, species, pairs // 4)),
         "columns",
         arrays(packed.shape)[0],
         [(blocks // 2, mixed, LANES)] * 2,

time: 46.5 us -> 45.3 us (0.974)
  blocking collectives: 12.6 us -> 28.6 us
  waiting for transfers between devices: 9.19 us -> 0.01 us
  starting transfers between devices: 13 us -> 7.04 us
  local copies, waits for them, and re-layouts: 1.96 us -> 0 us
    all_to_all x0 -> x1, blocking collectives: none -> 15.9 us  [body(): lax.all_to_all(packed, 'lev', split_axis=0, concat_axis=0, tiled=True)]
    all_to_all x1 -> x0, waiting for transfers between devices: 9.18 us -> none  [body(): lax.all_to_all(packed, 'lev', split_axis=0, concat_axis=0, tiled=True)]
    all_to_all x1 -> x0, starting transfers between devices: 5.81 us -> none  [body(): lax.all_to_all(packed, 'lev', split_axis=0, concat_axis=0, tiled=True)]
    unnamed x23 -> x0, local copies, waits for them, and re-layouts: 1.96 us -> none
    pallas_call x2 -> x1, Pallas kernels: 1.05 us -> 1.99 us  [body(): pl.pallas_call(functools.partial(early_kernel, sizes, blocks), out_shape=...]
    pallas_call x1, Pallas kernels: 2.48 us -> 1.72 us  [body(): kernel_call(functools.partial(advect_kernel, sizes), 'advect', arrays((bl...]
  transfers between devices with their start and end apart: 5 -> 4, of which waited for: 1 -> 0; matrix products, arithmetic and copies ran while one was open for 1% -> 0% of each run, Pallas kernels for 2% -> 4%
where the time goes in v5:
time: 45.3 us; the launch traced here: 45.1 us
  blocking collectives  28.6 us (63%)
  Pallas kernels  9.39 us (21%)
  starting transfers between devices  7.04 us (16%)
    all_to_all x1, blocking collectives, body(): lax.all_to_all(packed, 'lev', split_axis=0, concat_axis=0, tiled=True)  15.9 us
    all_to_all x1, blocking collectives, body(): lax.all_to_all(reacted, 'lev', split_axis=0, concat_axis=0, tiled=True)  12.7 us
    pallas_call x1, Pallas kernels, body(): kernel_call(functools.partial(column_kernel, (blocks, levels, species, pa...  4.84 us
    ppermute x1, starting transfers between devices, body(): core_band = lax.ppermute(species_fractions, 'lat', by_core)  4.38 us
    pallas_call x1, Pallas kernels, body(): pl.pallas_call(functools.partial(early_kernel, sizes, blocks), out_shape=...  1.99 us
    pallas_call x1, Pallas kernels, body(): kernel_call(functools.partial(advect_kernel, sizes), 'advect', arrays((bl...  1.72 us
    ppermute x1, starting transfers between devices, body(): core_wind = lax.ppermute(cell_flow_ratios, 'lat', by_core)  1.35 us
  transfers between devices with their start and end apart: 4, of which 0 were waited for; matrix products, arithmetic and copies ran while one was open for 0% of the time, Pallas kernels for 4%

profile of v5, /device:TPU:0, one launch (start us, length us, event | category | flops | bytes accessed | tf_op | source)
XLA Modules:
  0.0 45.1 jit_solution(16754526765523263961)
XLA Ops:
  0.0 0.7 %collective-permute-start.1 = (f32[32,4,4,128]{3,2,1,0:T(4,128)}, f32[32,4,4,128]{3,2,1,0:T(4,128)S(1)}, u32[]{:S(2)}, u32[]{:S(2)}) collective-permute-start(f32[32,4,4,128]{3,2,1,0:T(4,128)} %param.10), channel_id=1, source_target_pairs={{8,16},{16,8},{9,17},{17,9},{10,18},{18,10},{11,19},{19,11},{12,20... | collective-permute-start | bytes 786440 | tf_op jit(solution)/shard_map/ppermute | solution.py:445
  0.7 4.4 %collective-permute-start = (f32[32,4,4,128]{3,2,1,0:T(4,128)}, f32[32,4,4,128]{3,2,1,0:T(4,128)S(1)}, u32[]{:S(2)}, u32[]{:S(2)}) collective-permute-start(f32[32,4,4,128]{3,2,1,0:T(4,128)} %param.10), channel_id=1, source_target_pairs={{0,8},{8,0},{16,24},{24,16},{1,9},{9,1},{17,25},{25,17},{2,10},{10... | collective-permute-start | bytes 786440 | tf_op jit(solution)/shard_map/ppermute | solution.py:444
  5.1 0.7 %collective-permute-start.3 = (f32[2,4,4,128]{3,2,1,0:T(4,128)}, f32[2,4,4,128]{3,2,1,0:T(4,128)S(1)}, u32[]{:S(2)}, u32[]{:S(2)}) collective-permute-start(f32[2,4,4,128]{3,2,1,0:T(4,128)} %param.11), channel_id=1, source_target_pairs={{8,16},{16,8},{9,17},{17,9},{10,18},{18,10},{11,19},{19,11},{12,20... | collective-permute-start | bytes 49160 | tf_op jit(solution)/shard_map/ppermute | solution.py:447
  5.7 1.3 %collective-permute-start.2 = (f32[2,4,4,128]{3,2,1,0:T(4,128)}, f32[2,4,4,128]{3,2,1,0:T(4,128)S(1)}, u32[]{:S(2)}, u32[]{:S(2)}) collective-permute-start(f32[2,4,4,128]{3,2,1,0:T(4,128)} %param.11), channel_id=1, source_target_pairs={{0,8},{8,0},{16,24},{24,16},{1,9},{9,1},{17,25},{25,17},{2,10},{10... | collective-permute-start | bytes 49160 | tf_op jit(solution)/shard_map/ppermute | solution.py:446
  7.1 2.0 %early.1 = (f32[4,128,128]{2,1,0:T(8,128)S(1)}, f32[4,2,128,128]{3,2,1,0:T(8,128)S(1)}, f32[4,128,128]{2,1,0:T(8,128)S(1)}, f32[32,16,128]{2,1,0:T(8,128)S(1)}, ...) custom-call(f32[512,128]{1,0:T(8,128)} %bitcast.17, ...), custom_call_target="tpu_custom_call" | custom-call | flops 10000000 | bytes 7000000 | tf_op jit(solution)/shard_map/early/pallas_call | solution.py:469
  9.1 0.0 collective-permute-done.3
  9.1 0.0 collective-permute-done.2
  9.1 0.0 collective-permute-done.1
  9.1 0.0 collective-permute-done
  9.1 1.7 %advect.1 = f32[8,64,128]{2,1,0:T(8,128)S(1)} custom-call(f32[4,128,128]{2,1,0:T(8,128)S(1)} %get-tuple-element.13.own_ref, f32[4,2,128,128]{3,2,1,0:T(8,128)S(1)} %get-tuple-element.14.own_zonal, f32[4,128,128]{2,1,0:T(8,128)S(1)} %get-tuple-element.15.own_merid, f32[512,128]{1,0:T(8,128)S(1)} %bitcast.14, f32[512,128]{1,0:T(8,128)S(1)} %bitcast.13, ...), custom_call_target="tpu_custom_call" | custom-call | tf_op jit(solution)/shard_map/advect/pallas_call | solution.py:493
  10.8 15.9 %all_to_all.10.moved_ref = f32[8,64,128]{2,1,0:T(8,128)S(1)} all-to-all(f32[8,64,128]{2,1,0:T(8,128)S(1)} %advect.1), channel_id=1, replica_groups=mesh['lat'=4,'lev'=8] {'lev'}, dimensions={0} | all-to-all | bytes 524288 | tf_op jit(solution)/shard_map/all_to_all | solution.py:505
  26.7 4.8 %columns.1 = f32[8,64,128]{2,1,0:T(8,128)S(1)} custom-call(f32[8,64,128]{2,1,0:T(8,128)S(1)} %all_to_all.10.moved_ref, f32[32,16,128]{2,1,0:T(8,128)S(1)} %get-tuple-element.16.overlap_ref, f32[256,2048]{1,0:T(8,128)S(1)} %get-tuple-element.17.rate_ref, s32[4,128]{1,0:T(4,128)S(1)} %get-tuple-element.18.active_ref, ...), custom_call_target="tpu_custom_call" | custom-call | tf_op jit(solution)/shard_map/columns/pallas_call | solution.py:507
  31.6 12.7 %all_to_all.11.in_ref = f32[8,64,128]{2,1,0:T(8,128)S(1)} all-to-all(f32[8,64,128]{2,1,0:T(8,128)S(1)} %columns.1), channel_id=1, replica_groups=mesh['lat'=4,'lev'=8] {'lev'}, dimensions={0} | all-to-all | bytes 524288 | tf_op jit(solution)/shard_map/all_to_all | solution.py:513
  44.2 0.8 %spread.1 = f32[512,128]{1,0:T(8,128)} custom-call(f32[8,64,128]{2,1,0:T(8,128)S(1)} %all_to_all.11.in_ref), custom_call_target="tpu_custom_call" | custom-call | tf_op jit(solution)/shard_map/spread/pallas_call | solution.py:514
Async XLA Ops:
  0.0 9.1 %collective-permute-start.1 = (f32[32,4,4,128]{3,2,1,0:T(4,128)}, f32[32,4,4,128]{3,2,1,0:T(4,128)S(1)}, u32[]{:S(2)}, u32[]{:S(2)}) collective-permute-start(f32[32,4,4,128]{3,2,1,0:T(4,128)} %param.10), channel_id=1, source_target_pairs={{8,16},{16,8},{9,17},{17,9},{10,18},{18,10},{11,19},{19,11},{12,20... | collective-permute-start | bytes 786440 | tf_op jit(solution)/shard_map/ppermute | solution.py:445
  0.7 8.4 %collective-permute-start = (f32[32,4,4,128]{3,2,1,0:T(4,128)}, f32[32,4,4,128]{3,2,1,0:T(4,128)S(1)}, u32[]{:S(2)}, u32[]{:S(2)}) collective-permute-start(f32[32,4,4,128]{3,2,1,0:T(4,128)} %param.10), channel_id=1, source_target_pairs={{0,8},{8,0},{16,24},{24,16},{1,9},{9,1},{17,25},{25,17},{2,10},{10... | collective-permute-start | bytes 786440 | tf_op jit(solution)/shard_map/ppermute | solution.py:444
  5.1 4.0 %collective-permute-start.3 = (f32[2,4,4,128]{3,2,1,0:T(4,128)}, f32[2,4,4,128]{3,2,1,0:T(4,128)S(1)}, u32[]{:S(2)}, u32[]{:S(2)}) collective-permute-start(f32[2,4,4,128]{3,2,1,0:T(4,128)} %param.11), channel_id=1, source_target_pairs={{8,16},{16,8},{9,17},{17,9},{10,18},{18,10},{11,19},{19,11},{12,20... | collective-permute-start | bytes 49160 | tf_op jit(solution)/shard_map/ppermute | solution.py:447
  5.7 3.4 %collective-permute-start.2 = (f32[2,4,4,128]{3,2,1,0:T(4,128)}, f32[2,4,4,128]{3,2,1,0:T(4,128)S(1)}, u32[]{:S(2)}, u32[]{:S(2)}) collective-permute-start(f32[2,4,4,128]{3,2,1,0:T(4,128)} %param.11), channel_id=1, source_target_pairs={{0,8},{8,0},{16,24},{24,16},{1,9},{9,1},{17,25},{25,17},{2,10},{10... | collective-permute-start | bytes 49160 | tf_op jit(solution)/shard_map/ppermute | solution.py:446

commit v6 on v5

--- a/solution.py
+++ b/solution.py
@@ -67,11 +67,11 @@
     ]
 
 
-def flow_rows(sizes, ref, which, row):
+def flow_rows(sizes, ref, which, row, skip=0):
     species, levels, rows, parts, _ = sizes
     found = []
     for k in range(parts):
-        start = (which * levels * rows + row) * parts + k
+        start = ((skip + which) * levels * rows + row) * parts + k
         level_rows = ref[pl.ds(start, levels, rows * parts), :]
         tile = jnp.concatenate([level_rows] * (8 // levels), axis=0)
         found.append(jnp.concatenate([tile] * (species * levels // 8), axis=0))
@@ -89,16 +89,16 @@
 
 
 def own_rows(
-    sizes, band_ref, wind_ref, f_out, zonal_out, merid_out, f_ref, slope_ref, flux_ref, flow_ref
+    sizes, sent_ref, f_out, zonal_out, merid_out, f_ref, slope_ref, flux_ref, flow_ref
 ):
-    rows = sizes[2]
+    species, rows = sizes[0], sizes[2]
     for row in range(rows):
         courant, weight = zonal_weights(
-            flow_ref, row, turned(flow_rows(sizes, wind_ref, 0, row))
+            flow_ref, row, turned(flow_rows(sizes, sent_ref, 0, row, species))
         )
         zonal_out[row, 0], zonal_out[row, 1] = courant, weight
-        merid_out[row] = turned(flow_rows(sizes, wind_ref, 1, row))
-        put_cyclic(f_ref, row, turned(tracer_rows(sizes, band_ref, row)))
+        merid_out[row] = turned(flow_rows(sizes, sent_ref, 1, row, species))
+        put_cyclic(f_ref, row, turned(tracer_rows(sizes, sent_ref, row)))
         f_out[row] = lon_step(f_ref, slope_ref, flux_ref, row, courant, weight)
 
 
@@ -109,8 +109,6 @@
     own_merid,
     core_ref,
     chip_ref,
-    core_wind,
-    chip_wind,
     out_ref,
     f_ref,
     slope_ref,
@@ -133,10 +131,10 @@
 
     for row in range(rows):
         zonal = both_sides(
-            flow_rows(sizes, core_wind, 0, row), flow_rows(sizes, chip_wind, 0, row)
+            flow_rows(sizes, core_ref, 0, row, species), flow_rows(sizes, chip_ref, 0, row, species)
         )
         merid = both_sides(
-            flow_rows(sizes, core_wind, 1, row), flow_rows(sizes, chip_wind, 1, row)
+            flow_rows(sizes, core_ref, 1, row, species), flow_rows(sizes, chip_ref, 1, row, species)
         )
         tracer = both_sides(
             tracer_rows(sizes, core_ref, row), tracer_rows(sizes, chip_ref, row)
@@ -227,21 +225,33 @@
             ]
 
 
+def pack_kernel(tracer_ref, wind_ref, out_ref, sems):
+    size = tracer_ref.shape[0]
+    copies = [
+        pltpu.make_async_copy(tracer_ref, out_ref.at[:size], sems.at[0]),
+        pltpu.make_async_copy(wind_ref, out_ref.at[size:], sems.at[1]),
+    ]
+    for copy in copies:
+        copy.start()
+    for copy in copies:
+        copy.wait()
+
+
 def early_kernel(sizes, groups, *refs):
-    inputs, refs = refs[:10], refs[10:]
+    sent_ref, inputs, refs = refs[0], refs[1:9], refs[9:]
     outputs, refs = refs[:8], refs[8:]
-    places, sems = refs[:10], refs[10]
-    own_scratch, prepare_scratch = refs[11:15], refs[15:]
+    places, sems = refs[:8], refs[8]
+    own_scratch, prepare_scratch = refs[9:13], refs[13:]
     copies = [
         pltpu.make_async_copy(source, place, sems.at[i])
         for i, (source, place) in enumerate(zip(inputs, places, strict=True))
     ]
     for copy in copies:
         copy.start()
+    own_rows(sizes, sent_ref, *outputs[:3], *own_scratch)
     for copy in copies:
         copy.wait()
-    own_rows(sizes, *places[:2], *outputs[:3], *own_scratch)
-    prepare(groups, *places[2:], *outputs[3:], *prepare_scratch)
+    prepare(groups, *places, *outputs[3:], *prepare_scratch)
 
 
 def prepare(
@@ -441,13 +451,23 @@
     mixed = species * levels
 
     by_core, by_chip = swap_pairs(bands, 0), swap_pairs(bands, 1)
-    core_band = lax.ppermute(species_fractions, "lat", by_core)
-    chip_band = lax.ppermute(species_fractions, "lat", by_chip)
-    core_wind = lax.ppermute(cell_flow_ratios, "lat", by_core)
-    chip_wind = lax.ppermute(cell_flow_ratios, "lat", by_chip)
-
     def flat(value):
         return value.reshape(-1, LANES)
+
+    def in_hbm(*values):
+        return [pltpu.with_memory_space_constraint(item, pltpu.HBM) for item in values]
+
+    tracers, winds = flat(species_fractions), flat(cell_flow_ratios)
+    sent = pl.pallas_call(
+        pack_kernel,
+        out_shape=jax.ShapeDtypeStruct((len(tracers) + len(winds), LANES), F32),
+        in_specs=[pl.BlockSpec(memory_space=pltpu.HBM)] * 2,
+        scratch_shapes=[pltpu.SemaphoreType.DMA((2,))],
+        compiler_params=PARAMS,
+        name="pack",
+    )(*in_hbm(tracers, winds))
+    core_band = lax.ppermute(sent, "lat", by_core)
+    chip_band = lax.ppermute(sent, "lat", by_chip)
 
     def arrays(*shapes):
         return [jax.ShapeDtypeStruct(shape, F32) for shape in shapes]
@@ -455,8 +475,6 @@
     padded = lons + 2 * PAD
     pairs = all_levels // 2
     operands = (
-        flat(species_fractions),
-        flat(cell_flow_ratios),
         layer_pressure_depth.transpose(1, 2, 0),
         layer_thickness_fraction[None],
         cell_kelvin_field.transpose(1, 2, 0),
@@ -475,7 +493,8 @@
             jax.ShapeDtypeStruct((2 * reactions, 2 * species), jnp.bfloat16),
             jax.ShapeDtypeStruct((species, 2 * reactions), jnp.bfloat16),
         ],
-        in_specs=[pl.BlockSpec(memory_space=pltpu.HBM)] * len(operands),
+        in_specs=[pl.BlockSpec(memory_space=pltpu.VMEM)]
+        + [pl.BlockSpec(memory_space=pltpu.HBM)] * len(operands),
         scratch_shapes=[
             *[pltpu.VMEM(item.shape, item.dtype) for item in operands],
             pltpu.SemaphoreType.DMA((len(operands),)),
@@ -487,7 +506,7 @@
             flops=10**7, bytes_accessed=7 * 10**6, transcendentals=10**6
         ),
         name="early",
-    )(*[pltpu.with_memory_space_constraint(item, pltpu.HBM) for item in operands])
+    )(sent, *in_hbm(*operands))
     own, prepared = early[:3], early[3:]
 
     packed = kernel_call(
@@ -501,7 +520,7 @@
             (rows + 1, 2, lons, mixed),
             (2 * rows, padded, mixed),
         ],
-    )(*own, flat(core_band), flat(chip_band), flat(core_wind), flat(chip_wind))
+    )(*own, core_band, chip_band)
     moved = lax.all_to_all(packed, "lev", split_axis=0, concat_axis=0, tiled=True)
 
     reacted = kernel_call(

time: 45.3 us -> 43.7 us (0.965)
  starting transfers between devices: 7.04 us -> 5.06 us
  Pallas kernels: 9.39 us -> 10.1 us
    ppermute x4 -> x2, starting transfers between devices: 7.04 us -> 5.06 us  [the longest x1 4.38 us: body(): core_band = lax.ppermute(sent, 'lat', by_core)]
    all_to_all x1, blocking collectives: 15.9 us -> 14.4 us  [body(): lax.all_to_all(packed, 'lev', split_axis=0, concat_axis=0, tiled=True)]
    all_to_all x1, blocking collectives: 12.7 us -> 13.8 us  [body(): lax.all_to_all(reacted, 'lev', split_axis=0, concat_axis=0, tiled=True)]
    pallas_call x0 -> x1, Pallas kernels: none -> 0.97 us  [body(): pl.pallas_call(pack_kernel, out_shape=jax.ShapeDtypeStruct((len(tracers)...]
  transfers between devices with their start and end apart: 4 -> 2, of which waited for: 0 -> 0; matrix products, arithmetic and copies ran while one was open for 0% -> 0% of each run, Pallas kernels for 4% -> 4%
where the time goes in v6:
time: 43.7 us; the launch traced here: 43.4 us
  blocking collectives  28.2 us (65%)
  Pallas kernels  10.1 us (23%)
  starting transfers between devices  5.06 us (12%)
    all_to_all x1, blocking collectives, body(): lax.all_to_all(packed, 'lev', split_axis=0, concat_axis=0, tiled=True)  14.4 us
    all_to_all x1, blocking collectives, body(): lax.all_to_all(reacted, 'lev', split_axis=0, concat_axis=0, tiled=True)  13.8 us
    pallas_call x1, Pallas kernels, body(): kernel_call(functools.partial(column_kernel, (blocks, levels, species, pa...  4.84 us
    ppermute x1, starting transfers between devices, body(): core_band = lax.ppermute(sent, 'lat', by_core)  4.38 us
    pallas_call x1, Pallas kernels, body(): pl.pallas_call(functools.partial(early_kernel, sizes, blocks), out_shape=...  1.72 us
    pallas_call x1, Pallas kernels, body(): kernel_call(functools.partial(advect_kernel, sizes), 'advect', arrays((bl...  1.71 us
    pallas_call x1, Pallas kernels, body(): pl.pallas_call(pack_kernel, out_shape=jax.ShapeDtypeStruct((len(tracers)...  0.97 us
  transfers between devices with their start and end apart: 2, of which 0 were waited for; matrix products, arithmetic and copies ran while one was open for 0% of the time, Pallas kernels for 4%

profile of v6, /device:TPU:0, one launch (start us, length us, event | category | flops | bytes accessed | tf_op | source)
XLA Modules:
  0.0 43.4 jit_solution(10314235423282617996)
XLA Ops:
  0.0 1.0 %pack.1.refs_0_ = f32[544,128]{1,0:T(8,128)S(1)} custom-call(f32[512,128]{1,0:T(8,128)} %bitcast.9, f32[32,128]{1,0:T(8,128)} %bitcast.10), custom_call_target="tpu_custom_call" | custom-call | tf_op jit(solution)/shard_map/pack/pallas_call | solution.py:461
  1.0 0.7 %collective-permute-start.1 = (f32[544,128]{1,0:T(8,128)S(1)}, f32[544,128]{1,0:T(8,128)S(1)}, u32[]{:S(2)}, u32[]{:S(2)}) collective-permute-start(f32[544,128]{1,0:T(8,128)S(1)} %pack.1.refs_0_), channel_id=1, source_target_pairs={{8,16},{16,8},{9,17},{17,9},{10,18},{18,10},{11,19},{19,11},{12,20... | collective-permute-start | bytes 835592 | tf_op jit(solution)/shard_map/ppermute | solution.py:470
  1.7 4.4 %collective-permute-start = (f32[544,128]{1,0:T(8,128)S(1)}, f32[544,128]{1,0:T(8,128)S(1)}, u32[]{:S(2)}, u32[]{:S(2)}) collective-permute-start(f32[544,128]{1,0:T(8,128)S(1)} %pack.1.refs_0_), channel_id=1, source_target_pairs={{0,8},{8,0},{16,24},{24,16},{1,9},{9,1},{17,25},{25,17},{2,10},{10... | collective-permute-start | bytes 835592 | tf_op jit(solution)/shard_map/ppermute | solution.py:469
  6.0 1.7 %early.1 = (f32[4,128,128]{2,1,0:T(8,128)S(1)}, f32[4,2,128,128]{3,2,1,0:T(8,128)S(1)}, f32[4,128,128]{2,1,0:T(8,128)S(1)}, f32[32,16,128]{2,1,0:T(8,128)S(1)}, ...) custom-call(f32[544,128]{1,0:T(8,128)S(1)} %pack.1.refs_0_, ...), custom_call_target="tpu_custom_call" | custom-call | flops 10000000 | bytes 7000000 | tf_op jit(solution)/shard_map/early/pallas_call | solution.py:487
  7.8 0.0 collective-permute-done.1.chip_ref
  7.8 0.0 collective-permute-done.core_ref
  7.8 1.7 %advect.1 = f32[8,64,128]{2,1,0:T(8,128)S(1)} custom-call(f32[4,128,128]{2,1,0:T(8,128)S(1)} %get-tuple-element.13.own_ref, f32[4,2,128,128]{3,2,1,0:T(8,128)S(1)} %get-tuple-element.14.own_zonal, f32[4,128,128]{2,1,0:T(8,128)S(1)} %get-tuple-element.15.own_merid, f32[544,128]{1,0:T(8,128)S(1)} %collective-permute-done.core_ref, ...), custom_call_target="tpu_custom_call" | custom-call | tf_op jit(solution)/shard_map/advect/pallas_call | solution.py:512
  9.5 14.4 %all_to_all.10.moved_ref = f32[8,64,128]{2,1,0:T(8,128)S(1)} all-to-all(f32[8,64,128]{2,1,0:T(8,128)S(1)} %advect.1), channel_id=1, replica_groups=mesh['lat'=4,'lev'=8] {'lev'}, dimensions={0} | all-to-all | bytes 524288 | tf_op jit(solution)/shard_map/all_to_all | solution.py:524
  23.9 4.8 %columns.1 = f32[8,64,128]{2,1,0:T(8,128)S(1)} custom-call(f32[8,64,128]{2,1,0:T(8,128)S(1)} %all_to_all.10.moved_ref, f32[32,16,128]{2,1,0:T(8,128)S(1)} %get-tuple-element.16.overlap_ref, f32[256,2048]{1,0:T(8,128)S(1)} %get-tuple-element.17.rate_ref, s32[4,128]{1,0:T(4,128)S(1)} %get-tuple-element.18.active_ref, ...), custom_call_target="tpu_custom_call" | custom-call | tf_op jit(solution)/shard_map/columns/pallas_call | solution.py:526
  28.8 13.8 %all_to_all.11.in_ref = f32[8,64,128]{2,1,0:T(8,128)S(1)} all-to-all(f32[8,64,128]{2,1,0:T(8,128)S(1)} %columns.1), channel_id=1, replica_groups=mesh['lat'=4,'lev'=8] {'lev'}, dimensions={0} | all-to-all | bytes 524288 | tf_op jit(solution)/shard_map/all_to_all | solution.py:532
  42.6 0.8 %spread.1 = f32[512,128]{1,0:T(8,128)} custom-call(f32[8,64,128]{2,1,0:T(8,128)S(1)} %all_to_all.11.in_ref), custom_call_target="tpu_custom_call" | custom-call | tf_op jit(solution)/shard_map/spread/pallas_call | solution.py:533
Async XLA Ops:
  1.0 6.8 %collective-permute-start.1 = (f32[544,128]{1,0:T(8,128)S(1)}, f32[544,128]{1,0:T(8,128)S(1)}, u32[]{:S(2)}, u32[]{:S(2)}) collective-permute-start(f32[544,128]{1,0:T(8,128)S(1)} %pack.1.refs_0_), channel_id=1, source_target_pairs={{8,16},{16,8},{9,17},{17,9},{10,18},{18,10},{11,19},{19,11},{12,20... | collective-permute-start | bytes 835592 | tf_op jit(solution)/shard_map/ppermute | solution.py:470
  1.7 6.1 %collective-permute-start = (f32[544,128]{1,0:T(8,128)S(1)}, f32[544,128]{1,0:T(8,128)S(1)}, u32[]{:S(2)}, u32[]{:S(2)}) collective-permute-start(f32[544,128]{1,0:T(8,128)S(1)} %pack.1.refs_0_), channel_id=1, source_target_pairs={{0,8},{8,0},{16,24},{24,16},{1,9},{9,1},{17,25},{25,17},{2,10},{10... | collective-permute-start | bytes 835592 | tf_op jit(solution)/shard_map/ppermute | solution.py:469

commit v7 on v6

--- a/solution.py
+++ b/solution.py
@@ -107,8 +107,8 @@
     own_ref,
     own_zonal,
     own_merid,
+    chip_ref,
     core_ref,
-    chip_ref,
     out_ref,
     f_ref,
     slope_ref,
@@ -520,7 +520,7 @@
             (rows + 1, 2, lons, mixed),
             (2 * rows, padded, mixed),
         ],
-    )(*own, core_band, chip_band)
+    )(*own, chip_band, core_band)
     moved = lax.all_to_all(packed, "lev", split_axis=0, concat_axis=0, tiled=True)
 
     reacted = kernel_call(

time: 43.7 us -> 41.4 us (0.947)
  the two profiles are of different devices: /device:TPU:0 before, /device:TPU:4 now
where the time goes in v7:
time: 41.4 us; the launch traced here: 41.1 us
  blocking collectives  24.7 us (60%)
  Pallas kernels  10.1 us (24%)
  waiting for transfers between devices  4.2 us (10%)
  starting transfers between devices  1.99 us (5%)
    all_to_all x1, blocking collectives, body(): lax.all_to_all(packed, 'lev', split_axis=0, concat_axis=0, tiled=True)  13.8 us
    all_to_all x1, blocking collectives, body(): lax.all_to_all(reacted, 'lev', split_axis=0, concat_axis=0, tiled=True)  10.9 us
    pallas_call x1, Pallas kernels, body(): kernel_call(functools.partial(column_kernel, (blocks, levels, species, pa...  4.84 us
    ppermute x1, waiting for transfers between devices, body(): chip_band = lax.ppermute(sent, 'lat', by_chip)  4.19 us
    ppermute x1, starting transfers between devices, body(): chip_band = lax.ppermute(sent, 'lat', by_chip)  1.92 us
    pallas_call x1, Pallas kernels, body(): pl.pallas_call(functools.partial(early_kernel, sizes, blocks), out_shape=...  1.73 us
    pallas_call x1, Pallas kernels, body(): kernel_call(functools.partial(advect_kernel, sizes), 'advect', arrays((bl...  1.71 us
    pallas_call x1, Pallas kernels, body(): pl.pallas_call(pack_kernel, out_shape=jax.ShapeDtypeStruct((len(tracers)...  0.97 us
  transfers between devices with their start and end apart: 2, of which 1 were waited for; matrix products, arithmetic and copies ran while one was open for 0% of the time, Pallas kernels for 4%

profile of v7, /device:TPU:4, one launch (start us, length us, event | category | flops | bytes accessed | tf_op | source)
XLA Modules:
  0.0 41.1 jit_solution(15343214675546205436)
XLA Ops:
  0.0 1.0 %pack.1.refs_0_ = f32[544,128]{1,0:T(8,128)S(1)} custom-call(f32[512,128]{1,0:T(8,128)} %bitcast.9, f32[32,128]{1,0:T(8,128)} %bitcast.10), custom_call_target="tpu_custom_call" | custom-call | tf_op jit(solution)/shard_map/pack/pallas_call | solution.py:461
  1.0 0.1 collective-permute-start.1
  1.1 1.9 %collective-permute-start = (f32[544,128]{1,0:T(8,128)S(1)}, f32[544,128]{1,0:T(8,128)S(1)}, u32[]{:S(2)}, u32[]{:S(2)}) collective-permute-start(f32[544,128]{1,0:T(8,128)S(1)} %pack.1.refs_0_), channel_id=1, source_target_pairs={{8,16},{16,8},{9,17},{17,9},{10,18},{18,10},{11,19},{19,11},{12,20... | collective-permute-start | bytes 835592 | tf_op jit(solution)/shard_map/ppermute | solution.py:470
  3.0 1.7 %early.1 = (f32[4,128,128]{2,1,0:T(8,128)S(1)}, f32[4,2,128,128]{3,2,1,0:T(8,128)S(1)}, f32[4,128,128]{2,1,0:T(8,128)S(1)}, f32[32,16,128]{2,1,0:T(8,128)S(1)}, ...) custom-call(f32[544,128]{1,0:T(8,128)S(1)} %pack.1.refs_0_, ...), custom_call_target="tpu_custom_call" | custom-call | flops 10000000 | bytes 7000000 | tf_op jit(solution)/shard_map/early/pallas_call | solution.py:487
  4.7 0.0 collective-permute-done.1.core_ref
  4.7 4.2 %collective-permute-done.chip_ref = f32[544,128]{1,0:T(8,128)S(1)} collective-permute-done((f32[544,128]{1,0:T(8,128)S(1)}, f32[544,128]{1,0:T(8,128)S(1)}, u32[]{:S(2)}, u32[]{:S(2)}) %collective-permute-start) | collective-permute-done | bytes 278560 | tf_op jit(solution)/shard_map/ppermute | solution.py:470
  8.9 1.7 %advect.1 = f32[8,64,128]{2,1,0:T(8,128)S(1)} custom-call(f32[4,128,128]{2,1,0:T(8,128)S(1)} %get-tuple-element.13.own_ref, f32[4,2,128,128]{3,2,1,0:T(8,128)S(1)} %get-tuple-element.14.own_zonal, f32[4,128,128]{2,1,0:T(8,128)S(1)} %get-tuple-element.15.own_merid, f32[544,128]{1,0:T(8,128)S(1)} %collective-permute-done.chip_ref, ...), custom_call_target="tpu_custom_call" | custom-call | tf_op jit(solution)/shard_map/advect/pallas_call | solution.py:512
  10.6 13.8 %all_to_all.10.moved_ref = f32[8,64,128]{2,1,0:T(8,128)S(1)} all-to-all(f32[8,64,128]{2,1,0:T(8,128)S(1)} %advect.1), channel_id=1, replica_groups=mesh['lat'=4,'lev'=8] {'lev'}, dimensions={0} | all-to-all | bytes 524288 | tf_op jit(solution)/shard_map/all_to_all | solution.py:524
  24.5 4.8 %columns.1 = f32[8,64,128]{2,1,0:T(8,128)S(1)} custom-call(f32[8,64,128]{2,1,0:T(8,128)S(1)} %all_to_all.10.moved_ref, f32[32,16,128]{2,1,0:T(8,128)S(1)} %get-tuple-element.16.overlap_ref, f32[256,2048]{1,0:T(8,128)S(1)} %get-tuple-element.17.rate_ref, s32[4,128]{1,0:T(4,128)S(1)} %get-tuple-element.18.active_ref, ...), custom_call_target="tpu_custom_call" | custom-call | tf_op jit(solution)/shard_map/columns/pallas_call | solution.py:526
  29.3 10.9 %all_to_all.11.in_ref = f32[8,64,128]{2,1,0:T(8,128)S(1)} all-to-all(f32[8,64,128]{2,1,0:T(8,128)S(1)} %columns.1), channel_id=1, replica_groups=mesh['lat'=4,'lev'=8] {'lev'}, dimensions={0} | all-to-all | bytes 524288 | tf_op jit(solution)/shard_map/all_to_all | solution.py:532
  40.2 0.8 %spread.1 = f32[512,128]{1,0:T(8,128)} custom-call(f32[8,64,128]{2,1,0:T(8,128)S(1)} %all_to_all.11.in_ref), custom_call_target="tpu_custom_call" | custom-call | tf_op jit(solution)/shard_map/spread/pallas_call | solution.py:533
Async XLA Ops:
  1.0 3.7 %collective-permute-start.1 = (f32[544,128]{1,0:T(8,128)S(1)}, f32[544,128]{1,0:T(8,128)S(1)}, u32[]{:S(2)}, u32[]{:S(2)}) collective-permute-start(f32[544,128]{1,0:T(8,128)S(1)} %pack.1.refs_0_), channel_id=1, source_target_pairs={{0,8},{8,0},{16,24},{24,16},{1,9},{9,1},{17,25},{25,17},{2,10},{10... | collective-permute-start | bytes 835592 | tf_op jit(solution)/shard_map/ppermute | solution.py:469
  1.1 7.9 %collective-permute-start = (f32[544,128]{1,0:T(8,128)S(1)}, f32[544,128]{1,0:T(8,128)S(1)}, u32[]{:S(2)}, u32[]{:S(2)}) collective-permute-start(f32[544,128]{1,0:T(8,128)S(1)} %pack.1.refs_0_), channel_id=1, source_target_pairs={{8,16},{16,8},{9,17},{17,9},{10,18},{18,10},{11,19},{19,11},{12,20... | collective-permute-start | bytes 835592 | tf_op jit(solution)/shard_map/ppermute | solution.py:470

commit v8 on v7

--- a/solution.py
+++ b/solution.py
@@ -88,18 +88,31 @@
     return courant, slope_weight(courant)
 
 
-def own_rows(
-    sizes, sent_ref, f_out, zonal_out, merid_out, f_ref, slope_ref, flux_ref, flow_ref
+def near_rows(
+    sizes, sent_ref, core_ref, f_out, zonal_out, merid_out, f_ref, slope_ref, flux_ref, flow_ref
 ):
-    species, rows = sizes[0], sizes[2]
-    for row in range(rows):
-        courant, weight = zonal_weights(
-            flow_ref, row, turned(flow_rows(sizes, sent_ref, 0, row, species))
-        )
-        zonal_out[row, 0], zonal_out[row, 1] = courant, weight
-        merid_out[row] = turned(flow_rows(sizes, sent_ref, 1, row, species))
-        put_cyclic(f_ref, row, turned(tracer_rows(sizes, sent_ref, row)))
-        f_out[row] = lon_step(f_ref, slope_ref, flux_ref, row, courant, weight)
+    rows = sizes[2]
+    for side, source in enumerate((sent_ref, core_ref)):
+        for row in range(rows):
+            at = side * rows + row
+            first_sweep(
+                sizes, source, row, at, at, f_out, zonal_out, merid_out, f_ref, slope_ref, flux_ref, flow_ref
+            )
+
+
+def first_sweep(
+    sizes, source, row, at, to, f_out, zonal_out, merid_out, f_ref, slope_ref, flux_ref, flow_ref, skip=0
+):
+    species = sizes[0]
+    courant, weight = zonal_weights(
+        flow_ref, at, turned(flow_rows(sizes, source, 0, row, species))
+    )
+    zonal_out[to, 0], zonal_out[to, 1] = courant, weight
+    merid_out[to] = turned(flow_rows(sizes, source, 1, row, species))
+    put_cyclic(f_ref, at, turned(tracer_rows(sizes, source, row)))
+    f_out[to, skip : skip + courant.shape[0]] = lon_step(
+        f_ref, slope_ref, flux_ref, at, courant, weight
+    )
 
 
 def advect_kernel(
@@ -108,7 +121,6 @@
     own_zonal,
     own_merid,
     chip_ref,
-    core_ref,
     out_ref,
     f_ref,
     slope_ref,
@@ -121,33 +133,28 @@
 ):
     species, levels, rows, parts, width = sizes
     band = lax.axis_index("lat")
-    even = band % 2 == 0
-
-    def both_sides(by_core, by_chip):
-        pairs = list(zip(by_core, by_chip, strict=True))
-        before = [jnp.where(even, chip, core) for core, chip in pairs]
-        after = [jnp.where(even, core, chip) for core, chip in pairs]
-        return before, after
-
+    size = own_ref.shape[1]
+    chip_at = (band % 2) * rows
+    core_at = rows - chip_at
     for row in range(rows):
-        zonal = both_sides(
-            flow_rows(sizes, core_ref, 0, row, species), flow_rows(sizes, chip_ref, 0, row, species)
+        first_sweep(
+            sizes,
+            chip_ref,
+            row,
+            row,
+            chip_at + row,
+            f_ref,
+            halo_zonal,
+            halo_merid,
+            next_ref,
+            slope_ref,
+            flux_ref,
+            flow_ref,
+            PAD,
         )
-        merid = both_sides(
-            flow_rows(sizes, core_ref, 1, row, species), flow_rows(sizes, chip_ref, 1, row, species)
-        )
-        tracer = both_sides(
-            tracer_rows(sizes, core_ref, row), tracer_rows(sizes, chip_ref, row)
-        )
-        for side in range(2):
-            at = side * rows + row
-            courant, weight = zonal_weights(flow_ref, at, turned(zonal[side]))
-            halo_zonal[at, 0], halo_zonal[at, 1] = courant, weight
-            halo_merid[at] = turned(merid[side])
-            put_cyclic(f_ref, at, turned(tracer[side]))
-            f_ref[at, PAD : PAD + courant.shape[0]] = lon_step(
-                f_ref, slope_ref, flux_ref, at, courant, weight
-            )
+        f_ref[core_at + row, PAD : PAD + size] = own_ref[rows + row]
+        halo_zonal[core_at + row] = own_zonal[rows + row]
+        halo_merid[core_at + row] = own_merid[rows + row]
 
     def row_of(halo, own, row):
         if 0 <= row < rows:
@@ -155,7 +162,6 @@
         return halo, (row + rows if row < 0 else row)
 
     total = rows * lax.axis_size("lat")
-    size = own_ref.shape[1]
     first_face, last_face = 2 - 2 * SWEEPS, rows + 2 * SWEEPS - 2
     for chunk in range(size // width):
         there = slice(chunk * width, (chunk + 1) * width)
@@ -238,7 +244,7 @@
 
 
 def early_kernel(sizes, groups, *refs):
-    sent_ref, inputs, refs = refs[0], refs[1:9], refs[9:]
+    sent_ref, core_ref, inputs, refs = refs[0], refs[1], refs[2:10], refs[10:]
     outputs, refs = refs[:8], refs[8:]
     places, sems = refs[:8], refs[8]
     own_scratch, prepare_scratch = refs[9:13], refs[13:]
@@ -248,7 +254,7 @@
     ]
     for copy in copies:
         copy.start()
-    own_rows(sizes, sent_ref, *outputs[:3], *own_scratch)
+    near_rows(sizes, sent_ref, core_ref, *outputs[:3], *own_scratch)
     for copy in copies:
         copy.wait()
     prepare(groups, *places, *outputs[3:], *prepare_scratch)
@@ -487,18 +493,18 @@
     early = pl.pallas_call(
         functools.partial(early_kernel, sizes, blocks),
         out_shape=[
-            *arrays((rows, lons, mixed), (rows, 2, lons, mixed), (rows, lons, mixed)),
+            *arrays((2 * rows, lons, mixed), (2 * rows, 2, lons, mixed), (2 * rows, lons, mixed)),
             *arrays((all_levels, pairs, LANES), (reactions, pairs * LANES)),
             jax.ShapeDtypeStruct((substeps, LANES), jnp.int32),
             jax.ShapeDtypeStruct((2 * reactions, 2 * species), jnp.bfloat16),
             jax.ShapeDtypeStruct((species, 2 * reactions), jnp.bfloat16),
         ],
-        in_specs=[pl.BlockSpec(memory_space=pltpu.VMEM)]
+        in_specs=[pl.BlockSpec(memory_space=pltpu.VMEM)] * 2
         + [pl.BlockSpec(memory_space=pltpu.HBM)] * len(operands),
         scratch_shapes=[
             *[pltpu.VMEM(item.shape, item.dtype) for item in operands],
             pltpu.SemaphoreType.DMA((len(operands),)),
-            *[pltpu.VMEM((rows, padded, mixed), F32)] * 4,
+            *[pltpu.VMEM((2 * rows, padded, mixed), F32)] * 4,
             *[pltpu.VMEM((pairs, LANES), F32)] * 3,
         ],
         compiler_params=PARAMS,
@@ -506,8 +512,8 @@
             flops=10**7, bytes_accessed=7 * 10**6, transcendentals=10**6
         ),
         name="early",
-    )(sent, *in_hbm(*operands))
-    own, prepared = early[:3], early[3:]
+    )(sent, core_band, *in_hbm(*operands))
+    near, prepared = early[:3], early[3:]
 
     packed = kernel_call(
         functools.partial(advect_kernel, sizes),
@@ -520,7 +526,7 @@
             (rows + 1, 2, lons, mixed),
             (2 * rows, padded, mixed),
         ],
-    )(*own, chip_band, core_band)
+    )(*near, chip_band)
     moved = lax.all_to_all(packed, "lev", split_axis=0, concat_axis=0, tiled=True)
 
     reacted = kernel_call(

time: 41.4 us -> 41.1 us (level)
  transfers between devices with their start and end apart: 2 -> 2, of which waited for: 1 -> 1; matrix products, arithmetic and copies ran while one was open for 0% -> 0% of each run, Pallas kernels for 4% -> 5%
where the time goes in v8:
time: 41.1 us; the launch traced here: 40.8 us
  blocking collectives  24.7 us (60%)
  Pallas kernels  10.2 us (25%)
  waiting for transfers between devices  3.84 us (9%)
  starting transfers between devices  1.99 us (5%)
    all_to_all x1, blocking collectives, body(): lax.all_to_all(packed, 'lev', split_axis=0, concat_axis=0, tiled=True)  13.8 us
    all_to_all x1, blocking collectives, body(): lax.all_to_all(reacted, 'lev', split_axis=0, concat_axis=0, tiled=True)  10.9 us
    pallas_call x1, Pallas kernels, body(): kernel_call(functools.partial(column_kernel, (blocks, levels, species, pa...  4.84 us
    ppermute x1, waiting for transfers between devices, body(): chip_band = lax.ppermute(sent, 'lat', by_chip)  3.84 us
    pallas_call x1, Pallas kernels, body(): pl.pallas_call(functools.partial(early_kernel, sizes, blocks), out_shape=...  2.08 us
    ppermute x1, starting transfers between devices, body(): chip_band = lax.ppermute(sent, 'lat', by_chip)  1.92 us
    pallas_call x1, Pallas kernels, body(): kernel_call(functools.partial(advect_kernel, sizes), 'advect', arrays((bl...  1.45 us
    pallas_call x1, Pallas kernels, body(): pl.pallas_call(pack_kernel, out_shape=jax.ShapeDtypeStruct((len(tracers)...  0.97 us
  transfers between devices with their start and end apart: 2, of which 1 were waited for; matrix products, arithmetic and copies ran while one was open for 0% of the time, Pallas kernels for 5%

profile of v8, /device:TPU:4, one launch (start us, length us, event | category | flops | bytes accessed | tf_op | source)
XLA Modules:
  0.0 40.8 jit_solution(12586549861098917818)
XLA Ops:
  0.0 1.0 %pack.1.refs_0_ = f32[544,128]{1,0:T(8,128)S(1)} custom-call(f32[512,128]{1,0:T(8,128)} %bitcast.9, f32[32,128]{1,0:T(8,128)} %bitcast.10), custom_call_target="tpu_custom_call" | custom-call | tf_op jit(solution)/shard_map/pack/pallas_call | solution.py:467
  1.0 0.1 collective-permute-start
  1.1 1.9 %collective-permute-start.1 = (f32[544,128]{1,0:T(8,128)S(1)}, f32[544,128]{1,0:T(8,128)S(1)}, u32[]{:S(2)}, u32[]{:S(2)}) collective-permute-start(f32[544,128]{1,0:T(8,128)S(1)} %pack.1.refs_0_), channel_id=1, source_target_pairs={{8,16},{16,8},{9,17},{17,9},{10,18},{18,10},{11,19},{19,11},{12,20... | collective-permute-start | bytes 835592 | tf_op jit(solution)/shard_map/ppermute | solution.py:476
  3.0 0.0 collective-permute-done.refs_1_
  3.0 2.1 %early.1 = (f32[8,128,128]{2,1,0:T(8,128)S(1)}, f32[8,2,128,128]{3,2,1,0:T(8,128)S(1)}, f32[8,128,128]{2,1,0:T(8,128)S(1)}, f32[32,16,128]{2,1,0:T(8,128)S(1)}, ...) custom-call(f32[544,128]{1,0:T(8,128)S(1)} %pack.1.refs_0_, ...), custom_call_target="tpu_custom_call" | custom-call | flops 10000000 | bytes 7000000 | tf_op jit(solution)/shard_map/early/pallas_call | solution.py:493
  5.1 3.8 %collective-permute-done.1.chip_ref = f32[544,128]{1,0:T(8,128)S(1)} collective-permute-done((f32[544,128]{1,0:T(8,128)S(1)}, f32[544,128]{1,0:T(8,128)S(1)}, u32[]{:S(2)}, u32[]{:S(2)}) %collective-permute-start.1) | collective-permute-done | bytes 278560 | tf_op jit(solution)/shard_map/ppermute | solution.py:476
  8.9 1.5 %advect.1 = f32[8,64,128]{2,1,0:T(8,128)S(1)} custom-call(f32[8,128,128]{2,1,0:T(8,128)S(1)} %get-tuple-element.13.own_ref, f32[8,2,128,128]{3,2,1,0:T(8,128)S(1)} %get-tuple-element.14.own_zonal, f32[8,128,128]{2,1,0:T(8,128)S(1)} %get-tuple-element.15.own_merid, f32[544,128]{1,0:T(8,128)S(1)} %collective-permute-done.1.chip_ref), custom_call_target="tpu_custom_call" | custom-call | tf_op jit(solution)/shard_map/advect/pallas_call | solution.py:518
  10.4 13.8 %all_to_all.10.moved_ref = f32[8,64,128]{2,1,0:T(8,128)S(1)} all-to-all(f32[8,64,128]{2,1,0:T(8,128)S(1)} %advect.1), channel_id=1, replica_groups=mesh['lat'=4,'lev'=8] {'lev'}, dimensions={0} | all-to-all | bytes 524288 | tf_op jit(solution)/shard_map/all_to_all | solution.py:530
  24.2 4.8 %columns.1 = f32[8,64,128]{2,1,0:T(8,128)S(1)} custom-call(f32[8,64,128]{2,1,0:T(8,128)S(1)} %all_to_all.10.moved_ref, f32[32,16,128]{2,1,0:T(8,128)S(1)} %get-tuple-element.16.overlap_ref, f32[256,2048]{1,0:T(8,128)S(1)} %get-tuple-element.17.rate_ref, s32[4,128]{1,0:T(4,128)S(1)} %get-tuple-element.18.active_ref, ...), custom_call_target="tpu_custom_call" | custom-call | tf_op jit(solution)/shard_map/columns/pallas_call | solution.py:532
  29.1 10.9 %all_to_all.11.in_ref = f32[8,64,128]{2,1,0:T(8,128)S(1)} all-to-all(f32[8,64,128]{2,1,0:T(8,128)S(1)} %columns.1), channel_id=1, replica_groups=mesh['lat'=4,'lev'=8] {'lev'}, dimensions={0} | all-to-all | bytes 524288 | tf_op jit(solution)/shard_map/all_to_all | solution.py:538
  40.0 0.8 %spread.1 = f32[512,128]{1,0:T(8,128)} custom-call(f32[8,64,128]{2,1,0:T(8,128)S(1)} %all_to_all.11.in_ref), custom_call_target="tpu_custom_call" | custom-call | tf_op jit(solution)/shard_map/spread/pallas_call | solution.py:539
Async XLA Ops:
  1.0 2.0 %collective-permute-start = (f32[544,128]{1,0:T(8,128)S(1)}, f32[544,128]{1,0:T(8,128)S(1)}, u32[]{:S(2)}, u32[]{:S(2)}) collective-permute-start(f32[544,128]{1,0:T(8,128)S(1)} %pack.1.refs_0_), channel_id=1, source_target_pairs={{0,8},{8,0},{16,24},{24,16},{1,9},{9,1},{17,25},{25,17},{2,10},{10... | collective-permute-start | bytes 835592 | tf_op jit(solution)/shard_map/ppermute | solution.py:475
  1.1 7.9 %collective-permute-start.1 = (f32[544,128]{1,0:T(8,128)S(1)}, f32[544,128]{1,0:T(8,128)S(1)}, u32[]{:S(2)}, u32[]{:S(2)}) collective-permute-start(f32[544,128]{1,0:T(8,128)S(1)} %pack.1.refs_0_), channel_id=1, source_target_pairs={{8,16},{16,8},{9,17},{17,9},{10,18},{18,10},{11,19},{19,11},{12,20... | collective-permute-start | bytes 835592 | tf_op jit(solution)/shard_map/ppermute | solution.py:476

commit v9 on v8

--- a/solution.py
+++ b/solution.py
@@ -15,7 +15,7 @@
 
 
 def limited_slope(left, right):
-    return jnp.maximum(jnp.minimum(left, right), 0.0) + jnp.minimum(jnp.maximum(left, right), 0.0)
+    return jnp.maximum(jnp.minimum(right, jnp.maximum(left, 0.0)), jnp.minimum(left, 0.0))
 
 
 def slope_weight(courant):
@@ -117,6 +117,7 @@
 
 def advect_kernel(
     sizes,
+    inner_merid,
     own_ref,
     own_zonal,
     own_merid,
@@ -173,12 +174,16 @@
 
         weights = []
         for face in range(first_face, last_face + 1):
+            if 1 <= face < rows:
+                weights.append((inner_merid[face - 1, 0, there], inner_merid[face - 1, 1, there]))
+                continue
             place = band * rows + face
             open_face = jnp.logical_and(place >= 1, place <= total - 1).astype(F32)
             courant = 0.5 * (merid_at(face - 1) + merid_at(face)) * open_face
             weights.append((courant, slope_weight(courant)))
-            if 0 <= face <= rows:
-                merid_ref[face, 0, there], merid_ref[face, 1, there] = weights[-1]
+            if face in (0, rows):
+                at = face // rows
+                merid_ref[at, 0, there], merid_ref[at, 1, there] = weights[-1]
         f = []
         for row in range(-rows, 2 * rows):
             ref, at = row_of(f_ref, own_ref, row)
@@ -198,9 +203,8 @@
         there = slice(chunk * width, (chunk + 1) * width)
         inner = slice(PAD + chunk * width, PAD + (chunk + 1) * width)
         f = [f_ref[at, inner] for at in range(swept)]
-        weights = [
-            (merid_ref[face, 0, there], merid_ref[face, 1, there]) for face in range(rows + 1)
-        ]
+        faces = [(merid_ref, 0), *[(inner_merid, at) for at in range(rows - 1)], (merid_ref, 1)]
+        weights = [(ref[at, 0, there], ref[at, 1, there]) for ref, at in faces]
         for row, value in enumerate(lat_step(f, weights)):
             out_ref[chunk, row * width : (row + 1) * width] = value
 
@@ -245,6 +249,7 @@
 
 def early_kernel(sizes, groups, *refs):
     sent_ref, core_ref, inputs, refs = refs[0], refs[1], refs[2:10], refs[10:]
+    inner_out, refs = refs[0], refs[1:]
     outputs, refs = refs[:8], refs[8:]
     places, sems = refs[:8], refs[8]
     own_scratch, prepare_scratch = refs[9:13], refs[13:]
@@ -255,6 +260,10 @@
     for copy in copies:
         copy.start()
     near_rows(sizes, sent_ref, core_ref, *outputs[:3], *own_scratch)
+    merid = outputs[2]
+    for face in range(1, sizes[2]):
+        courant = 0.5 * (merid[face - 1] + merid[face])
+        inner_out[face - 1, 0], inner_out[face - 1, 1] = courant, slope_weight(courant)
     for copy in copies:
         copy.wait()
     prepare(groups, *places, *outputs[3:], *prepare_scratch)
@@ -493,6 +502,7 @@
     early = pl.pallas_call(
         functools.partial(early_kernel, sizes, blocks),
         out_shape=[
+            *arrays((rows - 1, 2, lons, mixed)),
             *arrays((2 * rows, lons, mixed), (2 * rows, 2, lons, mixed), (2 * rows, lons, mixed)),
             *arrays((all_levels, pairs, LANES), (reactions, pairs * LANES)),
             jax.ShapeDtypeStruct((substeps, LANES), jnp.int32),
@@ -513,7 +523,7 @@
         ),
         name="early",
     )(sent, core_band, *in_hbm(*operands))
-    near, prepared = early[:3], early[3:]
+    near, prepared = early[:4], early[4:]
 
     packed = kernel_call(
         functools.partial(advect_kernel, sizes),
@@ -523,7 +533,7 @@
         + [
             (2 * rows, 2, lons, mixed),
             (2 * rows, lons, mixed),
-            (rows + 1, 2, lons, mixed),
+            (2, 2, lons, mixed),
             (2 * rows, padded, mixed),
         ],
     )(*near, chip_band)

time: 41.1 us -> 40.8 us (level)
  no operation moved by 1% of the time
where the time goes in v9:
time: 40.8 us; the launch traced here: 40.5 us
  blocking collectives  24.7 us (61%)
  Pallas kernels  9.88 us (24%)
  waiting for transfers between devices  3.83 us (9%)
  starting transfers between devices  1.99 us (5%)
    all_to_all x1, blocking collectives, body(): lax.all_to_all(packed, 'lev', split_axis=0, concat_axis=0, tiled=True)  13.8 us
    all_to_all x1, blocking collectives, body(): lax.all_to_all(reacted, 'lev', split_axis=0, concat_axis=0, tiled=True)  10.9 us
    pallas_call x1, Pallas kernels, body(): kernel_call(functools.partial(column_kernel, (blocks, levels, species, pa...  4.63 us
    ppermute x1, waiting for transfers between devices, body(): chip_band = lax.ppermute(sent, 'lat', by_chip)  3.83 us
    pallas_call x1, Pallas kernels, body(): pl.pallas_call(functools.partial(early_kernel, sizes, blocks), out_shape=...  2.09 us
    ppermute x1, starting transfers between devices, body(): chip_band = lax.ppermute(sent, 'lat', by_chip)  1.92 us
    pallas_call x1, Pallas kernels, body(): kernel_call(functools.partial(advect_kernel, sizes), 'advect', arrays((bl...  1.36 us
    pallas_call x1, Pallas kernels, body(): pl.pallas_call(pack_kernel, out_shape=jax.ShapeDtypeStruct((len(tracers)...  0.97 us
  transfers between devices with their start and end apart: 2, of which 1 were waited for; matrix products, arithmetic and copies ran while one was open for 0% of the time, Pallas kernels for 5%

profile of v9, /device:TPU:4, one launch (start us, length us, event | category | flops | bytes accessed | tf_op | source)
XLA Modules:
  0.0 40.5 jit_solution(6198934975728555225)
XLA Ops:
  0.0 1.0 %pack.1.refs_0_ = f32[544,128]{1,0:T(8,128)S(1)} custom-call(f32[512,128]{1,0:T(8,128)} %bitcast.9, f32[32,128]{1,0:T(8,128)} %bitcast.10), custom_call_target="tpu_custom_call" | custom-call | tf_op jit(solution)/shard_map/pack/pallas_call | solution.py:476
  1.0 0.1 collective-permute-start
  1.1 1.9 %collective-permute-start.1 = (f32[544,128]{1,0:T(8,128)S(1)}, f32[544,128]{1,0:T(8,128)S(1)}, u32[]{:S(2)}, u32[]{:S(2)}) collective-permute-start(f32[544,128]{1,0:T(8,128)S(1)} %pack.1.refs_0_), channel_id=1, source_target_pairs={{8,16},{16,8},{9,17},{17,9},{10,18},{18,10},{11,19},{19,11},{12,20... | collective-permute-start | bytes 835592 | tf_op jit(solution)/shard_map/ppermute | solution.py:485
  3.0 0.0 collective-permute-done.refs_1_
  3.0 2.1 %early.1 = (f32[3,2,128,128]{3,2,1,0:T(8,128)S(1)}, f32[8,128,128]{2,1,0:T(8,128)S(1)}, f32[8,2,128,128]{3,2,1,0:T(8,128)S(1)}, f32[8,128,128]{2,1,0:T(8,128)S(1...) custom-call(f32[544,128]{1,0:T(8,128)S(1)} %pack.1.refs_0_, ...), custom_call_target="tpu_custom_call" | custom-call | flops 10000000 | bytes 7000000 | tf_op jit(solution)/shard_map/early/pallas_call | solution.py:502
  5.1 3.8 %collective-permute-done.1.chip_ref = f32[544,128]{1,0:T(8,128)S(1)} collective-permute-done((f32[544,128]{1,0:T(8,128)S(1)}, f32[544,128]{1,0:T(8,128)S(1)}, u32[]{:S(2)}, u32[]{:S(2)}) %collective-permute-start.1) | collective-permute-done | bytes 278560 | tf_op jit(solution)/shard_map/ppermute | solution.py:485
  8.9 1.4 %advect.1 = f32[8,64,128]{2,1,0:T(8,128)S(1)} custom-call(f32[3,2,128,128]{3,2,1,0:T(8,128)S(1)} %get-tuple-element.14.inner_merid, f32[8,128,128]{2,1,0:T(8,128)S(1)} %get-tuple-element.15.own_ref, f32[8,2,128,128]{3,2,1,0:T(8,128)S(1)} %get-tuple-element.16.own_zonal, f32[8,128,128]{2,1,0:T(8,128)S(1)} %get-tuple-element.17.own_merid, ...), custom_call_target="tpu_custom_call" | custom-call | tf_op jit(solution)/shard_map/advect/pallas_call | solution.py:528
  10.3 13.8 %all_to_all.10.moved_ref = f32[8,64,128]{2,1,0:T(8,128)S(1)} all-to-all(f32[8,64,128]{2,1,0:T(8,128)S(1)} %advect.1), channel_id=1, replica_groups=mesh['lat'=4,'lev'=8] {'lev'}, dimensions={0} | all-to-all | bytes 524288 | tf_op jit(solution)/shard_map/all_to_all | solution.py:540
  24.1 4.6 %columns.1 = f32[8,64,128]{2,1,0:T(8,128)S(1)} custom-call(f32[8,64,128]{2,1,0:T(8,128)S(1)} %all_to_all.10.moved_ref, f32[32,16,128]{2,1,0:T(8,128)S(1)} %get-tuple-element.18.overlap_ref, f32[256,2048]{1,0:T(8,128)S(1)} %get-tuple-element.19.rate_ref, s32[4,128]{1,0:T(4,128)S(1)} %get-tuple-element.20.active_ref, ...), custom_call_target="tpu_custom_call" | custom-call | tf_op jit(solution)/shard_map/columns/pallas_call | solution.py:542
  28.8 10.9 %all_to_all.11.in_ref = f32[8,64,128]{2,1,0:T(8,128)S(1)} all-to-all(f32[8,64,128]{2,1,0:T(8,128)S(1)} %columns.1), channel_id=1, replica_groups=mesh['lat'=4,'lev'=8] {'lev'}, dimensions={0} | all-to-all | bytes 524288 | tf_op jit(solution)/shard_map/all_to_all | solution.py:548
  39.7 0.8 %spread.1 = f32[512,128]{1,0:T(8,128)} custom-call(f32[8,64,128]{2,1,0:T(8,128)S(1)} %all_to_all.11.in_ref), custom_call_target="tpu_custom_call" | custom-call | tf_op jit(solution)/shard_map/spread/pallas_call | solution.py:549
Async XLA Ops:
  1.0 2.0 %collective-permute-start = (f32[544,128]{1,0:T(8,128)S(1)}, f32[544,128]{1,0:T(8,128)S(1)}, u32[]{:S(2)}, u32[]{:S(2)}) collective-permute-start(f32[544,128]{1,0:T(8,128)S(1)} %pack.1.refs_0_), channel_id=1, source_target_pairs={{0,8},{8,0},{16,24},{24,16},{1,9},{9,1},{17,25},{25,17},{2,10},{10... | collective-permute-start | bytes 835592 | tf_op jit(solution)/shard_map/ppermute | solution.py:484
  1.1 7.9 %collective-permute-start.1 = (f32[544,128]{1,0:T(8,128)S(1)}, f32[544,128]{1,0:T(8,128)S(1)}, u32[]{:S(2)}, u32[]{:S(2)}) collective-permute-start(f32[544,128]{1,0:T(8,128)S(1)} %pack.1.refs_0_), channel_id=1, source_target_pairs={{8,16},{16,8},{9,17},{17,9},{10,18},{18,10},{11,19},{19,11},{12,20... | collective-permute-start | bytes 835592 | tf_op jit(solution)/shard_map/ppermute | solution.py:485

commit v10 on v9

--- a/solution.py
+++ b/solution.py
@@ -19,7 +19,7 @@
 
 
 def slope_weight(courant):
-    return courant * (0.5 * (jnp.where(courant > 0.0, 1.0, -1.0) - courant))
+    return 0.5 * (jnp.abs(courant) - courant * courant)
 
 
 def face_flux(courant, weight, before, after, before_slope, after_slope):

time: 40.8 us -> 40.8 us (level)
  no operation moved by 1% of the time
where the time goes in v10:
time: 40.8 us; the launch traced here: 40.5 us
  blocking collectives  24.7 us (61%)
  Pallas kernels  9.71 us (24%)
  waiting for transfers between devices  4 us (10%)
  starting transfers between devices  1.99 us (5%)
    all_to_all x1, blocking collectives, body(): lax.all_to_all(packed, 'lev', split_axis=0, concat_axis=0, tiled=True)  13.8 us
    all_to_all x1, blocking collectives, body(): lax.all_to_all(reacted, 'lev', split_axis=0, concat_axis=0, tiled=True)  10.9 us
    pallas_call x1, Pallas kernels, body(): kernel_call(functools.partial(column_kernel, (blocks, levels, species, pa...  4.63 us
    ppermute x1, waiting for transfers between devices, body(): chip_band = lax.ppermute(sent, 'lat', by_chip)  4 us
    pallas_call x1, Pallas kernels, body(): pl.pallas_call(functools.partial(early_kernel, sizes, blocks), out_shape=...  1.92 us
    ppermute x1, starting transfers between devices, body(): chip_band = lax.ppermute(sent, 'lat', by_chip)  1.92 us
    pallas_call x1, Pallas kernels, body(): kernel_call(functools.partial(advect_kernel, sizes), 'advect', arrays((bl...  1.35 us
    pallas_call x1, Pallas kernels, body(): pl.pallas_call(pack_kernel, out_shape=jax.ShapeDtypeStruct((len(tracers)...  0.97 us
  transfers between devices with their start and end apart: 2, of which 1 were waited for; matrix products, arithmetic and copies ran while one was open for 0% of the time, Pallas kernels for 5%

profile of v10, /device:TPU:4, one launch (start us, length us, event | category | flops | bytes accessed | tf_op | source)
XLA Modules:
  0.0 40.5 jit_solution(11318349597606064482)
XLA Ops:
  0.0 1.0 %pack.1.refs_0_ = f32[544,128]{1,0:T(8,128)S(1)} custom-call(f32[512,128]{1,0:T(8,128)} %bitcast.9, f32[32,128]{1,0:T(8,128)} %bitcast.10), custom_call_target="tpu_custom_call" | custom-call | tf_op jit(solution)/shard_map/pack/pallas_call | solution.py:476
  1.0 0.1 collective-permute-start
  1.1 1.9 %collective-permute-start.1 = (f32[544,128]{1,0:T(8,128)S(1)}, f32[544,128]{1,0:T(8,128)S(1)}, u32[]{:S(2)}, u32[]{:S(2)}) collective-permute-start(f32[544,128]{1,0:T(8,128)S(1)} %pack.1.refs_0_), channel_id=1, source_target_pairs={{8,16},{16,8},{9,17},{17,9},{10,18},{18,10},{11,19},{19,11},{12,20... | collective-permute-start | bytes 835592 | tf_op jit(solution)/shard_map/ppermute | solution.py:485
  3.0 0.0 collective-permute-done.refs_1_
  3.0 1.9 %early.1 = (f32[3,2,128,128]{3,2,1,0:T(8,128)S(1)}, f32[8,128,128]{2,1,0:T(8,128)S(1)}, f32[8,2,128,128]{3,2,1,0:T(8,128)S(1)}, f32[8,128,128]{2,1,0:T(8,128)S(1...) custom-call(f32[544,128]{1,0:T(8,128)S(1)} %pack.1.refs_0_, ...), custom_call_target="tpu_custom_call" | custom-call | flops 10000000 | bytes 7000000 | tf_op jit(solution)/shard_map/early/pallas_call | solution.py:502
  4.9 4.0 %collective-permute-done.1.chip_ref = f32[544,128]{1,0:T(8,128)S(1)} collective-permute-done((f32[544,128]{1,0:T(8,128)S(1)}, f32[544,128]{1,0:T(8,128)S(1)}, u32[]{:S(2)}, u32[]{:S(2)}) %collective-permute-start.1) | collective-permute-done | bytes 278560 | tf_op jit(solution)/shard_map/ppermute | solution.py:485
  8.9 1.3 %advect.1 = f32[8,64,128]{2,1,0:T(8,128)S(1)} custom-call(f32[3,2,128,128]{3,2,1,0:T(8,128)S(1)} %get-tuple-element.14.inner_merid, f32[8,128,128]{2,1,0:T(8,128)S(1)} %get-tuple-element.15.own_ref, f32[8,2,128,128]{3,2,1,0:T(8,128)S(1)} %get-tuple-element.16.own_zonal, f32[8,128,128]{2,1,0:T(8,128)S(1)} %get-tuple-element.17.own_merid, ...), custom_call_target="tpu_custom_call" | custom-call | tf_op jit(solution)/shard_map/advect/pallas_call | solution.py:528
  10.3 13.8 %all_to_all.10.moved_ref = f32[8,64,128]{2,1,0:T(8,128)S(1)} all-to-all(f32[8,64,128]{2,1,0:T(8,128)S(1)} %advect.1), channel_id=1, replica_groups=mesh['lat'=4,'lev'=8] {'lev'}, dimensions={0} | all-to-all | bytes 524288 | tf_op jit(solution)/shard_map/all_to_all | solution.py:540
  24.1 4.6 %columns.1 = f32[8,64,128]{2,1,0:T(8,128)S(1)} custom-call(f32[8,64,128]{2,1,0:T(8,128)S(1)} %all_to_all.10.moved_ref, f32[32,16,128]{2,1,0:T(8,128)S(1)} %get-tuple-element.18.overlap_ref, f32[256,2048]{1,0:T(8,128)S(1)} %get-tuple-element.19.rate_ref, s32[4,128]{1,0:T(4,128)S(1)} %get-tuple-element.20.active_ref, ...), custom_call_target="tpu_custom_call" | custom-call | tf_op jit(solution)/shard_map/columns/pallas_call | solution.py:542
  28.7 10.9 %all_to_all.11.in_ref = f32[8,64,128]{2,1,0:T(8,128)S(1)} all-to-all(f32[8,64,128]{2,1,0:T(8,128)S(1)} %columns.1), channel_id=1, replica_groups=mesh['lat'=4,'lev'=8] {'lev'}, dimensions={0} | all-to-all | bytes 524288 | tf_op jit(solution)/shard_map/all_to_all | solution.py:548
  39.6 0.8 %spread.1 = f32[512,128]{1,0:T(8,128)} custom-call(f32[8,64,128]{2,1,0:T(8,128)S(1)} %all_to_all.11.in_ref), custom_call_target="tpu_custom_call" | custom-call | tf_op jit(solution)/shard_map/spread/pallas_call | solution.py:549
Async XLA Ops:
  1.0 2.0 %collective-permute-start = (f32[544,128]{1,0:T(8,128)S(1)}, f32[544,128]{1,0:T(8,128)S(1)}, u32[]{:S(2)}, u32[]{:S(2)}) collective-permute-start(f32[544,128]{1,0:T(8,128)S(1)} %pack.1.refs_0_), channel_id=1, source_target_pairs={{0,8},{8,0},{16,24},{24,16},{1,9},{9,1},{17,25},{25,17},{2,10},{10... | collective-permute-start | bytes 835592 | tf_op jit(solution)/shard_map/ppermute | solution.py:484
  1.1 7.9 %collective-permute-start.1 = (f32[544,128]{1,0:T(8,128)S(1)}, f32[544,128]{1,0:T(8,128)S(1)}, u32[]{:S(2)}, u32[]{:S(2)}) collective-permute-start(f32[544,128]{1,0:T(8,128)S(1)} %pack.1.refs_0_), channel_id=1, source_target_pairs={{8,16},{16,8},{9,17},{17,9},{10,18},{18,10},{11,19},{19,11},{12,20... | collective-permute-start | bytes 835592 | tf_op jit(solution)/shard_map/ppermute | solution.py:485
